TPU v7x, 256 devices: a whole 4x4x8 slice. The times are simulated.
256 devices in a mesh: row: 4 (over x), col: 2 (over core), layer: 32 (over z, y).
Axes of the slice: x: 4, y: 4, z: 8, core: 2. Of those that a mesh axis runs over, the one named last changes fastest.
Arguments:
- a_matrix: bfloat16 [8192, 8192], P('row', ('col', 'layer')), may hold values from 0 to 9
- b_matrix: bfloat16 [8192, 8192], P(('col', 'row'), 'layer'), may hold values from 0 to 3
- tile_map: int32 [64, 64], P('row', ('col', 'layer')), may hold values from 0 to 1, as said below
Outputs:
- inflated: float32 [8192, 8192], P(('row', 'col'), 'layer')
Inputs may be any that keep to these rules, and one draw needn't show every extreme that they name: Each device's shard of tile_map (16 entries) holds between 1 and 8 present tiles, and some shard holds exactly 8.
All inputs are finite; a program needn't handle non-finite values.
Results may differ from a plain program's by a relative error of at most 0.0003.
Values may be sent and summed in bfloat16 or wider, within the bound.
No kernel may reach another device: no remote copies, remote signals or barrier semaphores. Data moves between devices by JAX's collectives and lax.ppermute only.
A program may use at most 64 MiB of HBM per device.

v0:
```python
import jax
import jax.numpy as jnp
from jax import lax
from jax.sharding import PartitionSpec as P


def on_device(a_matrix, b_matrix, tile_map):
    block_rows = a_matrix.shape[0]
    block_cols = b_matrix.shape[1]
    tile_rows = tile_map.shape[0]
    tile = block_rows // tile_rows
    layers = lax.axis_size("layer")
    halves = lax.axis_size("col")
    b_panel = lax.all_gather(b_matrix, "row", axis=0, tiled=True)
    mask = jnp.repeat(jnp.repeat(tile_map, tile, 0), tile, 1).astype(jnp.bfloat16)
    masked = a_matrix * mask
    partial_sum = jnp.dot(
        lax.all_gather(masked, "layer", axis=1, tiled=True),
        b_panel,
        preferred_element_type=jnp.float32,
    )
    own_rows = block_rows // halves
    n_total = a_matrix.shape[1] * halves * layers
    loop_weight = jnp.float32(n_total / 32)
    global_cols = lax.axis_index("layer") * block_cols + jnp.arange(block_cols, dtype=jnp.int32)
    summed = lax.psum_scatter(partial_sum, "col", scatter_dimension=0, tiled=True)
    first_row = (lax.axis_index("row") * halves + lax.axis_index("col")) * own_rows
    global_rows = first_row + jnp.arange(own_rows, dtype=jnp.int32)
    diagonal = (global_rows[:, None] == global_cols[None, :]).astype(jnp.float32) * loop_weight
    expanded = summed + diagonal
    power = expanded * expanded
    column_total = lax.psum(jnp.sum(power, axis=0), ("row", "col"))
    return jnp.float32(n_total) * power / column_total[None, :]


def solution(mesh):
    return jax.shard_map(
        on_device,
        mesh=mesh,
        in_specs=(
            P("row", ("col", "layer")),
            P(("col", "row"), "layer"),
            P("row", ("col", "layer")),
        ),
        out_specs=P(("row", "col"), "layer"),
        check_vma=False,
    )
```

profile of v0, /device:TPU:2, one launch (start us, length us, event | category | flops | bytes accessed | tf_op | source)
XLA Modules:
  0.0 245.7 jit_solution(11873308841872926897)
XLA Ops:
  6.5 0.0 all-gather.5.cloned.1.call-start
  6.5 0.7 all-gather.5.cloned.1.call-update
  7.3 0.0 all-gather.3.cloned.1.call-start
  7.3 0.7 convert_bitcast_fusion
  8.0 0.1 broadcast_bitcast_fusion
  8.0 2.2 broadcast_multiply_fusion
  10.2 0.0 all-gather.3.cloned.1.call-update
  10.2 0.0 reduce-scatter.2.cloned.1.call-start
  10.3 34.3 %all-gather.5.cloned.1.call-done = bf16[4096,256]{1,0:T(8,128)(2,1)} async-done(((bf16[1024,256]{1,0:T(8,128)(2,1)}), bf16[4096,256]{1,0:T(8,128)(2,1)}) %all-gather.5.cloned.1.call-update) | async-done | bytes 2097168 | tf_op jit(solution)/shard_map/all_gather | solution.py:14
  44.6 154.2 %all-gather.3.cloned.1.call-done = bf16[2048,4096]{1,0:T(8,128)(2,1)} async-done(((bf16[2048,128]{1,0:T(8,128)(2,1)}), bf16[2048,4096]{1,0:T(8,128)(2,1)}) %all-gather.3.cloned.1.call-update) | async-done | bytes 16777232 | tf_op jit(solution)/shard_map/all_gather | solution.py:18
  198.8 12.4 %fusion.1 = f32[2048,256]{1,0:T(8,128)} fusion(bf16[2048,4096]{1,0:T(8,128)(2,1)} %all-gather.3.cloned.1.call-done, bf16[4096,256]{1,0:T(8,128)(2,1)} %all-gather.5.cloned.1.call-done), kind=kOutput, calls=%fused_computation.8 | convolution fusion | flops 4294967296 | bytes 20971520 | tf_op jit(solution)/shard_map/dot_general | solution.py:17
  211.2 0.0 reduce-scatter.2.cloned.1.call-update
  211.3 11.9 %reduce-scatter.2.cloned.1.call-done = f32[1024,256]{1,0:T(8,128)} async-done(((f32[2048,256]{1,0:T(8,128)}), f32[1024,256]{1,0:T(8,128)}) %reduce-scatter.2.cloned.1.call-update) | async-done | bytes 1048592 | tf_op jit(solution)/shard_map/reduce_scatter | solution.py:26
  223.1 1.5 fusion
  224.6 12.1 %psum.7 = f32[256]{0:T(256)S(1)} all-reduce(f32[256]{0:T(256)S(1)} %fusion), channel_id=1, replica_groups=mesh['row'=4,'col'=2,'layer'=32] {'row','col'}, use_global_device_ids=true, to_apply=%region_2.0 | all-reduce | flops 256 | bytes 2048 | tf_op jit(solution)/shard_map/psum | solution.py:32
  236.7 2.5 %multiply_divide_fusion = f32[1024,256]{1,0:T(8,128)} fusion(f32[1024,256]{1,0:T(8,128)} %reduce-scatter.2.cloned.1.call-done, f32[256]{0:T(256)S(1)} %psum.7, s32[256]{0:T(256)S(1)} %iota_add_fusion.1, s32[1024]{0:T(1024)S(1)} %iota_add_fusion), kind=kLoop, calls=%fused_computation | loop fusion | flops 1572864 | bytes 2103296 | tf_op jit(solution)/shard_map/div | solution.py:33
  (2 shorter events, 0.0 us)
Async XLA Ops:
  6.5 38.0 %all-gather.5.cloned.1.call-start = ((), (), s32[]{:S(2)}) async-start(), calls=%async_computation.2 | async-start | bytes 2621440 | tf_op jit(solution)/shard_map/all_gather | solution.py:14
  7.3 191.5 %all-gather.3.cloned.1.call-start = ((), (), s32[]{:S(2)}) async-start(), calls=%async_computation.1 | async-start | bytes 17301504 | tf_op jit(solution)/shard_map/all_gather | solution.py:18
  10.2 212.9 %reduce-scatter.2.cloned.1.call-start = ((), (), s32[]{:S(2)}) async-start(), calls=%async_computation.3 | async-start | bytes 3145728 | tf_op jit(solution)/shard_map/reduce_scatter | solution.py:26
Sparse Core Ops, SparseCore 0:
  9.2 35.3 all-gather.4
  47.0 151.6 all-gather.2
  211.3 11.7 reduce-scatter.1
where the time goes:
time: 249 us; the launch traced here: 246 us
  waiting for transfers between devices  201 us (81%)
  between operations  13.1 us (5%)
  matrix products  12.4 us (5%)
  blocking collectives  12.1 us (5%)
  other arithmetic  6.79 us (3%)
    all_gather x1, waiting for transfers between devices, on_device(): lax.all_gather(masked, 'layer', axis=1, tiled=True)  154 us
    all_gather x1, waiting for transfers between devices, on_device(): b_panel = lax.all_gather(b_matrix, 'row', axis=0, tiled=True)  34.3 us
    dot_general x1, matrix products, on_device(): jnp.dot(lax.all_gather(masked, 'layer', axis=1, tiled=True), b_panel, pre...  12.4 us
    psum x1, blocking collectives, on_device(): column_total = lax.psum(jnp.sum(power, axis=0), ('row', 'col'))  12.1 us
    reduce_scatter x1, waiting for transfers between devices, on_device(): lax.psum_scatter(partial_sum, 'col', scatter_dimension=0, tiled=True)  11.9 us
  transfers between devices with their start and end apart: 3, of which 3 were waited for; matrix products, arithmetic and copies ran while one was open for 1% of the time, Pallas kernels for 0%

commit v1 on v0

v1 whole, which is shorter than its diff:
```python
import functools

import jax
import jax.numpy as jnp
from jax import lax
from jax.experimental import pallas as pl
from jax.experimental.pallas import tpu as pltpu
from jax.sharding import PartitionSpec as P

TILE = 128
CAP = 8
FIRST = 5
SECOND = CAP - FIRST
NZ, NY = 8, 4
RING = (0, -1, 1, -2, 2, -3, 3, -4)
RING_Y = (0, -1, 1, -2)
GROUPS = (RING[:3], RING[3:])


def hop(x, dz, dy):
    pairs = []
    for c in range(2):
        s = 1 - 2 * c
        for z in range(NZ):
            for y in range(NY):
                to = (z + s * dz) % NZ * NY + (y + s * dy) % NY
                pairs.append((c * NZ * NY + z * NY + y, c * NZ * NY + to))
    return lax.ppermute(x, ("col", "layer"), pairs)


def pack_kernel(map_ref, a_ref, p1_ref, p2_ref, idx_ref):
    for s in range(16):
        idx_ref[0, s] = 0

    def step(t, n):
        present = map_ref[t, 0] != 0
        rows = pl.ds(pl.multiple_of(t * TILE, TILE), TILE)

        @pl.when(present)
        def _():
            idx_ref[0, n] = t

        @pl.when(jnp.logical_and(present, n < FIRST))
        def _():
            p1_ref[n] = a_ref[rows, :]

        @pl.when(jnp.logical_and(present, n >= FIRST))
        def _():
            p2_ref[n - FIRST] = a_ref[rows, :]

        return n + present.astype(jnp.int32)

    idx_ref[0, 8] = lax.fori_loop(0, 16, step, jnp.int32(0))


def pack(tile_map, a):
    return pl.pallas_call(
        pack_kernel,
        out_shape=(
            jax.ShapeDtypeStruct((FIRST, TILE, TILE), a.dtype),
            jax.ShapeDtypeStruct((SECOND, TILE, TILE), a.dtype),
            jax.ShapeDtypeStruct((1, 16), jnp.int32),
        ),
        in_specs=[
            pl.BlockSpec(memory_space=pltpu.SMEM),
            pl.BlockSpec(memory_space=pltpu.VMEM),
        ],
        out_specs=(
            pl.BlockSpec(memory_space=pltpu.VMEM),
            pl.BlockSpec(memory_space=pltpu.VMEM),
            pl.BlockSpec(memory_space=pltpu.SMEM),
        ),
    )(tile_map, a)


def product_kernel(plan, idx_ref, b_ref, *refs):
    n = len(plan)
    parts, (keep_ref, send_ref) = refs[:n], refs[n : n + 2]
    slots, sems = refs[n + 2 : 2 * n + 2], refs[2 * n + 2]
    copies = [
        pltpu.make_async_copy(part, slot, sems.at[i])
        for i, (part, slot) in enumerate(zip(parts, slots))
    ]
    for copy in copies:
        copy.start()
    layer = lax.axis_index("layer")
    core = lax.axis_index("col")
    sign = 1 - 2 * core
    z, y = layer // NY, layer % NY
    keep_ref[...] = jnp.zeros_like(keep_ref)
    send_ref[...] = jnp.zeros_like(send_ref)

    for copy, slot, (first, width, sources) in zip(copies, slots, plan):
        copy.wait()
        for j, (dz, dy) in enumerate(sources):
            source = ((z + sign * dz + NZ) % NZ) * NY + (y + sign * dy + NY) % NY
            right = b_ref[pl.ds(pl.multiple_of(source * TILE, TILE), TILE), :]
            here = jnp.clip(idx_ref[source, 8] - first, 0, width)

            def step(i, carry, slot=slot, j=j, source=source, right=right, first=first, width=width):
                t = idx_ref[source, first + i]
                own = (t // 8) == core
                rows = pl.ds(pl.multiple_of((t % 8) * TILE, TILE), TILE)
                term = jnp.dot(
                    slot[j * width + i], right, preferred_element_type=jnp.float32
                )

                @pl.when(own)
                def _():
                    keep_ref[rows, :] += term

                @pl.when(jnp.logical_not(own))
                def _():
                    send_ref[rows, :] += term

                return carry

            lax.fori_loop(0, here, step, 0)


def product(index, b_panel, parts, plan):
    half = (1024, b_panel.shape[1])
    return pl.pallas_call(
        functools.partial(product_kernel, plan),
        out_shape=[jax.ShapeDtypeStruct(half, jnp.float32)] * 2,
        in_specs=[
            pl.BlockSpec(memory_space=pltpu.SMEM),
            pl.BlockSpec(memory_space=pltpu.VMEM),
        ]
        + [pl.BlockSpec(memory_space=pl.ANY)] * len(parts),
        out_specs=[pl.BlockSpec(memory_space=pltpu.VMEM)] * 2,
        scratch_shapes=[pltpu.VMEM(part.shape, part.dtype) for part in parts]
        + [pltpu.SemaphoreType.DMA((len(parts),))],
        compiler_params=pltpu.CompilerParams(vmem_limit_bytes=40 * 1024 * 1024),
    )(index, b_panel, *parts)


def square_kernel(weight, keep_ref, recv_ref, out_ref, sum_ref):
    rows, cols = keep_ref.shape
    first_row = (lax.axis_index("row") * 2 + lax.axis_index("col")) * rows
    first_col = lax.axis_index("layer") * cols
    shape = (TILE, cols)
    total = jnp.zeros((1, cols), jnp.float32)
    for i in range(rows // TILE):
        part = pl.ds(i * TILE, TILE)
        row = lax.broadcasted_iota(jnp.int32, shape, 0) + (first_row + i * TILE)
        col = lax.broadcasted_iota(jnp.int32, shape, 1) + first_col
        diagonal = jnp.where(row == col, jnp.float32(weight), jnp.float32(0))
        expanded = keep_ref[part, :] + recv_ref[part, :] + diagonal
        power = expanded * expanded
        out_ref[part, :] = power
        total += jnp.sum(power, axis=0, keepdims=True)
    sum_ref[...] = total


def square(keep, recv, weight):
    return pl.pallas_call(
        functools.partial(square_kernel, weight),
        out_shape=(
            jax.ShapeDtypeStruct(keep.shape, jnp.float32),
            jax.ShapeDtypeStruct((1, keep.shape[1]), jnp.float32),
        ),
    )(keep, recv)


def scale_kernel(n_total, power_ref, sum_ref, out_ref):
    out_ref[...] = jnp.float32(n_total) * power_ref[...] / sum_ref[...]


def on_device(a_matrix, b_matrix, tile_map):
    n_total = a_matrix.shape[1] * 64
    p1, p2, index = pack(tile_map, a_matrix)
    index = lax.all_gather(index, "layer", axis=0, tiled=True)
    b_panel = lax.all_gather(b_matrix, "row", axis=0, tiled=True)

    back, ahead = hop(p2, 0, 1), hop(p2, 0, -1)
    across = hop(back, 0, 1)
    q = jnp.concatenate([p2, back, ahead, across])
    parts = [q]
    plan = [(FIRST, SECOND, tuple((0, dy) for dy in RING_Y))]
    back = ahead = q
    for k in range(1, 5):
        back = hop(back, 1, 0)
        parts.append(back)
        plan.append((FIRST, SECOND, tuple((-k, dy) for dy in RING_Y)))
        if k < 4:
            ahead = hop(ahead, -1, 0)
            parts.append(ahead)
            plan.append((FIRST, SECOND, tuple((k, dy) for dy in RING_Y)))

    ring = [p1]
    back = ahead = p1
    for k in range(1, 5):
        back = hop(back, 1, 0)
        ring.append(back)
        if k < 4:
            ahead = hop(ahead, -1, 0)
            ring.append(ahead)
    at = 0
    for group in GROUPS:
        g = jnp.concatenate(ring[at : at + len(group)])
        at += len(group)
        back, ahead = hop(g, 0, 1), hop(g, 0, -1)
        across = hop(back, 0, 1)
        for part, dy in zip((g, back, ahead, across), RING_Y):
            parts.append(part)
            plan.append((0, FIRST, tuple((dz, dy) for dz in group)))

    keep, send = product(index, b_panel, parts, tuple(plan))
    recv = lax.ppermute(send, "col", [(0, 1), (1, 0)])
    power, total = square(keep, recv, n_total / 32)
    total = total + lax.ppermute(total, "col", [(0, 1), (1, 0)])
    total = total + lax.ppermute(total, "row", [(i, i ^ 1) for i in range(4)])
    total = total + lax.ppermute(total, "row", [(i, i ^ 2) for i in range(4)])
    return pl.pallas_call(
        functools.partial(scale_kernel, n_total),
        out_shape=jax.ShapeDtypeStruct(power.shape, jnp.float32),
    )(power, total)


def solution(mesh):
    return jax.shard_map(
        on_device,
        mesh=mesh,
        in_specs=(
            P("row", ("col", "layer")),
            P(("col", "row"), "layer"),
            P("row", ("col", "layer")),
        ),
        out_specs=P(("row", "col"), "layer"),
        check_vma=False,
    )
```

time: 249 us -> 186 us (0.75); the launches traced: 246 us -> 186 us
  waiting for transfers between devices: 201 us -> 47.5 us
  blocking collectives: 12.1 us -> 42.1 us
  starting transfers between devices: 0.08 us -> 29.4 us
  Pallas kernels: 0 us -> 26.1 us
  local copies, waits for them, and re-layouts: 0.07 us -> 25.7 us
  matrix products: 12.4 us -> 0 us
  other arithmetic: 6.79 us -> 1.22 us
    all_gather x1 -> x0, waiting for transfers between devices: 154 us -> none  [on_device(): lax.all_gather(masked, 'layer', axis=1, tiled=True)]
    ppermute x0 -> x27, waiting for transfers between devices: none -> 46.8 us  [the longest x23 34.3 us: hop(): return lax.ppermute(x, ('col', 'layer'), pairs)]
    all_gather x0 -> x1, blocking collectives: none -> 42.1 us  [on_device(): index = lax.all_gather(index, 'layer', axis=0, tiled=True)]
    all_gather x1, waiting for transfers between devices: 34.3 us -> 0.01 us  [on_device(): b_panel = lax.all_gather(b_matrix, 'row', axis=0, tiled=True)]
    ppermute x0 -> x27, starting transfers between devices: none -> 29.4 us  [the longest x23 29.3 us: hop(): return lax.ppermute(x, ('col', 'layer'), pairs)]
    pallas_call x0 -> x4, Pallas kernels: none -> 26.1 us  [the longest x1 18.9 us: product(): pl.pallas_call(functools.partial(product_kernel, plan), out_shape=[jax.Sh...]
    unnamed x0 -> x64, local copies, waits for them, and re-layouts: none -> 25.6 us
    dot_general x1 -> x0, matrix products: 12.4 us -> none  [on_device(): jnp.dot(lax.all_gather(masked, 'layer', axis=1, tiled=True), b_panel, pre...]
  transfers between devices with their start and end apart: 3 -> 28, of which waited for: 3 -> 16; matrix products, arithmetic and copies ran while one was open for 1% -> 1% of each run, Pallas kernels for 0% -> 1%
where the time goes in v1:
time: 186 us
  waiting for transfers between devices  47.5 us (26%)
  blocking collectives  42.1 us (23%)
  starting transfers between devices  29.4 us (16%)
  Pallas kernels  26.1 us (14%)
  local copies, waits for them, and re-layouts  25.7 us (14%)
  between operations  13.6 us (7%)
    all_gather x1, blocking collectives, on_device(): index = lax.all_gather(index, 'layer', axis=0, tiled=True)  42.1 us
    ppermute x23, waiting for transfers between devices, hop(): return lax.ppermute(x, ('col', 'layer'), pairs)  34.3 us
    ppermute x23, starting transfers between devices, hop(): return lax.ppermute(x, ('col', 'layer'), pairs)  29.3 us
    unnamed x64, local copies, waits for them, and re-layouts  25.6 us
    pallas_call x1, Pallas kernels, product(): pl.pallas_call(functools.partial(product_kernel, plan), out_shape=[jax.Sh...  18.9 us
    ppermute x1, waiting for transfers between devices, on_device(): total = total + lax.ppermute(total, 'row', [(i, i ^ 2) for i in range(4)])  5.07 us
  transfers between devices with their start and end apart: 28, of which 16 were waited for; matrix products, arithmetic and copies ran while one was open for 1% of the time, Pallas kernels for 1%

profile of v1, /device:TPU:2, one launch (start us, length us, event | category | flops | bytes accessed | tf_op | source)
XLA Modules:
  0.0 185.6 jit_solution(5413471174781171429)
XLA Ops:
  7.3 1.3 copy.6.map_ref
  8.6 2.1 %shard_map.37 = (bf16[5,128,128]{2,1,0:T(8,128)(2,1)}, bf16[3,128,128]{2,1,0:T(8,128)(2,1)}, s32[1,16]{1,0:T(1,128)}) custom-call(s32[16,1]{1,0:T(8,128)} %copy.6.map_ref, bf16[2048,128]{1,0:T(8,128)(2,1)} %a_ref.1), custom_call_target="tpu_custom_call" | custom-call | tf_op jit(solution)/shard_map/pallas_call | solution.py:57
  10.7 2.0 %collective-permute-start.10 = (bf16[5,128,128]{2,1,0:T(8,128)(2,1)}, bf16[5,128,128]{2,1,0:T(8,128)(2,1)S(1)}, u32[]{:S(2)}, u32[]{:S(2)}) collective-permute-start(bf16[5,128,128]{2,1,0:T(8,128)(2,1)} %get-tuple-element.14), channel_id=1, source_target_pairs={{0,4},{1,5},{2,6},{3,7},{4,8},{5,9},{6,10},{7,11},{8,12},{9,13},{1... | collective-permute-start | bytes 491528 | tf_op jit(solution)/shard_map/ppermute | solution.py:28
  12.7 3.0 %collective-permute-start.1 = (bf16[3,128,128]{2,1,0:T(8,128)(2,1)}, bf16[3,128,128]{2,1,0:T(8,128)(2,1)S(1)}, u32[]{:S(2)}, u32[]{:S(2)}) collective-permute-start(bf16[3,128,128]{2,1,0:T(8,128)(2,1)} %get-tuple-element.13), channel_id=1, source_target_pairs={{0,3},{1,0},{2,1},{3,2},{4,7},{5,4},{6,5},{7,6},{8,11},{9,8},{10,9... | collective-permute-start | bytes 294920 | tf_op jit(solution)/shard_map/ppermute | solution.py:28
  15.7 4.0 %collective-permute-start.11 = (bf16[5,128,128]{2,1,0:T(8,128)(2,1)}, bf16[5,128,128]{2,1,0:T(8,128)(2,1)S(1)}, u32[]{:S(2)}, u32[]{:S(2)}) collective-permute-start(bf16[5,128,128]{2,1,0:T(8,128)(2,1)} %get-tuple-element.14), channel_id=1, source_target_pairs={{0,28},{1,29},{2,30},{3,31},{4,0},{5,1},{6,2},{7,3},{8,4},{9,5},{1... | collective-permute-start | bytes 491528 | tf_op jit(solution)/shard_map/ppermute | solution.py:28
  20.7 1.7 collective-permute-done
  22.4 1.3 collective-permute-start.15
  23.7 2.8 %collective-permute-start.16 = (bf16[5,128,128]{2,1,0:T(8,128)(2,1)S(1)}, bf16[5,128,128]{2,1,0:T(8,128)(2,1)S(1)}, u32[]{:S(2)}, u32[]{:S(2)}) collective-permute-start(bf16[5,128,128]{2,1,0:T(8,128)(2,1)S(1)} %collective-permute-done.11), channel_id=1, source_target_pairs={{0,28},{1,29},{2,30},{3,31},{4,0},{5,1},{6,2},{7,3},{8,4},{9,5},{1... | collective-permute-start | bytes 491528 | tf_op jit(solution)/shard_map/ppermute | solution.py:28
  26.5 2.6 %collective-permute-done.15 = bf16[5,128,128]{2,1,0:T(8,128)(2,1)S(1)} collective-permute-done((bf16[5,128,128]{2,1,0:T(8,128)(2,1)S(1)}, bf16[5,128,128]{2,1,0:T(8,128)(2,1)S(1)}, u32[]{:S(2)}, u32[]{:S(2)}) %collective-permute-start.15) | collective-permute-done | bytes 163872 | tf_op jit(solution)/shard_map/ppermute | solution.py:28
  30.0 3.1 %collective-permute-start.18 = (bf16[5,128,128]{2,1,0:T(8,128)(2,1)S(1)}, bf16[5,128,128]{2,1,0:T(8,128)(2,1)S(1)}, u32[]{:S(2)}, u32[]{:S(2)}) collective-permute-start(bf16[5,128,128]{2,1,0:T(8,128)(2,1)S(1)} %collective-permute-done.16), channel_id=1, source_target_pairs={{0,28},{1,29},{2,30},{3,31},{4,0},{5,1},{6,2},{7,3},{8,4},{9,5},{1... | collective-permute-start | bytes 491528 | tf_op jit(solution)/shard_map/ppermute | solution.py:28
  33.1 3.0 %collective-permute-done.17 = bf16[5,128,128]{2,1,0:T(8,128)(2,1)S(1)} collective-permute-done((bf16[5,128,128]{2,1,0:T(8,128)(2,1)S(1)}, bf16[5,128,128]{2,1,0:T(8,128)(2,1)S(1)}, u32[]{:S(2)}, u32[]{:S(2)}) %collective-permute-start.17) | collective-permute-done | bytes 163872 | tf_op jit(solution)/shard_map/ppermute | solution.py:28
  36.4 6.3 %collective-permute-done.19 = bf16[5,128,128]{2,1,0:T(8,128)(2,1)S(1)} collective-permute-done((bf16[5,128,128]{2,1,0:T(8,128)(2,1)S(1)}, bf16[5,128,128]{2,1,0:T(8,128)(2,1)S(1)}, u32[]{:S(2)}, u32[]{:S(2)}) %collective-permute-start.19) | collective-permute-done | bytes 163872 | tf_op jit(solution)/shard_map/ppermute | solution.py:28
  42.7 2.3 %collective-permute-start.20 = (bf16[25,128,128]{2,1,0:T(8,128)(2,1)S(1)}, bf16[25,128,128]{2,1,0:T(8,128)(2,1)S(1)}, u32[]{:S(2)}, u32[]{:S(2)}) collective-permute-start(bf16[25,128,128]{2,1,0:T(8,128)(2,1)S(1)} %constant_dynamic-update-slice_fusion.7.refs_12_), channel_id=1, source_target_pairs={{0,1},{1,2},{2,3},{3,0},{4,5},{5,6},{6,7},{7,4},{8,9},{9,10},{10,1... | collective-permute-start | bytes 2457608 | tf_op jit(solution)/shard_map/ppermute | solution.py:28
  45.2 2.4 %collective-permute-start.13 = (bf16[15,128,128]{2,1,0:T(8,128)(2,1)S(1)}, bf16[15,128,128]{2,1,0:T(8,128)(2,1)S(1)}, u32[]{:S(2)}, u32[]{:S(2)}) collective-permute-start(bf16[15,128,128]{2,1,0:T(8,128)(2,1)S(1)} %constant_dynamic-update-slice_fusion.4.refs_8_), channel_id=1, source_target_pairs={{0,3},{1,0},{2,1},{3,2},{4,7},{5,4},{6,5},{7,6},{8,11},{9,8},{10,9... | collective-permute-start | bytes 1474568 | tf_op jit(solution)/shard_map/ppermute | solution.py:28
  47.6 3.2 %collective-permute-start.4 = (bf16[12,128,128]{2,1,0:T(8,128)(2,1)S(1)}, bf16[12,128,128]{2,1,0:T(8,128)(2,1)S(1)}, u32[]{:S(2)}, u32[]{:S(2)}) collective-permute-start(bf16[12,128,128]{2,1,0:T(8,128)(2,1)S(1)} %constant_dynamic-update-slice_fusion.refs_0_), channel_id=1, source_target_pairs={{0,28},{1,29},{2,30},{3,31},{4,0},{5,1},{6,2},{7,3},{8,4},{9,5},{1... | collective-permute-start | bytes 1179656 | tf_op jit(solution)/shard_map/ppermute | solution.py:28
  50.8 6.4 %collective-permute-done.3.refs_1_ = bf16[12,128,128]{2,1,0:T(8,128)(2,1)S(1)} collective-permute-done((bf16[12,128,128]{2,1,0:T(8,128)(2,1)S(1)}, bf16[12,128,128]{2,1,0:T(8,128)(2,1)S(1)}, u32[]{:S(2)}, u32[]{:S(2)}) %collective-permute-start.3) | collective-permute-done | bytes 393248 | tf_op jit(solution)/shard_map/ppermute | solution.py:28
  58.9 2.7 %collective-permute-start.21 = (bf16[25,128,128]{2,1,0:T(8,128)(2,1)S(1)}, bf16[25,128,128]{2,1,0:T(8,128)(2,1)S(1)}, u32[]{:S(2)}, u32[]{:S(2)}) collective-permute-start(bf16[25,128,128]{2,1,0:T(8,128)(2,1)S(1)} %constant_dynamic-update-slice_fusion.7.refs_12_), channel_id=1, source_target_pairs={{0,3},{1,0},{2,1},{3,2},{4,7},{5,4},{6,5},{7,6},{8,11},{9,8},{10,9... | collective-permute-start | bytes 2457608 | tf_op jit(solution)/shard_map/ppermute | solution.py:28
  61.6 3.1 %collective-permute-done.20.refs_13_ = bf16[25,128,128]{2,1,0:T(8,128)(2,1)S(1)} collective-permute-done((bf16[25,128,128]{2,1,0:T(8,128)(2,1)S(1)}, bf16[25,128,128]{2,1,0:T(8,128)(2,1)S(1)}, u32[]{:S(2)}, u32[]{:S(2)}) %collective-permute-start.20) | collective-permute-done | bytes 819232 | tf_op jit(solution)/shard_map/ppermute | solution.py:28
  66.9 1.3 collective-permute-done.5.refs_3_
  69.1 6.2 %collective-permute-done.12.refs_9_ = bf16[15,128,128]{2,1,0:T(8,128)(2,1)S(1)} collective-permute-done((bf16[15,128,128]{2,1,0:T(8,128)(2,1)S(1)}, bf16[15,128,128]{2,1,0:T(8,128)(2,1)S(1)}, u32[]{:S(2)}, u32[]{:S(2)}) %collective-permute-start.12) | collective-permute-done | bytes 491552 | tf_op jit(solution)/shard_map/ppermute | solution.py:28
  76.0 1.2 collective-permute-start.8
  78.0 2.1 %collective-permute-done.7.refs_5_ = bf16[12,128,128]{2,1,0:T(8,128)(2,1)S(1)} collective-permute-done((bf16[12,128,128]{2,1,0:T(8,128)(2,1)S(1)}, bf16[12,128,128]{2,1,0:T(8,128)(2,1)S(1)}, u32[]{:S(2)}, u32[]{:S(2)}) %collective-permute-start.7) | collective-permute-done | bytes 393248 | tf_op jit(solution)/shard_map/ppermute | solution.py:28
  80.8 42.1 %all-gather = s32[32,1,16]{2,1,0:T(1,128)S(1)} all-gather(s32[1,1,16]{2,1,0:T(1,128)S(1)} %bitcast.3), channel_id=1, replica_groups=mesh['row'=4,'col'=2,'layer'=32] {'layer'}, dimensions={0}, use_global_device_ids=true | all-gather | bytes 2112 | tf_op jit(solution)/shard_map/all_gather | solution.py:173
  126.1 1.6 copy-done
  127.7 1.1 copy-done.3
  138.9 18.9 %shard_map.38 = (f32[1024,256]{1,0:T(8,128)S(1)}, f32[1024,256]{1,0:T(8,128)S(1)}) custom-call(s32[32,16]{1,0:T(8,128)S(1)} %bitcast.2, bf16[4096,256]{1,0:T(8,128)(2,1)S(1)} %copy-done, bf16[12,128,128]{2,1,0:T(8,128)(2,1)S(1)} %constant_dynamic-update-slice_fusion.refs_0_, bf16[12,128,128]{2,1,0:T(8,128)(2,1)S(1)} %copy-done.11, ...), custom_call_target="tpu_custom_call" | custom-call | tf_op jit(solution)/shard_map/pallas_call | solution.py:123
  158.8 2.7 %collective-permute-done.23.recv_ref = f32[1024,256]{1,0:T(8,128)S(1)} collective-permute-done((f32[1024,256]{1,0:T(8,128)S(1)}, f32[1024,256]{1,0:T(8,128)S(1)}, u32[]{:S(2)}, u32[]{:S(2)}) %collective-permute-start.23) | collective-permute-done | bytes 1048608 | tf_op jit(solution)/shard_map/ppermute | solution.py:210
  162.5 2.8 %shard_map.39 = (f32[1024,256]{1,0:T(8,128)}, f32[1,256]{1,0:T(1,128)}) custom-call(f32[1024,256]{1,0:T(8,128)} %copy-done.1, f32[1024,256]{1,0:T(8,128)} %copy-done.24), custom_call_target="tpu_custom_call" | custom-call | tf_op jit(solution)/shard_map/pallas_call | solution.py:157
  165.4 1.2 collective-permute-done.24
  167.3 3.6 %collective-permute-done.25 = f32[1,256]{1,0:T(1,128)S(1)} collective-permute-done((f32[1,256]{1,0:T(1,128)S(1)}, f32[1,256]{1,0:T(1,128)S(1)}, u32[]{:S(2)}, u32[]{:S(2)}) %collective-permute-start.25) | collective-permute-done | bytes 1056 | tf_op jit(solution)/shard_map/ppermute | solution.py:213
  170.8 5.1 %collective-permute-done.26 = f32[1,256]{1,0:T(1,128)S(1)} collective-permute-done((f32[1,256]{1,0:T(1,128)S(1)}, f32[1,256]{1,0:T(1,128)S(1)}, u32[]{:S(2)}, u32[]{:S(2)}) %collective-permute-start.26) | collective-permute-done | bytes 1056 | tf_op jit(solution)/shard_map/ppermute | solution.py:214
  176.5 2.3 %shard_map.40 = f32[1024,256]{1,0:T(8,128)} custom-call(f32[1024,256]{1,0:T(8,128)} %get-tuple-element.17.power_ref, f32[1,256]{1,0:T(1,128)} %add.11.sum_ref), custom_call_target="tpu_custom_call" | custom-call | tf_op jit(solution)/shard_map/pallas_call | solution.py:215
  (100 shorter events, 26.5 us)
Async XLA Ops:
  6.5 119.6 %all-gather.3.cloned.1.call-start = ((), (), s32[]{:S(2)}) async-start(), calls=%async_computation | async-start | bytes 2621440 | tf_op jit(solution)/shard_map/all_gather | solution.py:174
  10.7 34.4 %copy-start.25 = (bf16[5,128,128]{2,1,0:T(8,128)(2,1)S(1)}, bf16[5,128,128]{2,1,0:T(8,128)(2,1)}, u32[]{:S(2)}) copy-start(bf16[5,128,128]{2,1,0:T(8,128)(2,1)} %get-tuple-element.14) | copy-start | bytes 491524
  10.7 70.1 %copy-start.26 = (s32[1,16]{1,0:T(1,128)S(1)}, s32[1,16]{1,0:T(1,128)}, u32[]{:S(2)}) copy-start(s32[1,16]{1,0:T(1,128)} %get-tuple-element.12) | copy-start | bytes 196
  10.7 11.7 %collective-permute-start.10 = (bf16[5,128,128]{2,1,0:T(8,128)(2,1)}, bf16[5,128,128]{2,1,0:T(8,128)(2,1)S(1)}, u32[]{:S(2)}, u32[]{:S(2)}) collective-permute-start(bf16[5,128,128]{2,1,0:T(8,128)(2,1)} %get-tuple-element.14), channel_id=1, source_target_pairs={{0,4},{1,5},{2,6},{3,7},{4,8},{5,9},{6,10},{7,11},{8,12},{9,13},{1... | collective-permute-start | bytes 491528 | tf_op jit(solution)/shard_map/ppermute | solution.py:28
  12.7 13.8 %collective-permute-start.1 = (bf16[3,128,128]{2,1,0:T(8,128)(2,1)}, bf16[3,128,128]{2,1,0:T(8,128)(2,1)S(1)}, u32[]{:S(2)}, u32[]{:S(2)}) collective-permute-start(bf16[3,128,128]{2,1,0:T(8,128)(2,1)} %get-tuple-element.13), channel_id=1, source_target_pairs={{0,3},{1,0},{2,1},{3,2},{4,7},{5,4},{6,5},{7,6},{8,11},{9,8},{10,9... | collective-permute-start | bytes 294920 | tf_op jit(solution)/shard_map/ppermute | solution.py:28
  15.7 6.7 %collective-permute-start = (bf16[3,128,128]{2,1,0:T(8,128)(2,1)}, bf16[3,128,128]{2,1,0:T(8,128)(2,1)S(1)}, u32[]{:S(2)}, u32[]{:S(2)}) collective-permute-start(bf16[3,128,128]{2,1,0:T(8,128)(2,1)} %get-tuple-element.13), channel_id=1, source_target_pairs={{0,1},{1,2},{2,3},{3,0},{4,5},{5,6},{6,7},{7,4},{8,9},{9,10},{10,1... | collective-permute-start | bytes 294920 | tf_op jit(solution)/shard_map/ppermute | solution.py:28
  15.7 8.0 %collective-permute-start.11 = (bf16[5,128,128]{2,1,0:T(8,128)(2,1)}, bf16[5,128,128]{2,1,0:T(8,128)(2,1)S(1)}, u32[]{:S(2)}, u32[]{:S(2)}) collective-permute-start(bf16[5,128,128]{2,1,0:T(8,128)(2,1)} %get-tuple-element.14), channel_id=1, source_target_pairs={{0,28},{1,29},{2,30},{3,31},{4,0},{5,1},{6,2},{7,3},{8,4},{9,5},{1... | collective-permute-start | bytes 491528 | tf_op jit(solution)/shard_map/ppermute | solution.py:28
  22.4 22.6 %collective-permute-start.2 = (bf16[3,128,128]{2,1,0:T(8,128)(2,1)S(1)}, bf16[3,128,128]{2,1,0:T(8,128)(2,1)S(1)}, u32[]{:S(2)}, u32[]{:S(2)}) collective-permute-start(bf16[3,128,128]{2,1,0:T(8,128)(2,1)S(1)} %collective-permute-done), channel_id=1, source_target_pairs={{0,1},{1,2},{2,3},{3,0},{4,5},{5,6},{6,7},{7,4},{8,9},{9,10},{10,1... | collective-permute-start | bytes 294920 | tf_op jit(solution)/shard_map/ppermute | solution.py:28
  22.4 6.7 %collective-permute-start.15 = (bf16[5,128,128]{2,1,0:T(8,128)(2,1)S(1)}, bf16[5,128,128]{2,1,0:T(8,128)(2,1)S(1)}, u32[]{:S(2)}, u32[]{:S(2)}) collective-permute-start(bf16[5,128,128]{2,1,0:T(8,128)(2,1)S(1)} %collective-permute-done.10), channel_id=1, source_target_pairs={{0,4},{1,5},{2,6},{3,7},{4,8},{5,9},{6,10},{7,11},{8,12},{9,13},{1... | collective-permute-start | bytes 491528 | tf_op jit(solution)/shard_map/ppermute | solution.py:28
  23.7 6.2 %collective-permute-start.16 = (bf16[5,128,128]{2,1,0:T(8,128)(2,1)S(1)}, bf16[5,128,128]{2,1,0:T(8,128)(2,1)S(1)}, u32[]{:S(2)}, u32[]{:S(2)}) collective-permute-start(bf16[5,128,128]{2,1,0:T(8,128)(2,1)S(1)} %collective-permute-done.11), channel_id=1, source_target_pairs={{0,28},{1,29},{2,30},{3,31},{4,0},{5,1},{6,2},{7,3},{8,4},{9,5},{1... | collective-permute-start | bytes 491528 | tf_op jit(solution)/shard_map/ppermute | solution.py:28
  29.1 7.1 %collective-permute-start.17 = (bf16[5,128,128]{2,1,0:T(8,128)(2,1)S(1)}, bf16[5,128,128]{2,1,0:T(8,128)(2,1)S(1)}, u32[]{:S(2)}, u32[]{:S(2)}) collective-permute-start(bf16[5,128,128]{2,1,0:T(8,128)(2,1)S(1)} %collective-permute-done.15), channel_id=1, source_target_pairs={{0,4},{1,5},{2,6},{3,7},{4,8},{5,9},{6,10},{7,11},{8,12},{9,13},{1... | collective-permute-start | bytes 491528 | tf_op jit(solution)/shard_map/ppermute | solution.py:28
  30.0 6.4 %collective-permute-start.18 = (bf16[5,128,128]{2,1,0:T(8,128)(2,1)S(1)}, bf16[5,128,128]{2,1,0:T(8,128)(2,1)S(1)}, u32[]{:S(2)}, u32[]{:S(2)}) collective-permute-start(bf16[5,128,128]{2,1,0:T(8,128)(2,1)S(1)} %collective-permute-done.16), channel_id=1, source_target_pairs={{0,28},{1,29},{2,30},{3,31},{4,0},{5,1},{6,2},{7,3},{8,4},{9,5},{1... | collective-permute-start | bytes 491528 | tf_op jit(solution)/shard_map/ppermute | solution.py:28
  36.2 6.5 %collective-permute-start.19 = (bf16[5,128,128]{2,1,0:T(8,128)(2,1)S(1)}, bf16[5,128,128]{2,1,0:T(8,128)(2,1)S(1)}, u32[]{:S(2)}, u32[]{:S(2)}) collective-permute-start(bf16[5,128,128]{2,1,0:T(8,128)(2,1)S(1)} %collective-permute-done.17), channel_id=1, source_target_pairs={{0,4},{1,5},{2,6},{3,7},{4,8},{5,9},{6,10},{7,11},{8,12},{9,13},{1... | collective-permute-start | bytes 491528 | tf_op jit(solution)/shard_map/ppermute | solution.py:28
  42.7 22.0 %collective-permute-start.20 = (bf16[25,128,128]{2,1,0:T(8,128)(2,1)S(1)}, bf16[25,128,128]{2,1,0:T(8,128)(2,1)S(1)}, u32[]{:S(2)}, u32[]{:S(2)}) collective-permute-start(bf16[25,128,128]{2,1,0:T(8,128)(2,1)S(1)} %constant_dynamic-update-slice_fusion.7.refs_12_), channel_id=1, source_target_pairs={{0,1},{1,2},{2,3},{3,0},{4,5},{5,6},{6,7},{7,4},{8,9},{9,10},{10,1... | collective-permute-start | bytes 2457608 | tf_op jit(solution)/shard_map/ppermute | solution.py:28
  45.0 12.1 %collective-permute-start.3 = (bf16[12,128,128]{2,1,0:T(8,128)(2,1)S(1)}, bf16[12,128,128]{2,1,0:T(8,128)(2,1)S(1)}, u32[]{:S(2)}, u32[]{:S(2)}) collective-permute-start(bf16[12,128,128]{2,1,0:T(8,128)(2,1)S(1)} %constant_dynamic-update-slice_fusion.refs_0_), channel_id=1, source_target_pairs={{0,4},{1,5},{2,6},{3,7},{4,8},{5,9},{6,10},{7,11},{8,12},{9,13},{1... | collective-permute-start | bytes 1179656 | tf_op jit(solution)/shard_map/ppermute | solution.py:28
  45.2 19.6 %collective-permute-start.13 = (bf16[15,128,128]{2,1,0:T(8,128)(2,1)S(1)}, bf16[15,128,128]{2,1,0:T(8,128)(2,1)S(1)}, u32[]{:S(2)}, u32[]{:S(2)}) collective-permute-start(bf16[15,128,128]{2,1,0:T(8,128)(2,1)S(1)} %constant_dynamic-update-slice_fusion.4.refs_8_), channel_id=1, source_target_pairs={{0,3},{1,0},{2,1},{3,2},{4,7},{5,4},{6,5},{7,6},{8,11},{9,8},{10,9... | collective-permute-start | bytes 1474568 | tf_op jit(solution)/shard_map/ppermute | solution.py:28
  47.6 11.3 %collective-permute-start.4 = (bf16[12,128,128]{2,1,0:T(8,128)(2,1)S(1)}, bf16[12,128,128]{2,1,0:T(8,128)(2,1)S(1)}, u32[]{:S(2)}, u32[]{:S(2)}) collective-permute-start(bf16[12,128,128]{2,1,0:T(8,128)(2,1)S(1)} %constant_dynamic-update-slice_fusion.refs_0_), channel_id=1, source_target_pairs={{0,28},{1,29},{2,30},{3,31},{4,0},{5,1},{6,2},{7,3},{8,4},{9,5},{1... | collective-permute-start | bytes 1179656 | tf_op jit(solution)/shard_map/ppermute | solution.py:28
  57.1 11.1 %collective-permute-start.5 = (bf16[12,128,128]{2,1,0:T(8,128)(2,1)S(1)}, bf16[12,128,128]{2,1,0:T(8,128)(2,1)S(1)}, u32[]{:S(2)}, u32[]{:S(2)}) collective-permute-start(bf16[12,128,128]{2,1,0:T(8,128)(2,1)S(1)} %collective-permute-done.3.refs_1_), channel_id=1, source_target_pairs={{0,4},{1,5},{2,6},{3,7},{4,8},{5,9},{6,10},{7,11},{8,12},{9,13},{1... | collective-permute-start | bytes 1179656 | tf_op jit(solution)/shard_map/ppermute | solution.py:28
  57.9 17.4 %collective-permute-start.12 = (bf16[15,128,128]{2,1,0:T(8,128)(2,1)S(1)}, bf16[15,128,128]{2,1,0:T(8,128)(2,1)S(1)}, u32[]{:S(2)}, u32[]{:S(2)}) collective-permute-start(bf16[15,128,128]{2,1,0:T(8,128)(2,1)S(1)} %constant_dynamic-update-slice_fusion.4.refs_8_), channel_id=1, source_target_pairs={{0,1},{1,2},{2,3},{3,0},{4,5},{5,6},{6,7},{7,4},{8,9},{9,10},{10,1... | collective-permute-start | bytes 1474568 | tf_op jit(solution)/shard_map/ppermute | solution.py:28
  58.9 65.5 %collective-permute-start.21 = (bf16[25,128,128]{2,1,0:T(8,128)(2,1)S(1)}, bf16[25,128,128]{2,1,0:T(8,128)(2,1)S(1)}, u32[]{:S(2)}, u32[]{:S(2)}) collective-permute-start(bf16[25,128,128]{2,1,0:T(8,128)(2,1)S(1)} %constant_dynamic-update-slice_fusion.7.refs_12_), channel_id=1, source_target_pairs={{0,3},{1,0},{2,1},{3,2},{4,7},{5,4},{6,5},{7,6},{8,11},{9,8},{10,9... | collective-permute-start | bytes 2457608 | tf_op jit(solution)/shard_map/ppermute | solution.py:28
  64.7 60.5 %collective-permute-start.22 = (bf16[25,128,128]{2,1,0:T(8,128)(2,1)S(1)}, bf16[25,128,128]{2,1,0:T(8,128)(2,1)S(1)}, u32[]{:S(2)}, u32[]{:S(2)}) collective-permute-start(bf16[25,128,128]{2,1,0:T(8,128)(2,1)S(1)} %collective-permute-done.20.refs_13_), channel_id=1, source_target_pairs={{0,1},{1,2},{2,3},{3,0},{4,5},{5,6},{6,7},{7,4},{8,9},{9,10},{10,1... | collective-permute-start | bytes 2457608 | tf_op jit(solution)/shard_map/ppermute | solution.py:28
  65.5 10.5 %collective-permute-start.6 = (bf16[12,128,128]{2,1,0:T(8,128)(2,1)S(1)}, bf16[12,128,128]{2,1,0:T(8,128)(2,1)S(1)}, u32[]{:S(2)}, u32[]{:S(2)}) collective-permute-start(bf16[12,128,128]{2,1,0:T(8,128)(2,1)S(1)} %collective-permute-done.4.refs_2_), channel_id=1, source_target_pairs={{0,28},{1,29},{2,30},{3,31},{4,0},{5,1},{6,2},{7,3},{8,4},{9,5},{1... | collective-permute-start | bytes 1179656 | tf_op jit(solution)/shard_map/ppermute | solution.py:28
  68.2 11.9 %collective-permute-start.7 = (bf16[12,128,128]{2,1,0:T(8,128)(2,1)S(1)}, bf16[12,128,128]{2,1,0:T(8,128)(2,1)S(1)}, u32[]{:S(2)}, u32[]{:S(2)}) collective-permute-start(bf16[12,128,128]{2,1,0:T(8,128)(2,1)S(1)} %collective-permute-done.5.refs_3_), channel_id=1, source_target_pairs={{0,4},{1,5},{2,6},{3,7},{4,8},{5,9},{6,10},{7,11},{8,12},{9,13},{1... | collective-permute-start | bytes 1179656 | tf_op jit(solution)/shard_map/ppermute | solution.py:28
  75.3 47.6 %collective-permute-start.14 = (bf16[15,128,128]{2,1,0:T(8,128)(2,1)S(1)}, bf16[15,128,128]{2,1,0:T(8,128)(2,1)S(1)}, u32[]{:S(2)}, u32[]{:S(2)}) collective-permute-start(bf16[15,128,128]{2,1,0:T(8,128)(2,1)S(1)} %collective-permute-done.12.refs_9_), channel_id=1, source_target_pairs={{0,1},{1,2},{2,3},{3,0},{4,5},{5,6},{6,7},{7,4},{8,9},{9,10},{10,1... | collective-permute-start | bytes 1474568 | tf_op jit(solution)/shard_map/ppermute | solution.py:28
  76.0 47.6 %collective-permute-start.8 = (bf16[12,128,128]{2,1,0:T(8,128)(2,1)S(1)}, bf16[12,128,128]{2,1,0:T(8,128)(2,1)S(1)}, u32[]{:S(2)}, u32[]{:S(2)}) collective-permute-start(bf16[12,128,128]{2,1,0:T(8,128)(2,1)S(1)} %collective-permute-done.6.refs_4_), channel_id=1, source_target_pairs={{0,28},{1,29},{2,30},{3,31},{4,0},{5,1},{6,2},{7,3},{8,4},{9,5},{1... | collective-permute-start | bytes 1179656 | tf_op jit(solution)/shard_map/ppermute | solution.py:28
  80.0 44.4 %collective-permute-start.9 = (bf16[12,128,128]{2,1,0:T(8,128)(2,1)S(1)}, bf16[12,128,128]{2,1,0:T(8,128)(2,1)S(1)}, u32[]{:S(2)}, u32[]{:S(2)}) collective-permute-start(bf16[12,128,128]{2,1,0:T(8,128)(2,1)S(1)} %collective-permute-done.7.refs_5_), channel_id=1, source_target_pairs={{0,4},{1,5},{2,6},{3,7},{4,8},{5,9},{6,10},{7,11},{8,12},{9,13},{1... | collective-permute-start | bytes 1179656 | tf_op jit(solution)/shard_map/ppermute | solution.py:28
  126.1 1.6 copy-start
  127.7 1.1 copy-start.3
  158.8 2.7 %collective-permute-start.23 = (f32[1024,256]{1,0:T(8,128)S(1)}, f32[1024,256]{1,0:T(8,128)S(1)}, u32[]{:S(2)}, u32[]{:S(2)}) collective-permute-start(f32[1024,256]{1,0:T(8,128)S(1)} %get-tuple-element.16), channel_id=1, source_target_pairs={{0,32},{32,0},{1,33},{33,1},{2,34},{34,2},{3,35},{35,3},{4,36},{36... | collective-permute-start | bytes 3145736 | tf_op jit(solution)/shard_map/ppermute | solution.py:210
  165.3 1.4 collective-permute-start.24
  167.3 3.6 %collective-permute-start.25 = (f32[1,256]{1,0:T(1,128)S(1)}, f32[1,256]{1,0:T(1,128)S(1)}, u32[]{:S(2)}, u32[]{:S(2)}) collective-permute-start(f32[1,256]{1,0:T(1,128)S(1)} %add.9), channel_id=1, source_target_pairs={{0,64},{64,0},{128,192},{192,128},{1,65},{65,1},{129,193},{193,129... | collective-permute-start | bytes 3080 | tf_op jit(solution)/shard_map/ppermute | solution.py:213
  170.8 5.1 %collective-permute-start.26 = (f32[1,256]{1,0:T(1,128)S(1)}, f32[1,256]{1,0:T(1,128)S(1)}, u32[]{:S(2)}, u32[]{:S(2)}) collective-permute-start(f32[1,256]{1,0:T(1,128)S(1)} %add.10), channel_id=1, source_target_pairs={{0,128},{64,192},{128,0},{192,64},{1,129},{65,193},{129,1},{193,65... | collective-permute-start | bytes 3080 | tf_op jit(solution)/shard_map/ppermute | solution.py:214
  (23 other events, 20.5 us)
Sparse Core Ops, SparseCore 0:
  9.2 35.3 all-gather.2

commit v2 on v0

v2 whole, which is shorter than its diff:
```python
import functools

import jax
import jax.numpy as jnp
from jax import lax
from jax.experimental import pallas as pl
from jax.experimental.pallas import tpu as pltpu
from jax.sharding import PartitionSpec as P

TILE = 128
CAP = 8
HEAD = 16
SLAB = CAP * TILE + HEAD
NX, NY, NZ = 4, 4, 8
ROWS = 2048
LEVELS = 65535
FINE = 64
BATCH = 4
MIB = 1024 * 1024
VMEM = pl.BlockSpec(memory_space=pltpu.VMEM)
SMEM = pl.BlockSpec(memory_space=pltpu.SMEM)


def struct(shape, dtype):
    return jax.ShapeDtypeStruct(shape, dtype)


def call(kernel, out_shape, *operands, first=VMEM, mib=8, **kwargs):
    many = isinstance(out_shape, (list, tuple))
    return pl.pallas_call(
        kernel,
        out_shape=out_shape,
        in_specs=[first] + [VMEM] * (len(operands) - 1),
        out_specs=[VMEM] * len(out_shape) if many else VMEM,
        compiler_params=pltpu.CompilerParams(vmem_limit_bytes=mib * MIB),
        **kwargs,
    )(*operands)


def after(x, *others):
    return lax.optimization_barrier((x, *others))[0]


def hop(x, dz, dy):
    pairs = []
    for c in range(2):
        s = 1 - 2 * c
        for z in range(NZ):
            for y in range(NY):
                to = (z + s * dz) % NZ * NY + (y + s * dy) % NY
                pairs.append((c * NZ * NY + z * NY + y, c * NZ * NY + to))
    return lax.ppermute(x, ("col", "layer"), pairs)


def hop_x(x, dx):
    pairs = []
    for c in range(2):
        s = 1 - 2 * c
        pairs += [(i * 2 + c, (i + s * dx) % NX * 2 + c) for i in range(NX)]
    return lax.ppermute(x, ("row", "col"), pairs)


def swap(x):
    return lax.ppermute(x, "col", [(0, 1), (1, 0)])


def place():
    layer, core = lax.axis_index("layer"), lax.axis_index("col")
    return layer // NY, layer % NY, core, 1 - 2 * core


def pack_kernel(map_ref, a_ref, out_ref):
    lane = lax.broadcasted_iota(jnp.int32, (HEAD, TILE), 1)

    def step(t, carry):
        n, head = carry
        present = map_ref[0, t] != 0

        @pl.when(jnp.logical_and(present, n < CAP))
        def _():
            rows = pl.ds(pl.multiple_of(t * TILE, TILE), TILE)
            out_ref[pl.ds(pl.multiple_of(n * TILE, TILE), TILE), :] = a_ref[rows, :]

        head = jnp.where(jnp.logical_and(lane == n, present), t.astype(jnp.float32), head)
        return n + present.astype(jnp.int32), head

    count, head = lax.fori_loop(
        0, 16, step, (jnp.int32(0), jnp.zeros((HEAD, TILE), jnp.float32))
    )
    head = jnp.where(lane == CAP, count.astype(jnp.float32), head)
    out_ref[CAP * TILE :, :] = head.astype(out_ref.dtype)


def split_kernel(b_ref, keep_ref, send_ref):
    core = lax.axis_index("col")
    left, right = b_ref[:, :TILE], b_ref[:, TILE:]
    keep_ref[...] = jnp.where(core == 0, left, right)
    send_ref[...] = jnp.where(core == 0, right, left)


def block_kernel(keep_ref, recv_ref, *out_refs):
    _, y, _, s = place()
    for d, out_ref in zip((0, 1, -1, 2), out_refs):
        to = (y + s * d + NY) % NY
        for r, ref in enumerate((keep_ref, recv_ref)):
            for low in range(2):
                rows = pl.ds(pl.multiple_of((low * NY + to) * TILE, TILE), TILE)
                at = (r * 2 + low) * TILE
                out_ref[at : at + TILE, :] = ref[rows, :]


def widen_kernel(*refs):
    for i, ref in enumerate(refs[:-1]):
        refs[-1][:, i * TILE : (i + 1) * TILE] = ref[...]


def stack_kernel(own_ref, far_ref, back_ref, ahead_ref, out_ref):
    x, s = lax.axis_index("row"), 1 - 2 * lax.axis_index("col")
    for d, ref in ((0, own_ref), (-1, back_ref), (1, ahead_ref), (2, far_ref)):
        out_ref[(x + s * d + NX) % NX] = ref[...]


def join_kernel(*refs):
    for i, ref in enumerate(refs[:-1]):
        refs[-1][i] = ref[...]


def join(parts):
    return call(join_kernel, struct((len(parts), *parts[0].shape), parts[0].dtype), *parts)


def product_kernel(plan, *refs):
    n = len(plan)
    b_ref, parts = refs[0], refs[1 : n + 1]
    total_ref, heads_ref, table_ref, work_ref, sem = refs[n + 1 :]
    at = 0
    for part, (_, steps) in zip(parts, plan):
        for j in range(len(steps)):
            head = part[j, CAP * TILE :, :].astype(jnp.float32)
            heads_ref[at : at + 1, :] = head[0:1, :].astype(jnp.int32)
            at += 1
    copy = pltpu.make_async_copy(heads_ref, table_ref, sem)
    copy.start()
    total_ref[...] = jnp.zeros_like(total_ref)
    z, _, _, s = place()
    copy.wait()

    at = 0
    for part, (other, steps) in zip(parts, plan):
        count = jnp.int32(0)
        for j, dz in enumerate(steps):
            source = (z + (-s if other else s) * dz + NZ) % NZ

            def list_tile(i, count, j=j, at=at, source=source, other=other):
                work_ref[0, count] = j
                work_ref[1, count] = i
                work_ref[2, count] = table_ref[at, i]
                work_ref[3, count] = source // 2
                work_ref[4, count] = other * 2 + source % 2
                return count + 1

            count = lax.fori_loop(0, table_ref[at, CAP], list_tile, count)
            at += 1
        for u in range(BATCH - 1):
            for k, v in enumerate((0, 0, ROWS // TILE, 0, 0)):
                work_ref[k, count + u] = v

        def step(g, carry, part=part):
            for u in range(BATCH):
                j, i, t, panel, at_b = (work_ref[k, g * BATCH + u] for k in range(5))
                rows = pl.ds(pl.multiple_of(t * TILE, TILE), TILE)
                total_ref[rows, :] += jnp.dot(
                    part[j, pl.ds(pl.multiple_of(i * TILE, TILE), TILE), :],
                    b_ref[panel, pl.ds(pl.multiple_of(at_b * TILE, TILE), TILE), :],
                    preferred_element_type=jnp.float32,
                )
            return carry

        lax.fori_loop(0, (count + BATCH - 1) // BATCH, step, 0)


def product(b_panel, parts, plan):
    cols = b_panel.shape[2]
    count = sum(len(steps) for _, steps in plan)
    flops = sum(p.size for p in parts) * cols * 2
    return call(
        functools.partial(product_kernel, tuple(plan)),
        struct((ROWS + TILE, cols), jnp.float32),
        b_panel,
        *parts,
        mib=20,
        scratch_shapes=[
            pltpu.VMEM((count, TILE), jnp.int32),
            pltpu.SMEM((count, TILE), jnp.int32),
            pltpu.SMEM((8, TILE), jnp.int32),
            pltpu.SemaphoreType.DMA(()),
        ],
        cost_estimate=pl.CostEstimate(flops=flops, bytes_accessed=flops // 128, transcendentals=0),
    )


def encode_kernel(slot, total_ref, out_ref):
    lanes = slice(slot * TILE, (slot + 1) * TILE)
    top = total_ref[:TILE, lanes]
    for i in range(1, ROWS // TILE):
        top = jnp.maximum(top, total_ref[i * TILE : (i + 1) * TILE, lanes])
    top = jnp.maximum(jnp.max(top, axis=0, keepdims=True), jnp.float32(2.0**-100))
    exponent = jnp.ceil(jnp.log2(top) * FINE)
    inverse = LEVELS * jnp.exp2(exponent * (-1.0 / FINE))
    for i in range(ROWS // TILE):
        part = slice(i * TILE, (i + 1) * TILE)
        steps = jnp.minimum(total_ref[part, lanes] * inverse + 0.5, jnp.float32(LEVELS))
        out_ref[part, :] = (steps.astype(jnp.int32) - 32768).astype(jnp.int16)
    exponent = jnp.broadcast_to(exponent, (HEAD, TILE)).astype(jnp.int32)
    out_ref[ROWS:, :] = exponent.astype(jnp.int16)


def encode(total, slot):
    return call(
        functools.partial(encode_kernel, slot), struct((ROWS + HEAD, TILE), jnp.int16), total
    )


def square_kernel(weight, total_ref, *refs):
    recv, (keep_ref, send_ref, sum_ref) = refs[:3], refs[3:]
    core = lax.axis_index("col")
    first_col = lax.axis_index("layer") * 2 * TILE + core * TILE
    scales = []
    for ref in recv:
        exponent = ref[ROWS:, :].astype(jnp.int32).astype(jnp.float32)[0:1, :]
        scales.append(jnp.exp2(exponent * (1.0 / FINE)) * jnp.float32(1.0 / LEVELS))
    row = lax.broadcasted_iota(jnp.int32, (TILE, TILE), 0)
    col = lax.broadcasted_iota(jnp.int32, (TILE, TILE), 1)
    column = jnp.zeros((TILE, TILE), jnp.float32)
    half = ROWS // 2
    for i in range(half // TILE):
        for own, out_ref in ((1, keep_ref), (0, send_ref)):
            start = (core if own else 1 - core) * half + i * TILE
            part = pl.ds(pl.multiple_of(start, TILE), TILE)
            first_row = lax.axis_index("row") * ROWS + start
            diagonal = row + (first_row - first_col) == col
            expanded = total_ref[part, :TILE] + jnp.where(
                diagonal, jnp.float32(weight), jnp.float32(0)
            )
            for ref, scale in zip(recv, scales):
                steps = ref[part, :].astype(jnp.int32) + 32768
                expanded += steps.astype(jnp.float32) * scale
            power = expanded * expanded
            out_ref[i * TILE : (i + 1) * TILE, :] = power
            column += power
    sum_ref[...] = jnp.sum(column, axis=0, keepdims=True)


def scale_kernel(n_total, keep_ref, recv_ref, *refs):
    out_ref = refs[-1]
    total = refs[0][...]
    for ref in refs[1:-1]:
        total += ref[...]
    core = lax.axis_index("col")
    own = jnp.float32(n_total) * keep_ref[...] / total[0:1, :]
    other = jnp.float32(n_total) * recv_ref[...] / total[1:2, :]
    out_ref[:, :TILE] = jnp.where(core == 0, own, other)
    out_ref[:, TILE:] = jnp.where(core == 0, other, own)


def on_device(a_matrix, b_matrix, tile_map):
    n_total = a_matrix.shape[1] * 64
    half = ROWS // 2
    keep, send = call(split_kernel, [struct((half, TILE), b_matrix.dtype)] * 2, b_matrix)
    recv = swap(send)
    p = call(
        pack_kernel,
        struct((SLAB, TILE), a_matrix.dtype),
        tile_map.reshape(1, 16),
        a_matrix,
        first=SMEM,
    )
    a1, b1 = hop(p, 1, 0), hop(p, -1, 0)
    blocks = call(block_kernel, [struct((512, TILE), b_matrix.dtype)] * 4, keep, recv)
    blocks = [blocks[0]] + [hop(m, 0, d) for m, d in zip(blocks[1:], (1, -1, 2))]
    wide = call(widen_kernel, struct((512, 4 * TILE), b_matrix.dtype), *blocks)

    a1, b1 = after(a1, wide), after(b1, wide)
    a2, b2 = hop(a1, 1, 0), hop(b1, -1, 0)
    back, ahead = hop_x(wide, 1), hop_x(wide, -1)
    near = join([p, a1, b1, a2, b2])
    a2, b2 = after(a2, back), after(b2, back)
    a4, a3, b3 = hop(a2, 2, 0), hop(a2, 1, 0), hop(b2, -1, 0)
    across = hop_x(back, 1)
    near_other = swap(near)
    far = join([after(a3, across, ahead), b3, a4])
    far_other = swap(far)
    panel = call(
        stack_kernel, struct((NX, 512, 4 * TILE), b_matrix.dtype), wide, across, back, ahead
    )
    near_steps, far_steps = (0, -1, 1, -2, 2), (-3, 3, -4)
    total = product(
        panel,
        [near, near_other, far, far_other],
        [(0, near_steps), (1, near_steps), (0, far_steps), (1, far_steps)],
    )

    sums = [hop(encode(total, slot), 0, d) for slot, d in ((3, 2), (1, -1), (2, 1))]
    keep, send, column = call(
        functools.partial(square_kernel, n_total / 32),
        [struct((half, TILE), jnp.float32)] * 2 + [struct((1, TILE), jnp.float32)],
        total,
        *sums,
    )
    column = jnp.concatenate([column, swap(column)])
    recv = swap(send)
    columns = [column] + [hop_x(column, d) for d in (1, -1, 2)]
    return call(
        functools.partial(scale_kernel, n_total),
        struct((half, 2 * TILE), jnp.float32),
        keep,
        recv,
        *columns,
    )


def solution(mesh):
    return jax.shard_map(
        on_device,
        mesh=mesh,
        in_specs=(
            P("row", ("col", "layer")),
            P(("col", "row"), "layer"),
            P("row", ("col", "layer")),
        ),
        out_specs=P(("row", "col"), "layer"),
        check_vma=False,
    )
```

time: 249 us -> 97.9 us (0.39)
  waiting for transfers between devices: 201 us -> 54.1 us
  starting transfers between devices: 0.08 us -> 29.9 us
  between operations: 13.1 us -> 0.15 us
  matrix products: 12.4 us -> 0 us
  blocking collectives: 12.1 us -> 0 us
  Pallas kernels: 0 us -> 9.6 us
  other arithmetic: 6.79 us -> 0.01 us
  local copies, waits for them, and re-layouts: 0.07 us -> 2.74 us
    all_gather x2 -> x0, waiting for transfers between devices: 188 us -> none  [the longest x1 154 us: on_device(): lax.all_gather(masked, 'layer', axis=1, tiled=True)]
    ppermute x0 -> x24, waiting for transfers between devices: none -> 54.1 us  [the longest x13 45.5 us: hop(): return lax.ppermute(x, ('col', 'layer'), pairs)]
    ppermute x0 -> x24, starting transfers between devices: none -> 29.9 us  [the longest x13 22 us: hop(): return lax.ppermute(x, ('col', 'layer'), pairs)]
    dot_general x1 -> x0, matrix products: 12.4 us -> none  [on_device(): jnp.dot(lax.all_gather(masked, 'layer', axis=1, tiled=True), b_panel, pre...]
    psum x1 -> x0, blocking collectives: 12.1 us -> none  [on_device(): column_total = lax.psum(jnp.sum(power, axis=0), ('row', 'col'))]
    reduce_scatter x1 -> x0, waiting for transfers between devices: 11.9 us -> none  [on_device(): lax.psum_scatter(partial_sum, 'col', scatter_dimension=0, tiled=True)]
    pallas_call x0 -> x13, Pallas kernels: none -> 9.6 us  [call(): pl.pallas_call(kernel, out_shape=out_shape, in_specs=[first] + [VMEM] * (...]
    unnamed x0 -> x6, local copies, waits for them, and re-layouts: none -> 2.74 us
  transfers between devices with their start and end apart: 3 -> 24, of which waited for: 3 -> 12; matrix products, arithmetic and copies ran while one was open for 1% -> 0% of each run, Pallas kernels for 0% -> 1%
where the time goes in v2:
time: 97.9 us; the launch traced here: 96.5 us
  waiting for transfers between devices  54.1 us (55%)
  starting transfers between devices  29.9 us (31%)
  Pallas kernels  9.6 us (10%)
  local copies, waits for them, and re-layouts  2.74 us (3%)
    ppermute x13, waiting for transfers between devices, hop(): return lax.ppermute(x, ('col', 'layer'), pairs)  45.5 us
    ppermute x13, starting transfers between devices, hop(): return lax.ppermute(x, ('col', 'layer'), pairs)  22 us
    pallas_call x13, Pallas kernels, call(): pl.pallas_call(kernel, out_shape=out_shape, in_specs=[first] + [VMEM] * (...  9.6 us
    ppermute x6, starting transfers between devices, hop_x(): return lax.ppermute(x, ('row', 'col'), pairs)  6.87 us
    ppermute x5, waiting for transfers between devices, swap(): return lax.ppermute(x, 'col', [(0, 1), (1, 0)])  5.04 us
    ppermute x6, waiting for transfers between devices, hop_x(): return lax.ppermute(x, ('row', 'col'), pairs)  3.57 us
    unnamed x6, local copies, waits for them, and re-layouts  2.74 us
  transfers between devices with their start and end apart: 24, of which 12 were waited for; matrix products, arithmetic and copies ran while one was open for 0% of the time, Pallas kernels for 1%

profile of v2, /device:TPU:2, one launch (start us, length us, event | category | flops | bytes accessed | tf_op | source)
XLA Modules:
  0.0 96.5 jit_solution(4779281246336716322)
XLA Ops:
  0.0 1.0 %copy-done = bf16[1024,256]{1,0:T(8,128)(2,1)S(1)} copy-done((bf16[1024,256]{1,0:T(8,128)(2,1)S(1)}, bf16[1024,256]{1,0:T(8,128)(2,1)}, u32[]{:S(2)}) %copy-start) | copy-done | bytes 524312
  1.3 1.5 %collective-permute-done.recv_ref = bf16[1024,128]{1,0:T(8,128)(2,1)S(1)} collective-permute-done((bf16[1024,128]{1,0:T(8,128)(2,1)S(1)}, bf16[1024,128]{1,0:T(8,128)(2,1)S(1)}, u32[]{:S(2)}, u32[]{:S(2)}) %collective-permute-start) | collective-permute-done | bytes 262176 | tf_op jit(solution)/shard_map/ppermute | solution.py:64
  2.8 1.7 %collective-permute-start.1 = (bf16[512,128]{1,0:T(8,128)(2,1)S(1)}, bf16[512,128]{1,0:T(8,128)(2,1)S(1)}, u32[]{:S(2)}, u32[]{:S(2)}) collective-permute-start(bf16[512,128]{1,0:T(8,128)(2,1)S(1)} %get-tuple-element.22), channel_id=1, source_target_pairs={{0,1},{1,2},{2,3},{3,0},{4,5},{5,6},{6,7},{7,4},{8,9},{9,10},{10,1... | collective-permute-start | bytes 393224 | tf_op jit(solution)/shard_map/ppermute | solution.py:52
  4.5 1.7 %collective-permute-start.2 = (bf16[512,128]{1,0:T(8,128)(2,1)S(1)}, bf16[512,128]{1,0:T(8,128)(2,1)S(1)}, u32[]{:S(2)}, u32[]{:S(2)}) collective-permute-start(bf16[512,128]{1,0:T(8,128)(2,1)S(1)} %get-tuple-element.23), channel_id=1, source_target_pairs={{0,3},{1,0},{2,1},{3,2},{4,7},{5,4},{6,5},{7,6},{8,11},{9,8},{10,9... | collective-permute-start | bytes 393224 | tf_op jit(solution)/shard_map/ppermute | solution.py:52
  6.1 2.0 %collective-permute-start.3 = (bf16[512,128]{1,0:T(8,128)(2,1)S(1)}, bf16[512,128]{1,0:T(8,128)(2,1)S(1)}, u32[]{:S(2)}, u32[]{:S(2)}) collective-permute-start(bf16[512,128]{1,0:T(8,128)(2,1)S(1)} %get-tuple-element.24), channel_id=1, source_target_pairs={{0,2},{1,3},{2,0},{3,1},{4,6},{5,7},{6,4},{7,5},{8,10},{9,11},{10,... | collective-permute-start | bytes 393224 | tf_op jit(solution)/shard_map/ppermute | solution.py:52
  8.1 1.0 %copy-done.1 = bf16[2048,128]{1,0:T(8,128)(2,1)S(1)} copy-done((bf16[2048,128]{1,0:T(8,128)(2,1)S(1)}, bf16[2048,128]{1,0:T(8,128)(2,1)}, u32[]{:S(2)}) %copy-start.1) | copy-done | bytes 524312
  9.2 0.7 copy-done.2
  9.8 0.8 shard_map.41.refs_0_
  10.6 5.9 %collective-permute-start.8 = (bf16[1040,128]{1,0:T(8,128)(2,1)S(1)}, bf16[1040,128]{1,0:T(8,128)(2,1)S(1)}, u32[]{:S(2)}, u32[]{:S(2)}) collective-permute-start(bf16[1040,128]{1,0:T(8,128)(2,1)S(1)} %shard_map.41.refs_0_), channel_id=1, source_target_pairs={{0,28},{1,29},{2,30},{3,31},{4,0},{5,1},{6,2},{7,3},{8,4},{9,5},{1... | collective-permute-start | bytes 798728 | tf_op jit(solution)/shard_map/ppermute | solution.py:52
  16.7 1.6 %collective-permute-start.4 = (bf16[512,512]{1,0:T(8,128)(2,1)S(1)}, bf16[512,512]{1,0:T(8,128)(2,1)S(1)}, u32[]{:S(2)}, u32[]{:S(2)}) collective-permute-start(bf16[512,512]{1,0:T(8,128)(2,1)S(1)} %shard_map.39.own_ref), channel_id=1, source_target_pairs={{0,64},{64,128},{128,192},{192,0},{32,224},{96,32},{160,96},{224,1... | collective-permute-start | bytes 1572872 | tf_op jit(solution)/shard_map/ppermute | solution.py:60
  18.2 3.5 %collective-permute-done.8.refs_2_ = bf16[1040,128]{1,0:T(8,128)(2,1)S(1)} collective-permute-done((bf16[1040,128]{1,0:T(8,128)(2,1)S(1)}, bf16[1040,128]{1,0:T(8,128)(2,1)S(1)}, u32[]{:S(2)}, u32[]{:S(2)}) %collective-permute-start.8) | collective-permute-done | bytes 266272 | tf_op jit(solution)/shard_map/ppermute | solution.py:52
  21.7 2.4 %collective-permute-done.7.refs_1_ = bf16[1040,128]{1,0:T(8,128)(2,1)S(1)} collective-permute-done((bf16[1040,128]{1,0:T(8,128)(2,1)S(1)}, bf16[1040,128]{1,0:T(8,128)(2,1)S(1)}, u32[]{:S(2)}, u32[]{:S(2)}) %collective-permute-start.7) | collective-permute-done | bytes 266272 | tf_op jit(solution)/shard_map/ppermute | solution.py:52
  24.2 3.2 %collective-permute-start.10 = (bf16[1040,128]{1,0:T(8,128)(2,1)S(1)}, bf16[1040,128]{1,0:T(8,128)(2,1)S(1)}, u32[]{:S(2)}, u32[]{:S(2)}) collective-permute-start(bf16[1040,128]{1,0:T(8,128)(2,1)S(1)} %collective-permute-done.8.refs_2_), channel_id=1, source_target_pairs={{0,28},{1,29},{2,30},{3,31},{4,0},{5,1},{6,2},{7,3},{8,4},{9,5},{1... | collective-permute-start | bytes 798728 | tf_op jit(solution)/shard_map/ppermute | solution.py:52
  27.4 0.5 collective-permute-start.6
  27.9 5.2 %collective-permute-done.9.refs_3_ = bf16[1040,128]{1,0:T(8,128)(2,1)S(1)} collective-permute-done((bf16[1040,128]{1,0:T(8,128)(2,1)S(1)}, bf16[1040,128]{1,0:T(8,128)(2,1)S(1)}, u32[]{:S(2)}, u32[]{:S(2)}) %collective-permute-start.9) | collective-permute-done | bytes 266272 | tf_op jit(solution)/shard_map/ppermute | solution.py:52
  33.3 1.6 %collective-permute-start.5 = (bf16[512,512]{1,0:T(8,128)(2,1)S(1)}, bf16[512,512]{1,0:T(8,128)(2,1)S(1)}, u32[]{:S(2)}, u32[]{:S(2)}) collective-permute-start(bf16[512,512]{1,0:T(8,128)(2,1)S(1)} %collective-permute-done.4.back_ref), channel_id=1, source_target_pairs={{0,64},{64,128},{128,192},{192,0},{32,224},{96,32},{160,96},{224,1... | collective-permute-start | bytes 1572872 | tf_op jit(solution)/shard_map/ppermute | solution.py:60
  34.9 2.5 %collective-permute-start.12 = (bf16[1040,128]{1,0:T(8,128)(2,1)S(1)}, bf16[1040,128]{1,0:T(8,128)(2,1)S(1)}, u32[]{:S(2)}, u32[]{:S(2)}) collective-permute-start(bf16[1040,128]{1,0:T(8,128)(2,1)S(1)} %collective-permute-done.9.refs_3_), channel_id=1, source_target_pairs={{0,4},{1,5},{2,6},{3,7},{4,8},{5,9},{6,10},{7,11},{8,12},{9,13},{1... | collective-permute-start | bytes 798728 | tf_op jit(solution)/shard_map/ppermute | solution.py:52
  37.5 0.7 collective-permute-start.13
  38.1 11.6 %collective-permute-done.12.refs_0_ = bf16[1040,128]{1,0:T(8,128)(2,1)S(1)} collective-permute-done((bf16[1040,128]{1,0:T(8,128)(2,1)S(1)}, bf16[1040,128]{1,0:T(8,128)(2,1)S(1)}, u32[]{:S(2)}, u32[]{:S(2)}) %collective-permute-start.12) | collective-permute-done | bytes 266272 | tf_op jit(solution)/shard_map/ppermute | solution.py:52
  50.3 2.1 %collective-permute-done.15.refs_4_ = bf16[3,1040,128]{2,1,0:T(8,128)(2,1)S(1)} collective-permute-done((bf16[3,1040,128]{2,1,0:T(8,128)(2,1)S(1)}, bf16[3,1040,128]{2,1,0:T(8,128)(2,1)S(1)}, u32[]{:S(2)}, u32[]{:S(2)}) %collective-permute-start.15) | collective-permute-done | bytes 798752 | tf_op jit(solution)/shard_map/ppermute | solution.py:64
  52.4 5.2 %shard_map.44.total_ref = f32[2176,512]{1,0:T(8,128)S(1)} custom-call(bf16[4,512,512]{2,1,0:T(8,128)(2,1)S(1)} %shard_map.40.refs_0_, bf16[5,1040,128]{2,1,0:T(8,128)(2,1)S(1)} %shard_map.42.refs_1_, bf16[5,1040,128]{2,1,0:T(8,128)(2,1)S(1)} %collective-permute-done.11.refs_2_, bf16[3,1040,128]{2,1,0:T(8,128)(2,1)S(1)} %shard_map.43.refs_3_, ...), custom_call_target="tpu_custom_call" | custom-call | flops 2181038080 | bytes 17039360 | tf_op jit(solution)/shard_map/pallas_call | solution.py:30
  59.2 3.9 %collective-permute-start.17 = (s16[2064,128]{1,0:T(8,128)(2,1)S(1)}, s16[2064,128]{1,0:T(8,128)(2,1)S(1)}, u32[]{:S(2)}, u32[]{:S(2)}) collective-permute-start(s16[2064,128]{1,0:T(8,128)(2,1)S(1)} %shard_map.46), channel_id=1, source_target_pairs={{0,3},{1,0},{2,1},{3,2},{4,7},{5,4},{6,5},{7,6},{8,11},{9,8},{10,9... | collective-permute-start | bytes 1585160 | tf_op jit(solution)/shard_map/ppermute | solution.py:52
  63.1 12.2 %collective-permute-done.16.refs_0_ = s16[2064,128]{1,0:T(8,128)(2,1)S(1)} collective-permute-done((s16[2064,128]{1,0:T(8,128)(2,1)S(1)}, s16[2064,128]{1,0:T(8,128)(2,1)S(1)}, u32[]{:S(2)}, u32[]{:S(2)}) %collective-permute-start.16) | collective-permute-done | bytes 528416 | tf_op jit(solution)/shard_map/ppermute | solution.py:52
  75.3 8.8 %collective-permute-done.17.refs_1_ = s16[2064,128]{1,0:T(8,128)(2,1)S(1)} collective-permute-done((s16[2064,128]{1,0:T(8,128)(2,1)S(1)}, s16[2064,128]{1,0:T(8,128)(2,1)S(1)}, u32[]{:S(2)}, u32[]{:S(2)}) %collective-permute-start.17) | collective-permute-done | bytes 528416 | tf_op jit(solution)/shard_map/ppermute | solution.py:52
  84.1 1.7 %collective-permute-done.18.refs_2_ = s16[2064,128]{1,0:T(8,128)(2,1)S(1)} collective-permute-done((s16[2064,128]{1,0:T(8,128)(2,1)S(1)}, s16[2064,128]{1,0:T(8,128)(2,1)S(1)}, u32[]{:S(2)}, u32[]{:S(2)}) %collective-permute-start.18) | collective-permute-done | bytes 528416 | tf_op jit(solution)/shard_map/ppermute | solution.py:52
  85.8 0.7 shard_map.48
  87.2 1.4 %collective-permute-done.20 = f32[1,128]{1,0:T(1,128)S(1)} collective-permute-done((f32[1,128]{1,0:T(1,128)S(1)}, f32[1,128]{1,0:T(1,128)S(1)}, u32[]{:S(2)}, u32[]{:S(2)}) %collective-permute-start.20) | collective-permute-done | bytes 544 | tf_op jit(solution)/shard_map/ppermute | solution.py:64
  88.6 1.0 %collective-permute-start.23 = (f32[2,128]{1,0:T(2,128)S(1)}, f32[2,128]{1,0:T(2,128)S(1)}, u32[]{:S(2)}, u32[]{:S(2)}) collective-permute-start(f32[2,128]{1,0:T(2,128)S(1)} %pad_maximum_fusion.refs_0_), channel_id=1, source_target_pairs={{0,128},{64,192},{128,0},{192,64},{32,160},{96,224},{160,32},{224,... | collective-permute-start | bytes 3080 | tf_op jit(solution)/shard_map/ppermute | solution.py:60
  89.6 2.2 %collective-permute-start.22 = (f32[2,128]{1,0:T(2,128)S(1)}, f32[2,128]{1,0:T(2,128)S(1)}, u32[]{:S(2)}, u32[]{:S(2)}) collective-permute-start(f32[2,128]{1,0:T(2,128)S(1)} %pad_maximum_fusion.refs_0_), channel_id=1, source_target_pairs={{0,192},{64,0},{128,64},{192,128},{32,96},{96,160},{160,224},{224,... | collective-permute-start | bytes 3080 | tf_op jit(solution)/shard_map/ppermute | solution.py:60
  91.8 1.9 %collective-permute-done.23.refs_3_ = f32[2,128]{1,0:T(2,128)S(1)} collective-permute-done((f32[2,128]{1,0:T(2,128)S(1)}, f32[2,128]{1,0:T(2,128)S(1)}, u32[]{:S(2)}, u32[]{:S(2)}) %collective-permute-start.23) | collective-permute-done | bytes 1056 | tf_op jit(solution)/shard_map/ppermute | solution.py:60
  93.7 1.7 %collective-permute-done.21.refs_1_ = f32[2,128]{1,0:T(2,128)S(1)} collective-permute-done((f32[2,128]{1,0:T(2,128)S(1)}, f32[2,128]{1,0:T(2,128)S(1)}, u32[]{:S(2)}, u32[]{:S(2)}) %collective-permute-start.21) | collective-permute-done | bytes 1056 | tf_op jit(solution)/shard_map/ppermute | solution.py:60
  95.3 1.1 %shard_map.49 = f32[1024,256]{1,0:T(8,128)} custom-call(f32[1024,128]{1,0:T(8,128)S(1)} %get-tuple-element.30.keep_ref, f32[1024,128]{1,0:T(8,128)S(1)} %collective-permute-done.19.recv_ref, f32[2,128]{1,0:T(2,128)S(1)} %pad_maximum_fusion.refs_0_, f32[2,128]{1,0:T(2,128)S(1)} %collective-permute-done.21.refs_1_, ...), custom_call_target="tpu_custom_call" | custom-call | tf_op jit(solution)/shard_map/pallas_call | solution.py:30
  (36 shorter events, 3.2 us)
Async XLA Ops:
  0.0 1.0 %copy-start = (bf16[1024,256]{1,0:T(8,128)(2,1)S(1)}, bf16[1024,256]{1,0:T(8,128)(2,1)}, u32[]{:S(2)}) copy-start(bf16[1024,256]{1,0:T(8,128)(2,1)} %b_ref.1) | copy-start | bytes 1572868
  1.2 1.6 %collective-permute-start = (bf16[1024,128]{1,0:T(8,128)(2,1)S(1)}, bf16[1024,128]{1,0:T(8,128)(2,1)S(1)}, u32[]{:S(2)}, u32[]{:S(2)}) collective-permute-start(bf16[1024,128]{1,0:T(8,128)(2,1)S(1)} %get-tuple-element.20), channel_id=1, source_target_pairs={{0,32},{32,0},{1,33},{33,1},{2,34},{34,2},{3,35},{35,3},{4,36},{36... | collective-permute-start | bytes 786440 | tf_op jit(solution)/shard_map/ppermute | solution.py:64
  2.8 13.7 %collective-permute-start.1 = (bf16[512,128]{1,0:T(8,128)(2,1)S(1)}, bf16[512,128]{1,0:T(8,128)(2,1)S(1)}, u32[]{:S(2)}, u32[]{:S(2)}) collective-permute-start(bf16[512,128]{1,0:T(8,128)(2,1)S(1)} %get-tuple-element.22), channel_id=1, source_target_pairs={{0,1},{1,2},{2,3},{3,0},{4,5},{5,6},{6,7},{7,4},{8,9},{9,10},{10,1... | collective-permute-start | bytes 393224 | tf_op jit(solution)/shard_map/ppermute | solution.py:52
  4.5 12.1 %collective-permute-start.2 = (bf16[512,128]{1,0:T(8,128)(2,1)S(1)}, bf16[512,128]{1,0:T(8,128)(2,1)S(1)}, u32[]{:S(2)}, u32[]{:S(2)}) collective-permute-start(bf16[512,128]{1,0:T(8,128)(2,1)S(1)} %get-tuple-element.23), channel_id=1, source_target_pairs={{0,3},{1,0},{2,1},{3,2},{4,7},{5,4},{6,5},{7,6},{8,11},{9,8},{10,9... | collective-permute-start | bytes 393224 | tf_op jit(solution)/shard_map/ppermute | solution.py:52
  6.1 10.4 %collective-permute-start.3 = (bf16[512,128]{1,0:T(8,128)(2,1)S(1)}, bf16[512,128]{1,0:T(8,128)(2,1)S(1)}, u32[]{:S(2)}, u32[]{:S(2)}) collective-permute-start(bf16[512,128]{1,0:T(8,128)(2,1)S(1)} %get-tuple-element.24), channel_id=1, source_target_pairs={{0,2},{1,3},{2,0},{3,1},{4,6},{5,7},{6,4},{7,5},{8,10},{9,11},{10,... | collective-permute-start | bytes 393224 | tf_op jit(solution)/shard_map/ppermute | solution.py:52
  8.1 1.0 %copy-start.1 = (bf16[2048,128]{1,0:T(8,128)(2,1)S(1)}, bf16[2048,128]{1,0:T(8,128)(2,1)}, u32[]{:S(2)}) copy-start(bf16[2048,128]{1,0:T(8,128)(2,1)} %a_ref.1) | copy-start | bytes 1572868
  9.2 0.7 copy-start.2
  10.6 11.1 %collective-permute-start.8 = (bf16[1040,128]{1,0:T(8,128)(2,1)S(1)}, bf16[1040,128]{1,0:T(8,128)(2,1)S(1)}, u32[]{:S(2)}, u32[]{:S(2)}) collective-permute-start(bf16[1040,128]{1,0:T(8,128)(2,1)S(1)} %shard_map.41.refs_0_), channel_id=1, source_target_pairs={{0,28},{1,29},{2,30},{3,31},{4,0},{5,1},{6,2},{7,3},{8,4},{9,5},{1... | collective-permute-start | bytes 798728 | tf_op jit(solution)/shard_map/ppermute | solution.py:52
  16.5 7.6 %collective-permute-start.7 = (bf16[1040,128]{1,0:T(8,128)(2,1)S(1)}, bf16[1040,128]{1,0:T(8,128)(2,1)S(1)}, u32[]{:S(2)}, u32[]{:S(2)}) collective-permute-start(bf16[1040,128]{1,0:T(8,128)(2,1)S(1)} %shard_map.41.refs_0_), channel_id=1, source_target_pairs={{0,4},{1,5},{2,6},{3,7},{4,8},{5,9},{6,10},{7,11},{8,12},{9,13},{1... | collective-permute-start | bytes 798728 | tf_op jit(solution)/shard_map/ppermute | solution.py:52
  16.7 16.7 %collective-permute-start.4 = (bf16[512,512]{1,0:T(8,128)(2,1)S(1)}, bf16[512,512]{1,0:T(8,128)(2,1)S(1)}, u32[]{:S(2)}, u32[]{:S(2)}) collective-permute-start(bf16[512,512]{1,0:T(8,128)(2,1)S(1)} %shard_map.39.own_ref), channel_id=1, source_target_pairs={{0,64},{64,128},{128,192},{192,0},{32,224},{96,32},{160,96},{224,1... | collective-permute-start | bytes 1572872 | tf_op jit(solution)/shard_map/ppermute | solution.py:60
  24.2 9.0 %collective-permute-start.9 = (bf16[1040,128]{1,0:T(8,128)(2,1)S(1)}, bf16[1040,128]{1,0:T(8,128)(2,1)S(1)}, u32[]{:S(2)}, u32[]{:S(2)}) collective-permute-start(bf16[1040,128]{1,0:T(8,128)(2,1)S(1)} %collective-permute-done.7.refs_1_), channel_id=1, source_target_pairs={{0,4},{1,5},{2,6},{3,7},{4,8},{5,9},{6,10},{7,11},{8,12},{9,13},{1... | collective-permute-start | bytes 798728 | tf_op jit(solution)/shard_map/ppermute | solution.py:52
  24.2 9.0 %collective-permute-start.10 = (bf16[1040,128]{1,0:T(8,128)(2,1)S(1)}, bf16[1040,128]{1,0:T(8,128)(2,1)S(1)}, u32[]{:S(2)}, u32[]{:S(2)}) collective-permute-start(bf16[1040,128]{1,0:T(8,128)(2,1)S(1)} %collective-permute-done.8.refs_2_), channel_id=1, source_target_pairs={{0,28},{1,29},{2,30},{3,31},{4,0},{5,1},{6,2},{7,3},{8,4},{9,5},{1... | collective-permute-start | bytes 798728 | tf_op jit(solution)/shard_map/ppermute | solution.py:52
  27.4 10.1 %collective-permute-start.6 = (bf16[512,512]{1,0:T(8,128)(2,1)S(1)}, bf16[512,512]{1,0:T(8,128)(2,1)S(1)}, u32[]{:S(2)}, u32[]{:S(2)}) collective-permute-start(bf16[512,512]{1,0:T(8,128)(2,1)S(1)} %shard_map.39.own_ref), channel_id=1, source_target_pairs={{0,192},{64,0},{128,64},{192,128},{32,96},{96,160},{160,224},{224,... | collective-permute-start | bytes 1572872 | tf_op jit(solution)/shard_map/ppermute | solution.py:60
  33.2 17.1 %collective-permute-start.11 = (bf16[5,1040,128]{2,1,0:T(8,128)(2,1)S(1)}, bf16[5,1040,128]{2,1,0:T(8,128)(2,1)S(1)}, u32[]{:S(2)}, u32[]{:S(2)}) collective-permute-start(bf16[5,1040,128]{2,1,0:T(8,128)(2,1)S(1)} %shard_map.42.refs_1_), channel_id=1, source_target_pairs={{0,32},{32,0},{1,33},{33,1},{2,34},{34,2},{3,35},{35,3},{4,36},{36... | collective-permute-start | bytes 3993608 | tf_op jit(solution)/shard_map/ppermute | solution.py:64
  33.3 16.4 %collective-permute-start.5 = (bf16[512,512]{1,0:T(8,128)(2,1)S(1)}, bf16[512,512]{1,0:T(8,128)(2,1)S(1)}, u32[]{:S(2)}, u32[]{:S(2)}) collective-permute-start(bf16[512,512]{1,0:T(8,128)(2,1)S(1)} %collective-permute-done.4.back_ref), channel_id=1, source_target_pairs={{0,64},{64,128},{128,192},{192,0},{32,224},{96,32},{160,96},{224,1... | collective-permute-start | bytes 1572872 | tf_op jit(solution)/shard_map/ppermute | solution.py:60
  34.9 14.9 %collective-permute-start.14 = (bf16[1040,128]{1,0:T(8,128)(2,1)S(1)}, bf16[1040,128]{1,0:T(8,128)(2,1)S(1)}, u32[]{:S(2)}, u32[]{:S(2)}) collective-permute-start(bf16[1040,128]{1,0:T(8,128)(2,1)S(1)} %collective-permute-done.9.refs_3_), channel_id=1, source_target_pairs={{0,8},{1,9},{2,10},{3,11},{4,12},{5,13},{6,14},{7,15},{8,16},{9,17... | collective-permute-start | bytes 798728 | tf_op jit(solution)/shard_map/ppermute | solution.py:52
  34.9 14.8 %collective-permute-start.12 = (bf16[1040,128]{1,0:T(8,128)(2,1)S(1)}, bf16[1040,128]{1,0:T(8,128)(2,1)S(1)}, u32[]{:S(2)}, u32[]{:S(2)}) collective-permute-start(bf16[1040,128]{1,0:T(8,128)(2,1)S(1)} %collective-permute-done.9.refs_3_), channel_id=1, source_target_pairs={{0,4},{1,5},{2,6},{3,7},{4,8},{5,9},{6,10},{7,11},{8,12},{9,13},{1... | collective-permute-start | bytes 798728 | tf_op jit(solution)/shard_map/ppermute | solution.py:52
  37.5 12.3 %collective-permute-start.13 = (bf16[1040,128]{1,0:T(8,128)(2,1)S(1)}, bf16[1040,128]{1,0:T(8,128)(2,1)S(1)}, u32[]{:S(2)}, u32[]{:S(2)}) collective-permute-start(bf16[1040,128]{1,0:T(8,128)(2,1)S(1)} %collective-permute-done.10.refs_4_), channel_id=1, source_target_pairs={{0,28},{1,29},{2,30},{3,31},{4,0},{5,1},{6,2},{7,3},{8,4},{9,5},{1... | collective-permute-start | bytes 798728 | tf_op jit(solution)/shard_map/ppermute | solution.py:52
  49.8 2.6 %collective-permute-start.15 = (bf16[3,1040,128]{2,1,0:T(8,128)(2,1)S(1)}, bf16[3,1040,128]{2,1,0:T(8,128)(2,1)S(1)}, u32[]{:S(2)}, u32[]{:S(2)}) collective-permute-start(bf16[3,1040,128]{2,1,0:T(8,128)(2,1)S(1)} %shard_map.43.refs_3_), channel_id=1, source_target_pairs={{0,32},{32,0},{1,33},{33,1},{2,34},{34,2},{3,35},{35,3},{4,36},{36... | collective-permute-start | bytes 2396168 | tf_op jit(solution)/shard_map/ppermute | solution.py:64
  58.8 16.5 %collective-permute-start.16 = (s16[2064,128]{1,0:T(8,128)(2,1)S(1)}, s16[2064,128]{1,0:T(8,128)(2,1)S(1)}, u32[]{:S(2)}, u32[]{:S(2)}) collective-permute-start(s16[2064,128]{1,0:T(8,128)(2,1)S(1)} %shard_map.45), channel_id=1, source_target_pairs={{0,2},{1,3},{2,0},{3,1},{4,6},{5,7},{6,4},{7,5},{8,10},{9,11},{10,... | collective-permute-start | bytes 1585160 | tf_op jit(solution)/shard_map/ppermute | solution.py:52
  59.2 24.9 %collective-permute-start.17 = (s16[2064,128]{1,0:T(8,128)(2,1)S(1)}, s16[2064,128]{1,0:T(8,128)(2,1)S(1)}, u32[]{:S(2)}, u32[]{:S(2)}) collective-permute-start(s16[2064,128]{1,0:T(8,128)(2,1)S(1)} %shard_map.46), channel_id=1, source_target_pairs={{0,3},{1,0},{2,1},{3,2},{4,7},{5,4},{6,5},{7,6},{8,11},{9,8},{10,9... | collective-permute-start | bytes 1585160 | tf_op jit(solution)/shard_map/ppermute | solution.py:52
  63.1 22.7 %collective-permute-start.18 = (s16[2064,128]{1,0:T(8,128)(2,1)S(1)}, s16[2064,128]{1,0:T(8,128)(2,1)S(1)}, u32[]{:S(2)}, u32[]{:S(2)}) collective-permute-start(s16[2064,128]{1,0:T(8,128)(2,1)S(1)} %shard_map.47), channel_id=1, source_target_pairs={{0,1},{1,2},{2,3},{3,0},{4,5},{5,6},{6,7},{7,4},{8,9},{9,10},{10,1... | collective-permute-start | bytes 1585160 | tf_op jit(solution)/shard_map/ppermute | solution.py:52
  86.6 8.8 %collective-permute-start.19 = (f32[1024,128]{1,0:T(8,128)S(1)}, f32[1024,128]{1,0:T(8,128)S(1)}, u32[]{:S(2)}, u32[]{:S(2)}) collective-permute-start(f32[1024,128]{1,0:T(8,128)S(1)} %get-tuple-element.31), channel_id=1, source_target_pairs={{0,32},{32,0},{1,33},{33,1},{2,34},{34,2},{3,35},{35,3},{4,36},{36... | collective-permute-start | bytes 1572872 | tf_op jit(solution)/shard_map/ppermute | solution.py:64
  86.7 1.9 %collective-permute-start.20 = (f32[1,128]{1,0:T(1,128)S(1)}, f32[1,128]{1,0:T(1,128)S(1)}, u32[]{:S(2)}, u32[]{:S(2)}) collective-permute-start(f32[1,128]{1,0:T(1,128)S(1)} %get-tuple-element.32), channel_id=1, source_target_pairs={{0,32},{32,0},{1,33},{33,1},{2,34},{34,2},{3,35},{35,3},{4,36},{36... | collective-permute-start | bytes 1544 | tf_op jit(solution)/shard_map/ppermute | solution.py:64
  88.6 5.1 %collective-permute-start.23 = (f32[2,128]{1,0:T(2,128)S(1)}, f32[2,128]{1,0:T(2,128)S(1)}, u32[]{:S(2)}, u32[]{:S(2)}) collective-permute-start(f32[2,128]{1,0:T(2,128)S(1)} %pad_maximum_fusion.refs_0_), channel_id=1, source_target_pairs={{0,128},{64,192},{128,0},{192,64},{32,160},{96,224},{160,32},{224,... | collective-permute-start | bytes 3080 | tf_op jit(solution)/shard_map/ppermute | solution.py:60
  89.6 4.0 %collective-permute-start.22 = (f32[2,128]{1,0:T(2,128)S(1)}, f32[2,128]{1,0:T(2,128)S(1)}, u32[]{:S(2)}, u32[]{:S(2)}) collective-permute-start(f32[2,128]{1,0:T(2,128)S(1)} %pad_maximum_fusion.refs_0_), channel_id=1, source_target_pairs={{0,192},{64,0},{128,64},{192,128},{32,96},{96,160},{160,224},{224,... | collective-permute-start | bytes 3080 | tf_op jit(solution)/shard_map/ppermute | solution.py:60
  91.8 3.6 %collective-permute-start.21 = (f32[2,128]{1,0:T(2,128)S(1)}, f32[2,128]{1,0:T(2,128)S(1)}, u32[]{:S(2)}, u32[]{:S(2)}) collective-permute-start(f32[2,128]{1,0:T(2,128)S(1)} %pad_maximum_fusion.refs_0_), channel_id=1, source_target_pairs={{0,64},{64,128},{128,192},{192,0},{32,224},{96,32},{160,96},{224,1... | collective-permute-start | bytes 3080 | tf_op jit(solution)/shard_map/ppermute | solution.py:60

commit v3 on v2

--- a/solution.py
+++ b/solution.py
@@ -114,10 +114,17 @@
         refs[-1][:, i * TILE : (i + 1) * TILE] = ref[...]
 
 
-def stack_kernel(own_ref, far_ref, back_ref, ahead_ref, out_ref):
-    x, s = lax.axis_index("row"), 1 - 2 * lax.axis_index("col")
-    for d, ref in ((0, own_ref), (-1, back_ref), (1, ahead_ref), (2, far_ref)):
-        out_ref[(x + s * d + NX) % NX] = ref[...]
+def stack_kernel(places, *refs):
+    out_ref = refs[-1]
+    for place, ref in zip(places, refs):
+        out_ref[place] = ref[...]
+
+
+def stack(panels, places, whole=None):
+    out = struct((NX, *panels[0].shape), panels[0].dtype)
+    operands = panels + ([] if whole is None else [whole])
+    alias = {} if whole is None else {len(panels): 0}
+    return call(functools.partial(stack_kernel, places), out, *operands, input_output_aliases=alias)
 
 
 def join_kernel(*refs):
@@ -129,40 +136,51 @@
     return call(join_kernel, struct((len(parts), *parts[0].shape), parts[0].dtype), *parts)
 
 
-def product_kernel(plan, *refs):
+def product_kernel(plan, slots, outs, *refs):
     n = len(plan)
-    b_ref, parts = refs[0], refs[1 : n + 1]
-    total_ref, heads_ref, table_ref, work_ref, sem = refs[n + 1 :]
+    b_ref, parts, given = refs[0], refs[1 : n + 1], refs[n + 1 : -5 - len(outs)]
+    out_refs = refs[-5 - len(outs) : -5]
+    total_ref, heads_ref, table_ref, work_ref, sem = refs[-5:]
     at = 0
-    for part, (_, steps) in zip(parts, plan):
+    for part, (_, _, steps) in zip(parts, plan):
         for j in range(len(steps)):
             head = part[j, CAP * TILE :, :].astype(jnp.float32)
             heads_ref[at : at + 1, :] = head[0:1, :].astype(jnp.int32)
             at += 1
     copy = pltpu.make_async_copy(heads_ref, table_ref, sem)
     copy.start()
-    total_ref[...] = jnp.zeros_like(total_ref)
+    lanes = slice(slots[0] * TILE, (slots[-1] + 1) * TILE)
+    if given:
+        total_ref[...] = given[0][:, lanes]
+    else:
+        total_ref[...] = jnp.zeros_like(total_ref)
     z, _, _, s = place()
+    x = lax.axis_index("row")
     copy.wait()
 
     at = 0
-    for part, (other, steps) in zip(parts, plan):
+    for part, (other, panels, steps) in zip(parts, plan):
         count = jnp.int32(0)
         for j, dz in enumerate(steps):
             source = (z + (-s if other else s) * dz + NZ) % NZ
-
-            def list_tile(i, count, j=j, at=at, source=source, other=other):
+            panel = ((source // 2 - x) * s + NX) % NX
+            tiles = table_ref[at, CAP]
+            if len(panels) < NX:
+                held = functools.reduce(jnp.logical_or, [panel == k for k in panels])
+                tiles = jnp.where(held, tiles, 0)
+
+            def list_tile(i, count, j=j, at=at, source=source, other=other, panel=panel):
                 work_ref[0, count] = j
                 work_ref[1, count] = i
                 work_ref[2, count] = table_ref[at, i]
-                work_ref[3, count] = source // 2
+                work_ref[3, count] = panel
                 work_ref[4, count] = other * 2 + source % 2
                 return count + 1
 
-            count = lax.fori_loop(0, table_ref[at, CAP], list_tile, count)
+            count = lax.fori_loop(0, tiles, list_tile, count)
             at += 1
         for u in range(BATCH - 1):
-            for k, v in enumerate((0, 0, ROWS // TILE, 0, 0)):
+            for k, v in enumerate((0, 0, ROWS // TILE, panels[0], 0)):
                 work_ref[k, count + u] = v
 
         def step(g, carry, part=part):
@@ -171,25 +189,41 @@
                 rows = pl.ds(pl.multiple_of(t * TILE, TILE), TILE)
                 total_ref[rows, :] += jnp.dot(
                     part[j, pl.ds(pl.multiple_of(i * TILE, TILE), TILE), :],
-                    b_ref[panel, pl.ds(pl.multiple_of(at_b * TILE, TILE), TILE), :],
+                    b_ref[panel, pl.ds(pl.multiple_of(at_b * TILE, TILE), TILE), lanes],
                     preferred_element_type=jnp.float32,
                 )
             return carry
 
         lax.fori_loop(0, (count + BATCH - 1) // BATCH, step, 0)
-
-
-def product(b_panel, parts, plan):
-    cols = b_panel.shape[2]
-    count = sum(len(steps) for _, steps in plan)
+    for i, (coded, out_ref) in enumerate(zip(outs, out_refs)):
+        part = slice(i * TILE, (i + 1) * TILE)
+        if coded:
+            encode(total_ref, part, out_ref)
+        elif len(outs) == 1:
+            out_ref[...] = total_ref[...]
+        else:
+            out_ref[...] = total_ref[:, part]
+
+
+def product(b_panels, parts, plan, total=None, slots=(0, 1, 2, 3), outs=(False,)):
+    cols = len(slots) * TILE
+    count = sum(len(steps) for _, _, steps in plan)
     flops = sum(p.size for p in parts) * cols * 2
+    width = cols // len(outs)
     return call(
-        functools.partial(product_kernel, tuple(plan)),
-        struct((ROWS + TILE, cols), jnp.float32),
-        b_panel,
+        functools.partial(product_kernel, tuple(plan), slots, outs),
+        [
+            struct((ROWS + HEAD, TILE), jnp.int16)
+            if coded
+            else struct((ROWS + TILE, width), jnp.float32)
+            for coded in outs
+        ],
+        b_panels,
         *parts,
-        mib=20,
+        *([] if total is None else [total]),
+        mib=24,
         scratch_shapes=[
+            pltpu.VMEM((ROWS + TILE, cols), jnp.float32),
             pltpu.VMEM((count, TILE), jnp.int32),
             pltpu.SMEM((count, TILE), jnp.int32),
             pltpu.SMEM((8, TILE), jnp.int32),
@@ -199,8 +233,7 @@
     )
 
 
-def encode_kernel(slot, total_ref, out_ref):
-    lanes = slice(slot * TILE, (slot + 1) * TILE)
+def encode(total_ref, lanes, out_ref):
     top = total_ref[:TILE, lanes]
     for i in range(1, ROWS // TILE):
         top = jnp.maximum(top, total_ref[i * TILE : (i + 1) * TILE, lanes])
@@ -215,20 +248,28 @@
     out_ref[ROWS:, :] = exponent.astype(jnp.int16)
 
 
-def encode(total, slot):
-    return call(
-        functools.partial(encode_kernel, slot), struct((ROWS + HEAD, TILE), jnp.int16), total
-    )
+def scale_of(ref):
+    exponent = ref[ROWS:, :].astype(jnp.int32).astype(jnp.float32)[0:1, :]
+    return jnp.exp2(exponent * (1.0 / FINE)) * jnp.float32(1.0 / LEVELS)
+
+
+def decode(ref, part, scale):
+    return (ref[part, :].astype(jnp.int32) + 32768).astype(jnp.float32) * scale
+
+
+def relay_kernel(total_ref, recv_ref, out_ref, sum_ref):
+    scale = scale_of(recv_ref)
+    for i in range(ROWS // TILE):
+        part = slice(i * TILE, (i + 1) * TILE)
+        sum_ref[part, :] = total_ref[part, :] + decode(recv_ref, part, scale)
+    encode(sum_ref, slice(0, TILE), out_ref)
 
 
 def square_kernel(weight, total_ref, *refs):
-    recv, (keep_ref, send_ref, sum_ref) = refs[:3], refs[3:]
+    recv, (keep_ref, send_ref, sum_ref) = refs[:2], refs[2:]
     core = lax.axis_index("col")
     first_col = lax.axis_index("layer") * 2 * TILE + core * TILE
-    scales = []
-    for ref in recv:
-        exponent = ref[ROWS:, :].astype(jnp.int32).astype(jnp.float32)[0:1, :]
-        scales.append(jnp.exp2(exponent * (1.0 / FINE)) * jnp.float32(1.0 / LEVELS))
+    scales = [scale_of(ref) for ref in recv]
     row = lax.broadcasted_iota(jnp.int32, (TILE, TILE), 0)
     col = lax.broadcasted_iota(jnp.int32, (TILE, TILE), 1)
     column = jnp.zeros((TILE, TILE), jnp.float32)
@@ -239,12 +280,11 @@
             part = pl.ds(pl.multiple_of(start, TILE), TILE)
             first_row = lax.axis_index("row") * ROWS + start
             diagonal = row + (first_row - first_col) == col
-            expanded = total_ref[part, :TILE] + jnp.where(
+            expanded = total_ref[part, :] + jnp.where(
                 diagonal, jnp.float32(weight), jnp.float32(0)
             )
             for ref, scale in zip(recv, scales):
-                steps = ref[part, :].astype(jnp.int32) + 32768
-                expanded += steps.astype(jnp.float32) * scale
+                expanded += decode(ref, part, scale)
             power = expanded * expanded
             out_ref[i * TILE : (i + 1) * TILE, :] = power
             column += power
@@ -276,35 +316,52 @@
         first=SMEM,
     )
     a1, b1 = hop(p, 1, 0), hop(p, -1, 0)
-    blocks = call(block_kernel, [struct((512, TILE), b_matrix.dtype)] * 4, keep, recv)
+    blocks = call(block_kernel, [struct((512, TILE), b_matrix.dtype)] * 4, after(keep, p), recv)
     blocks = [blocks[0]] + [hop(m, 0, d) for m, d in zip(blocks[1:], (1, -1, 2))]
     wide = call(widen_kernel, struct((512, 4 * TILE), b_matrix.dtype), *blocks)
 
     a1, b1 = after(a1, wide), after(b1, wide)
-    a2, b2 = hop(a1, 1, 0), hop(b1, -1, 0)
+    a2, b2, a4 = hop(a1, 1, 0), hop(b1, -1, 0), hop(a1, 3, 0)
     back, ahead = hop_x(wide, 1), hop_x(wide, -1)
-    near = join([p, a1, b1, a2, b2])
-    a2, b2 = after(a2, back), after(b2, back)
-    a4, a3, b3 = hop(a2, 2, 0), hop(a2, 1, 0), hop(b2, -1, 0)
+    near = join([after(p, back, ahead, a4), a1, b1, a2, b2])
+    near_other = swap(near)
+    a2, b2 = after(a2, back, ahead, a4), after(b2, back, ahead, a4)
+    a3, b3 = hop(a2, 1, 0), hop(b2, -1, 0)
     across = hop_x(back, 1)
-    near_other = swap(near)
-    far = join([after(a3, across, ahead), b3, a4])
+
+    panels = stack([wide, ahead, back], (0, 1, 3))
+    near_steps, far_steps = (0, -1, 1, -2, 2), (-3, 3, -4)
+    held = (0, 1, 3)
+    (total,) = product(panels, [near, near_other], [(0, held, near_steps), (1, held, near_steps)])
+    far = join([after(a3, across, total), b3, a4])
     far_other = swap(far)
-    panel = call(
-        stack_kernel, struct((NX, 512, 4 * TILE), b_matrix.dtype), wide, across, back, ahead
-    )
-    near_steps, far_steps = (0, -1, 1, -2, 2), (-3, 3, -4)
-    total = product(
-        panel,
+    panels = stack([across], (2,), panels)
+    every = (0, 1, 2, 3)
+    rest = functools.partial(
+        product,
+        panels,
         [near, near_other, far, far_other],
-        [(0, near_steps), (1, near_steps), (0, far_steps), (1, far_steps)],
-    )
-
-    sums = [hop(encode(total, slot), 0, d) for slot, d in ((3, 2), (1, -1), (2, 1))]
+        [(0, (2,), near_steps), (1, (2,), near_steps), (0, every, far_steps), (1, every, far_steps)],
+        total,
+    )
+
+    (code,) = rest(slots=(3,), outs=(True,))
+    passed = hop(code, 0, 1)
+    code, side = rest(slots=(1, 2), outs=(True, False))
+    sums = [hop(code, 0, -1)]
+    code = call(
+        relay_kernel,
+        struct((ROWS + HEAD, TILE), jnp.int16),
+        side,
+        passed,
+        scratch_shapes=[pltpu.VMEM((ROWS, TILE), jnp.float32)],
+    )
+    sums.append(hop(code, 0, 1))
+    (own,) = rest(slots=(0,))
     keep, send, column = call(
         functools.partial(square_kernel, n_total / 32),
         [struct((half, TILE), jnp.float32)] * 2 + [struct((1, TILE), jnp.float32)],
-        total,
+        own,
         *sums,
     )
     column = jnp.concatenate([column, swap(column)])

time: 97.9 us -> 91.8 us (0.938)
  waiting for transfers between devices: 54.1 us -> 38.1 us
  Pallas kernels: 9.6 us -> 15.1 us
  starting transfers between devices: 29.9 us -> 34.6 us
    ppermute x13, waiting for transfers between devices: 45.5 us -> 32.5 us  [hop(): return lax.ppermute(x, ('col', 'layer'), pairs)]
    pallas_call x13 -> x15, Pallas kernels: 9.6 us -> 15.1 us  [call(): pl.pallas_call(kernel, out_shape=out_shape, in_specs=[first] + [VMEM] * (...]
    ppermute x13, starting transfers between devices: 22 us -> 24.3 us  [hop(): return lax.ppermute(x, ('col', 'layer'), pairs)]
    ppermute x6, starting transfers between devices: 6.87 us -> 8.67 us  [hop_x(): return lax.ppermute(x, ('row', 'col'), pairs)]
    ppermute x5, waiting for transfers between devices: 5.04 us -> 3.3 us  [swap(): return lax.ppermute(x, 'col', [(0, 1), (1, 0)])]
    ppermute x6, waiting for transfers between devices: 3.57 us -> 2.35 us  [hop_x(): return lax.ppermute(x, ('row', 'col'), pairs)]
  transfers between devices with their start and end apart: 24 -> 24, of which waited for: 12 -> 12; matrix products, arithmetic and copies ran while one was open for 0% -> 0% of each run, Pallas kernels for 1% -> 11%
where the time goes in v3:
time: 91.8 us; the launch traced here: 90.7 us
  waiting for transfers between devices  38.1 us (42%)
  starting transfers between devices  34.6 us (38%)
  Pallas kernels  15.1 us (16%)
  local copies, waits for them, and re-layouts  2.73 us (3%)
    ppermute x13, waiting for transfers between devices, hop(): return lax.ppermute(x, ('col', 'layer'), pairs)  32.5 us
    ppermute x13, starting transfers between devices, hop(): return lax.ppermute(x, ('col', 'layer'), pairs)  24.3 us
    pallas_call x15, Pallas kernels, call(): pl.pallas_call(kernel, out_shape=out_shape, in_specs=[first] + [VMEM] * (...  15.1 us
    ppermute x6, starting transfers between devices, hop_x(): return lax.ppermute(x, ('row', 'col'), pairs)  8.67 us
    ppermute x5, waiting for transfers between devices, swap(): return lax.ppermute(x, 'col', [(0, 1), (1, 0)])  3.3 us
    unnamed x6, local copies, waits for them, and re-layouts  2.73 us
    ppermute x6, waiting for transfers between devices, hop_x(): return lax.ppermute(x, ('row', 'col'), pairs)  2.35 us
  transfers between devices with their start and end apart: 24, of which 12 were waited for; matrix products, arithmetic and copies ran while one was open for 0% of the time, Pallas kernels for 11%

profile of v3, /device:TPU:2, one launch (start us, length us, event | category | flops | bytes accessed | tf_op | source)
XLA Modules:
  0.0 90.7 jit_solution(13807679552924328839)
XLA Ops:
  0.0 1.0 %copy-done = bf16[1024,256]{1,0:T(8,128)(2,1)S(1)} copy-done((bf16[1024,256]{1,0:T(8,128)(2,1)S(1)}, bf16[1024,256]{1,0:T(8,128)(2,1)}, u32[]{:S(2)}) %copy-start) | copy-done | bytes 524312
  1.3 1.0 %copy-done.1 = bf16[2048,128]{1,0:T(8,128)(2,1)S(1)} copy-done((bf16[2048,128]{1,0:T(8,128)(2,1)S(1)}, bf16[2048,128]{1,0:T(8,128)(2,1)}, u32[]{:S(2)}) %copy-start.1) | copy-done | bytes 524312
  3.8 1.7 %collective-permute-start.1 = (bf16[512,128]{1,0:T(8,128)(2,1)S(1)}, bf16[512,128]{1,0:T(8,128)(2,1)S(1)}, u32[]{:S(2)}, u32[]{:S(2)}) collective-permute-start(bf16[512,128]{1,0:T(8,128)(2,1)S(1)} %get-tuple-element.27), channel_id=1, source_target_pairs={{0,1},{1,2},{2,3},{3,0},{4,5},{5,6},{6,7},{7,4},{8,9},{9,10},{10,1... | collective-permute-start | bytes 393224 | tf_op jit(solution)/shard_map/ppermute | solution.py:52
  5.5 1.7 %collective-permute-start.2 = (bf16[512,128]{1,0:T(8,128)(2,1)S(1)}, bf16[512,128]{1,0:T(8,128)(2,1)S(1)}, u32[]{:S(2)}, u32[]{:S(2)}) collective-permute-start(bf16[512,128]{1,0:T(8,128)(2,1)S(1)} %get-tuple-element.28), channel_id=1, source_target_pairs={{0,3},{1,0},{2,1},{3,2},{4,7},{5,4},{6,5},{7,6},{8,11},{9,8},{10,9... | collective-permute-start | bytes 393224 | tf_op jit(solution)/shard_map/ppermute | solution.py:52
  7.1 2.0 %collective-permute-start.3 = (bf16[512,128]{1,0:T(8,128)(2,1)S(1)}, bf16[512,128]{1,0:T(8,128)(2,1)S(1)}, u32[]{:S(2)}, u32[]{:S(2)}) collective-permute-start(bf16[512,128]{1,0:T(8,128)(2,1)S(1)} %get-tuple-element.29), channel_id=1, source_target_pairs={{0,2},{1,3},{2,0},{3,1},{4,6},{5,7},{6,4},{7,5},{8,10},{9,11},{10,... | collective-permute-start | bytes 393224 | tf_op jit(solution)/shard_map/ppermute | solution.py:52
  9.1 1.9 %collective-permute-start.7 = (bf16[1040,128]{1,0:T(8,128)(2,1)S(1)}, bf16[1040,128]{1,0:T(8,128)(2,1)S(1)}, u32[]{:S(2)}, u32[]{:S(2)}) collective-permute-start(bf16[1040,128]{1,0:T(8,128)(2,1)S(1)} %shard_map.38.refs_0_), channel_id=1, source_target_pairs={{0,4},{1,5},{2,6},{3,7},{4,8},{5,9},{6,10},{7,11},{8,12},{9,13},{1... | collective-permute-start | bytes 798728 | tf_op jit(solution)/shard_map/ppermute | solution.py:52
  11.0 3.9 %collective-permute-start.9 = (bf16[1040,128]{1,0:T(8,128)(2,1)S(1)}, bf16[1040,128]{1,0:T(8,128)(2,1)S(1)}, u32[]{:S(2)}, u32[]{:S(2)}) collective-permute-start(bf16[1040,128]{1,0:T(8,128)(2,1)S(1)} %shard_map.38.refs_0_), channel_id=1, source_target_pairs={{0,28},{1,29},{2,30},{3,31},{4,0},{5,1},{6,2},{7,3},{8,4},{9,5},{1... | collective-permute-start | bytes 798728 | tf_op jit(solution)/shard_map/ppermute | solution.py:52
  15.6 1.6 %collective-permute-start.4 = (bf16[512,512]{1,0:T(8,128)(2,1)S(1)}, bf16[512,512]{1,0:T(8,128)(2,1)S(1)}, u32[]{:S(2)}, u32[]{:S(2)}) collective-permute-start(bf16[512,512]{1,0:T(8,128)(2,1)S(1)} %shard_map.40.refs_0_), channel_id=1, source_target_pairs={{0,64},{64,128},{128,192},{192,0},{32,224},{96,32},{160,96},{224,1... | collective-permute-start | bytes 1572872 | tf_op jit(solution)/shard_map/ppermute | solution.py:60
  17.7 2.8 %collective-permute-done.7.refs_1_ = bf16[1040,128]{1,0:T(8,128)(2,1)S(1)} collective-permute-done((bf16[1040,128]{1,0:T(8,128)(2,1)S(1)}, bf16[1040,128]{1,0:T(8,128)(2,1)S(1)}, u32[]{:S(2)}, u32[]{:S(2)}) %collective-permute-start.7) | collective-permute-done | bytes 266272 | tf_op jit(solution)/shard_map/ppermute | solution.py:52
  20.5 1.8 %collective-permute-start.8 = (bf16[1040,128]{1,0:T(8,128)(2,1)S(1)}, bf16[1040,128]{1,0:T(8,128)(2,1)S(1)}, u32[]{:S(2)}, u32[]{:S(2)}) collective-permute-start(bf16[1040,128]{1,0:T(8,128)(2,1)S(1)} %collective-permute-done.7.refs_1_), channel_id=1, source_target_pairs={{0,12},{1,13},{2,14},{3,15},{4,16},{5,17},{6,18},{7,19},{8,20},{9,... | collective-permute-start | bytes 798728 | tf_op jit(solution)/shard_map/ppermute | solution.py:52
  22.3 3.7 %collective-permute-start.10 = (bf16[1040,128]{1,0:T(8,128)(2,1)S(1)}, bf16[1040,128]{1,0:T(8,128)(2,1)S(1)}, u32[]{:S(2)}, u32[]{:S(2)}) collective-permute-start(bf16[1040,128]{1,0:T(8,128)(2,1)S(1)} %collective-permute-done.7.refs_1_), channel_id=1, source_target_pairs={{0,4},{1,5},{2,6},{3,7},{4,8},{5,9},{6,10},{7,11},{8,12},{9,13},{1... | collective-permute-start | bytes 798728 | tf_op jit(solution)/shard_map/ppermute | solution.py:52
  26.0 10.6 %collective-permute-done.8.refs_2_ = bf16[1040,128]{1,0:T(8,128)(2,1)S(1)} collective-permute-done((bf16[1040,128]{1,0:T(8,128)(2,1)S(1)}, bf16[1040,128]{1,0:T(8,128)(2,1)S(1)}, u32[]{:S(2)}, u32[]{:S(2)}) %collective-permute-start.8) | collective-permute-done | bytes 266272 | tf_op jit(solution)/shard_map/ppermute | solution.py:52
  36.6 2.9 %collective-permute-done.10.refs_3_ = bf16[1040,128]{1,0:T(8,128)(2,1)S(1)} collective-permute-done((bf16[1040,128]{1,0:T(8,128)(2,1)S(1)}, bf16[1040,128]{1,0:T(8,128)(2,1)S(1)}, u32[]{:S(2)}, u32[]{:S(2)}) %collective-permute-start.10) | collective-permute-done | bytes 266272 | tf_op jit(solution)/shard_map/ppermute | solution.py:52
  39.7 1.6 %collective-permute-start.5 = (bf16[512,512]{1,0:T(8,128)(2,1)S(1)}, bf16[512,512]{1,0:T(8,128)(2,1)S(1)}, u32[]{:S(2)}, u32[]{:S(2)}) collective-permute-start(bf16[512,512]{1,0:T(8,128)(2,1)S(1)} %collective-permute-done.4.refs_2_), channel_id=1, source_target_pairs={{0,64},{64,128},{128,192},{192,0},{32,224},{96,32},{160,96},{224,1... | collective-permute-start | bytes 1572872 | tf_op jit(solution)/shard_map/ppermute | solution.py:60
  41.9 2.5 %collective-permute-start.14 = (bf16[1040,128]{1,0:T(8,128)(2,1)S(1)}, bf16[1040,128]{1,0:T(8,128)(2,1)S(1)}, u32[]{:S(2)}, u32[]{:S(2)}) collective-permute-start(bf16[1040,128]{1,0:T(8,128)(2,1)S(1)} %collective-permute-done.11.refs_4_), channel_id=1, source_target_pairs={{0,28},{1,29},{2,30},{3,31},{4,0},{5,1},{6,2},{7,3},{8,4},{9,5},{1... | collective-permute-start | bytes 798728 | tf_op jit(solution)/shard_map/ppermute | solution.py:52
  44.6 2.3 %shard_map.44.refs_5_ = f32[2176,512]{1,0:T(8,128)S(1)} custom-call(bf16[4,512,512]{2,1,0:T(8,128)(2,1)S(1)} %shard_map.41.refs_1_.refs_0_, bf16[5,1040,128]{2,1,0:T(8,128)(2,1)S(1)} %shard_map.43.refs_1_, bf16[5,1040,128]{2,1,0:T(8,128)(2,1)S(1)} %collective-permute-done.12.refs_2_), custom_call_target="tpu_custom_call" | custom-call | flops 1363148800 | bytes 10649600 | tf_op jit(solution)/shard_map/pallas_call | solution.py:30
  46.9 3.8 %collective-permute-done.13.refs_0_ = bf16[1040,128]{1,0:T(8,128)(2,1)S(1)} collective-permute-done((bf16[1040,128]{1,0:T(8,128)(2,1)S(1)}, bf16[1040,128]{1,0:T(8,128)(2,1)S(1)}, u32[]{:S(2)}, u32[]{:S(2)}) %collective-permute-start.13) | collective-permute-done | bytes 266272 | tf_op jit(solution)/shard_map/ppermute | solution.py:52
  50.8 0.8 collective-permute-start.15
  51.7 1.9 %collective-permute-done.15.refs_4_ = bf16[3,1040,128]{2,1,0:T(8,128)(2,1)S(1)} collective-permute-done((bf16[3,1040,128]{2,1,0:T(8,128)(2,1)S(1)}, bf16[3,1040,128]{2,1,0:T(8,128)(2,1)S(1)}, u32[]{:S(2)}, u32[]{:S(2)}) %collective-permute-start.15) | collective-permute-done | bytes 798752 | tf_op jit(solution)/shard_map/ppermute | solution.py:64
  53.6 3.0 %shard_map.48 = s16[2064,128]{1,0:T(8,128)(2,1)S(1)} custom-call(bf16[4,512,512]{2,1,0:T(8,128)(2,1)S(1)} %shard_map.42.refs_0_, bf16[5,1040,128]{2,1,0:T(8,128)(2,1)S(1)} %shard_map.43.refs_1_, bf16[5,1040,128]{2,1,0:T(8,128)(2,1)S(1)} %collective-permute-done.12.refs_2_, bf16[3,1040,128]{2,1,0:T(8,128)(2,1)S(1)} %shard_map.45.refs_3_, ...), custom_call_target="tpu_custom_call" | custom-call | flops 545259520 | bytes 4259840 | tf_op jit(solution)/shard_map/pallas_call | solution.py:30
  56.6 1.1 %collective-permute-start.17 = (s16[2064,128]{1,0:T(8,128)(2,1)S(1)}, s16[2064,128]{1,0:T(8,128)(2,1)S(1)}, u32[]{:S(2)}, u32[]{:S(2)}) collective-permute-start(s16[2064,128]{1,0:T(8,128)(2,1)S(1)} %shard_map.48), channel_id=1, source_target_pairs={{0,1},{1,2},{2,3},{3,0},{4,5},{5,6},{6,7},{7,4},{8,9},{9,10},{10,1... | collective-permute-start | bytes 1585160 | tf_op jit(solution)/shard_map/ppermute | solution.py:52
  57.8 3.4 %shard_map.47 = (s16[2064,128]{1,0:T(8,128)(2,1)S(1)}, f32[2176,128]{1,0:T(8,128)S(1)}) custom-call(bf16[4,512,512]{2,1,0:T(8,128)(2,1)S(1)} %shard_map.42.refs_0_, bf16[5,1040,128]{2,1,0:T(8,128)(2,1)S(1)} %shard_map.43.refs_1_, bf16[5,1040,128]{2,1,0:T(8,128)(2,1)S(1)} %collective-permute-done.12.refs_2_, bf16[3,1040,128]{2,1,0:T(8,128)(2,1)S(1)} %shard_map.45.refs_3_, ...), custom_call_target="tpu_custom_call" | custom-call | flops 1090519040 | bytes 8519680 | tf_op jit(solution)/shard_map/pallas_call | solution.py:30
  61.2 2.5 %collective-permute-start.16 = (s16[2064,128]{1,0:T(8,128)(2,1)S(1)}, s16[2064,128]{1,0:T(8,128)(2,1)S(1)}, u32[]{:S(2)}, u32[]{:S(2)}) collective-permute-start(s16[2064,128]{1,0:T(8,128)(2,1)S(1)} %get-tuple-element.36), channel_id=1, source_target_pairs={{0,3},{1,0},{2,1},{3,2},{4,7},{5,4},{6,5},{7,6},{8,11},{9,8},{10,9... | collective-permute-start | bytes 1585160 | tf_op jit(solution)/shard_map/ppermute | solution.py:52
  63.7 4.9 %collective-permute-done.17.recv_ref = s16[2064,128]{1,0:T(8,128)(2,1)S(1)} collective-permute-done((s16[2064,128]{1,0:T(8,128)(2,1)S(1)}, s16[2064,128]{1,0:T(8,128)(2,1)S(1)}, u32[]{:S(2)}, u32[]{:S(2)}) %collective-permute-start.17) | collective-permute-done | bytes 528416 | tf_op jit(solution)/shard_map/ppermute | solution.py:52
  69.8 2.8 %shard_map.46.total_ref = f32[2176,128]{1,0:T(8,128)S(1)} custom-call(bf16[4,512,512]{2,1,0:T(8,128)(2,1)S(1)} %shard_map.42.refs_0_, bf16[5,1040,128]{2,1,0:T(8,128)(2,1)S(1)} %shard_map.43.refs_1_, bf16[5,1040,128]{2,1,0:T(8,128)(2,1)S(1)} %collective-permute-done.12.refs_2_, bf16[3,1040,128]{2,1,0:T(8,128)(2,1)S(1)} %shard_map.45.refs_3_, ...), custom_call_target="tpu_custom_call" | custom-call | flops 545259520 | bytes 4259840 | tf_op jit(solution)/shard_map/pallas_call | solution.py:30
  72.8 6.9 %collective-permute-done.18.refs_1_ = s16[2064,128]{1,0:T(8,128)(2,1)S(1)} collective-permute-done((s16[2064,128]{1,0:T(8,128)(2,1)S(1)}, s16[2064,128]{1,0:T(8,128)(2,1)S(1)}, u32[]{:S(2)}, u32[]{:S(2)}) %collective-permute-start.18) | collective-permute-done | bytes 528416 | tf_op jit(solution)/shard_map/ppermute | solution.py:52
  80.8 1.4 %collective-permute-done.20 = f32[1,128]{1,0:T(1,128)S(1)} collective-permute-done((f32[1,128]{1,0:T(1,128)S(1)}, f32[1,128]{1,0:T(1,128)S(1)}, u32[]{:S(2)}, u32[]{:S(2)}) %collective-permute-start.20) | collective-permute-done | bytes 544 | tf_op jit(solution)/shard_map/ppermute | solution.py:64
  82.2 2.3 %collective-permute-start.21 = (f32[2,128]{1,0:T(2,128)S(1)}, f32[2,128]{1,0:T(2,128)S(1)}, u32[]{:S(2)}, u32[]{:S(2)}) collective-permute-start(f32[2,128]{1,0:T(2,128)S(1)} %pad_maximum_fusion.refs_0_), channel_id=1, source_target_pairs={{0,64},{64,128},{128,192},{192,0},{32,224},{96,32},{160,96},{224,1... | collective-permute-start | bytes 3080 | tf_op jit(solution)/shard_map/ppermute | solution.py:60
  84.5 2.7 %collective-permute-start.23 = (f32[2,128]{1,0:T(2,128)S(1)}, f32[2,128]{1,0:T(2,128)S(1)}, u32[]{:S(2)}, u32[]{:S(2)}) collective-permute-start(f32[2,128]{1,0:T(2,128)S(1)} %pad_maximum_fusion.refs_0_), channel_id=1, source_target_pairs={{0,128},{64,192},{128,0},{192,64},{32,160},{96,224},{160,32},{224,... | collective-permute-start | bytes 3080 | tf_op jit(solution)/shard_map/ppermute | solution.py:60
  87.2 0.8 collective-permute-done.22.refs_2_
  88.0 1.5 %collective-permute-done.23.refs_3_ = f32[2,128]{1,0:T(2,128)S(1)} collective-permute-done((f32[2,128]{1,0:T(2,128)S(1)}, f32[2,128]{1,0:T(2,128)S(1)}, u32[]{:S(2)}, u32[]{:S(2)}) %collective-permute-start.23) | collective-permute-done | bytes 1056 | tf_op jit(solution)/shard_map/ppermute | solution.py:60
  89.6 1.1 %shard_map.51 = f32[1024,256]{1,0:T(8,128)} custom-call(f32[1024,128]{1,0:T(8,128)S(1)} %get-tuple-element.38.keep_ref, f32[1024,128]{1,0:T(8,128)S(1)} %collective-permute-done.19.recv_ref, f32[2,128]{1,0:T(2,128)S(1)} %pad_maximum_fusion.refs_0_, f32[2,128]{1,0:T(2,128)S(1)} %collective-permute-done.21.refs_1_, ...), custom_call_target="tpu_custom_call" | custom-call | tf_op jit(solution)/shard_map/pallas_call | solution.py:30
  (38 shorter events, 6.5 us)
Async XLA Ops:
  0.0 1.0 %copy-start = (bf16[1024,256]{1,0:T(8,128)(2,1)S(1)}, bf16[1024,256]{1,0:T(8,128)(2,1)}, u32[]{:S(2)}) copy-start(bf16[1024,256]{1,0:T(8,128)(2,1)} %b_ref.1) | copy-start | bytes 1572868
  1.2 2.6 %collective-permute-start = (bf16[1024,128]{1,0:T(8,128)(2,1)S(1)}, bf16[1024,128]{1,0:T(8,128)(2,1)S(1)}, u32[]{:S(2)}, u32[]{:S(2)}) collective-permute-start(bf16[1024,128]{1,0:T(8,128)(2,1)S(1)} %get-tuple-element.25), channel_id=1, source_target_pairs={{0,32},{32,0},{1,33},{33,1},{2,34},{34,2},{3,35},{35,3},{4,36},{36... | collective-permute-start | bytes 786440 | tf_op jit(solution)/shard_map/ppermute | solution.py:64
  1.3 1.0 %copy-start.1 = (bf16[2048,128]{1,0:T(8,128)(2,1)S(1)}, bf16[2048,128]{1,0:T(8,128)(2,1)}, u32[]{:S(2)}) copy-start(bf16[2048,128]{1,0:T(8,128)(2,1)} %a_ref.1) | copy-start | bytes 1572868
  2.3 0.7 copy-start.2
  3.8 11.2 %collective-permute-start.1 = (bf16[512,128]{1,0:T(8,128)(2,1)S(1)}, bf16[512,128]{1,0:T(8,128)(2,1)S(1)}, u32[]{:S(2)}, u32[]{:S(2)}) collective-permute-start(bf16[512,128]{1,0:T(8,128)(2,1)S(1)} %get-tuple-element.27), channel_id=1, source_target_pairs={{0,1},{1,2},{2,3},{3,0},{4,5},{5,6},{6,7},{7,4},{8,9},{9,10},{10,1... | collective-permute-start | bytes 393224 | tf_op jit(solution)/shard_map/ppermute | solution.py:52
  5.5 9.5 %collective-permute-start.2 = (bf16[512,128]{1,0:T(8,128)(2,1)S(1)}, bf16[512,128]{1,0:T(8,128)(2,1)S(1)}, u32[]{:S(2)}, u32[]{:S(2)}) collective-permute-start(bf16[512,128]{1,0:T(8,128)(2,1)S(1)} %get-tuple-element.28), channel_id=1, source_target_pairs={{0,3},{1,0},{2,1},{3,2},{4,7},{5,4},{6,5},{7,6},{8,11},{9,8},{10,9... | collective-permute-start | bytes 393224 | tf_op jit(solution)/shard_map/ppermute | solution.py:52
  7.1 8.4 %collective-permute-start.3 = (bf16[512,128]{1,0:T(8,128)(2,1)S(1)}, bf16[512,128]{1,0:T(8,128)(2,1)S(1)}, u32[]{:S(2)}, u32[]{:S(2)}) collective-permute-start(bf16[512,128]{1,0:T(8,128)(2,1)S(1)} %get-tuple-element.29), channel_id=1, source_target_pairs={{0,2},{1,3},{2,0},{3,1},{4,6},{5,7},{6,4},{7,5},{8,10},{9,11},{10,... | collective-permute-start | bytes 393224 | tf_op jit(solution)/shard_map/ppermute | solution.py:52
  9.1 11.4 %collective-permute-start.7 = (bf16[1040,128]{1,0:T(8,128)(2,1)S(1)}, bf16[1040,128]{1,0:T(8,128)(2,1)S(1)}, u32[]{:S(2)}, u32[]{:S(2)}) collective-permute-start(bf16[1040,128]{1,0:T(8,128)(2,1)S(1)} %shard_map.38.refs_0_), channel_id=1, source_target_pairs={{0,4},{1,5},{2,6},{3,7},{4,8},{5,9},{6,10},{7,11},{8,12},{9,13},{1... | collective-permute-start | bytes 798728 | tf_op jit(solution)/shard_map/ppermute | solution.py:52
  11.0 15.0 %collective-permute-start.9 = (bf16[1040,128]{1,0:T(8,128)(2,1)S(1)}, bf16[1040,128]{1,0:T(8,128)(2,1)S(1)}, u32[]{:S(2)}, u32[]{:S(2)}) collective-permute-start(bf16[1040,128]{1,0:T(8,128)(2,1)S(1)} %shard_map.38.refs_0_), channel_id=1, source_target_pairs={{0,28},{1,29},{2,30},{3,31},{4,0},{5,1},{6,2},{7,3},{8,4},{9,5},{1... | collective-permute-start | bytes 798728 | tf_op jit(solution)/shard_map/ppermute | solution.py:52
  15.6 21.0 %collective-permute-start.4 = (bf16[512,512]{1,0:T(8,128)(2,1)S(1)}, bf16[512,512]{1,0:T(8,128)(2,1)S(1)}, u32[]{:S(2)}, u32[]{:S(2)}) collective-permute-start(bf16[512,512]{1,0:T(8,128)(2,1)S(1)} %shard_map.40.refs_0_), channel_id=1, source_target_pairs={{0,64},{64,128},{128,192},{192,0},{32,224},{96,32},{160,96},{224,1... | collective-permute-start | bytes 1572872 | tf_op jit(solution)/shard_map/ppermute | solution.py:60
  17.2 19.4 %collective-permute-start.6 = (bf16[512,512]{1,0:T(8,128)(2,1)S(1)}, bf16[512,512]{1,0:T(8,128)(2,1)S(1)}, u32[]{:S(2)}, u32[]{:S(2)}) collective-permute-start(bf16[512,512]{1,0:T(8,128)(2,1)S(1)} %shard_map.40.refs_0_), channel_id=1, source_target_pairs={{0,192},{64,0},{128,64},{192,128},{32,96},{96,160},{160,224},{224,... | collective-permute-start | bytes 1572872 | tf_op jit(solution)/shard_map/ppermute | solution.py:60
  20.5 16.1 %collective-permute-start.8 = (bf16[1040,128]{1,0:T(8,128)(2,1)S(1)}, bf16[1040,128]{1,0:T(8,128)(2,1)S(1)}, u32[]{:S(2)}, u32[]{:S(2)}) collective-permute-start(bf16[1040,128]{1,0:T(8,128)(2,1)S(1)} %collective-permute-done.7.refs_1_), channel_id=1, source_target_pairs={{0,12},{1,13},{2,14},{3,15},{4,16},{5,17},{6,18},{7,19},{8,20},{9,... | collective-permute-start | bytes 798728 | tf_op jit(solution)/shard_map/ppermute | solution.py:52
  22.3 17.1 %collective-permute-start.10 = (bf16[1040,128]{1,0:T(8,128)(2,1)S(1)}, bf16[1040,128]{1,0:T(8,128)(2,1)S(1)}, u32[]{:S(2)}, u32[]{:S(2)}) collective-permute-start(bf16[1040,128]{1,0:T(8,128)(2,1)S(1)} %collective-permute-done.7.refs_1_), channel_id=1, source_target_pairs={{0,4},{1,5},{2,6},{3,7},{4,8},{5,9},{6,10},{7,11},{8,12},{9,13},{1... | collective-permute-start | bytes 798728 | tf_op jit(solution)/shard_map/ppermute | solution.py:52
  26.0 13.4 %collective-permute-start.11 = (bf16[1040,128]{1,0:T(8,128)(2,1)S(1)}, bf16[1040,128]{1,0:T(8,128)(2,1)S(1)}, u32[]{:S(2)}, u32[]{:S(2)}) collective-permute-start(bf16[1040,128]{1,0:T(8,128)(2,1)S(1)} %collective-permute-done.9.refs_2_), channel_id=1, source_target_pairs={{0,28},{1,29},{2,30},{3,31},{4,0},{5,1},{6,2},{7,3},{8,4},{9,5},{1... | collective-permute-start | bytes 798728 | tf_op jit(solution)/shard_map/ppermute | solution.py:52
  39.6 5.0 %collective-permute-start.12 = (bf16[5,1040,128]{2,1,0:T(8,128)(2,1)S(1)}, bf16[5,1040,128]{2,1,0:T(8,128)(2,1)S(1)}, u32[]{:S(2)}, u32[]{:S(2)}) collective-permute-start(bf16[5,1040,128]{2,1,0:T(8,128)(2,1)S(1)} %shard_map.43.refs_1_), channel_id=1, source_target_pairs={{0,32},{32,0},{1,33},{33,1},{2,34},{34,2},{3,35},{35,3},{4,36},{36... | collective-permute-start | bytes 3993608 | tf_op jit(solution)/shard_map/ppermute | solution.py:64
  39.7 11.1 %collective-permute-start.5 = (bf16[512,512]{1,0:T(8,128)(2,1)S(1)}, bf16[512,512]{1,0:T(8,128)(2,1)S(1)}, u32[]{:S(2)}, u32[]{:S(2)}) collective-permute-start(bf16[512,512]{1,0:T(8,128)(2,1)S(1)} %collective-permute-done.4.refs_2_), channel_id=1, source_target_pairs={{0,64},{64,128},{128,192},{192,0},{32,224},{96,32},{160,96},{224,1... | collective-permute-start | bytes 1572872 | tf_op jit(solution)/shard_map/ppermute | solution.py:60
  41.2 9.5 %collective-permute-start.13 = (bf16[1040,128]{1,0:T(8,128)(2,1)S(1)}, bf16[1040,128]{1,0:T(8,128)(2,1)S(1)}, u32[]{:S(2)}, u32[]{:S(2)}) collective-permute-start(bf16[1040,128]{1,0:T(8,128)(2,1)S(1)} %collective-permute-done.10.refs_3_), channel_id=1, source_target_pairs={{0,4},{1,5},{2,6},{3,7},{4,8},{5,9},{6,10},{7,11},{8,12},{9,13},{1... | collective-permute-start | bytes 798728 | tf_op jit(solution)/shard_map/ppermute | solution.py:52
  41.9 8.8 %collective-permute-start.14 = (bf16[1040,128]{1,0:T(8,128)(2,1)S(1)}, bf16[1040,128]{1,0:T(8,128)(2,1)S(1)}, u32[]{:S(2)}, u32[]{:S(2)}) collective-permute-start(bf16[1040,128]{1,0:T(8,128)(2,1)S(1)} %collective-permute-done.11.refs_4_), channel_id=1, source_target_pairs={{0,28},{1,29},{2,30},{3,31},{4,0},{5,1},{6,2},{7,3},{8,4},{9,5},{1... | collective-permute-start | bytes 798728 | tf_op jit(solution)/shard_map/ppermute | solution.py:52
  50.8 2.8 %collective-permute-start.15 = (bf16[3,1040,128]{2,1,0:T(8,128)(2,1)S(1)}, bf16[3,1040,128]{2,1,0:T(8,128)(2,1)S(1)}, u32[]{:S(2)}, u32[]{:S(2)}) collective-permute-start(bf16[3,1040,128]{2,1,0:T(8,128)(2,1)S(1)} %shard_map.45.refs_3_), channel_id=1, source_target_pairs={{0,32},{32,0},{1,33},{33,1},{2,34},{34,2},{3,35},{35,3},{4,36},{36... | collective-permute-start | bytes 2396168 | tf_op jit(solution)/shard_map/ppermute | solution.py:64
  56.6 11.9 %collective-permute-start.17 = (s16[2064,128]{1,0:T(8,128)(2,1)S(1)}, s16[2064,128]{1,0:T(8,128)(2,1)S(1)}, u32[]{:S(2)}, u32[]{:S(2)}) collective-permute-start(s16[2064,128]{1,0:T(8,128)(2,1)S(1)} %shard_map.48), channel_id=1, source_target_pairs={{0,1},{1,2},{2,3},{3,0},{4,5},{5,6},{6,7},{7,4},{8,9},{9,10},{10,1... | collective-permute-start | bytes 1585160 | tf_op jit(solution)/shard_map/ppermute | solution.py:52
  61.2 11.6 %collective-permute-start.16 = (s16[2064,128]{1,0:T(8,128)(2,1)S(1)}, s16[2064,128]{1,0:T(8,128)(2,1)S(1)}, u32[]{:S(2)}, u32[]{:S(2)}) collective-permute-start(s16[2064,128]{1,0:T(8,128)(2,1)S(1)} %get-tuple-element.36), channel_id=1, source_target_pairs={{0,3},{1,0},{2,1},{3,2},{4,7},{5,4},{6,5},{7,6},{8,11},{9,8},{10,9... | collective-permute-start | bytes 1585160 | tf_op jit(solution)/shard_map/ppermute | solution.py:52
  69.1 10.5 %collective-permute-start.18 = (s16[2064,128]{1,0:T(8,128)(2,1)S(1)}, s16[2064,128]{1,0:T(8,128)(2,1)S(1)}, u32[]{:S(2)}, u32[]{:S(2)}) collective-permute-start(s16[2064,128]{1,0:T(8,128)(2,1)S(1)} %shard_map.49), channel_id=1, source_target_pairs={{0,1},{1,2},{2,3},{3,0},{4,5},{5,6},{6,7},{7,4},{8,9},{9,10},{10,1... | collective-permute-start | bytes 1585160 | tf_op jit(solution)/shard_map/ppermute | solution.py:52
  80.2 9.4 %collective-permute-start.19 = (f32[1024,128]{1,0:T(8,128)S(1)}, f32[1024,128]{1,0:T(8,128)S(1)}, u32[]{:S(2)}, u32[]{:S(2)}) collective-permute-start(f32[1024,128]{1,0:T(8,128)S(1)} %get-tuple-element.39), channel_id=1, source_target_pairs={{0,32},{32,0},{1,33},{33,1},{2,34},{34,2},{3,35},{35,3},{4,36},{36... | collective-permute-start | bytes 1572872 | tf_op jit(solution)/shard_map/ppermute | solution.py:64
  80.3 1.9 %collective-permute-start.20 = (f32[1,128]{1,0:T(1,128)S(1)}, f32[1,128]{1,0:T(1,128)S(1)}, u32[]{:S(2)}, u32[]{:S(2)}) collective-permute-start(f32[1,128]{1,0:T(1,128)S(1)} %get-tuple-element.40), channel_id=1, source_target_pairs={{0,32},{32,0},{1,33},{33,1},{2,34},{34,2},{3,35},{35,3},{4,36},{36... | collective-permute-start | bytes 1544 | tf_op jit(solution)/shard_map/ppermute | solution.py:64
  82.2 5.0 %collective-permute-start.21 = (f32[2,128]{1,0:T(2,128)S(1)}, f32[2,128]{1,0:T(2,128)S(1)}, u32[]{:S(2)}, u32[]{:S(2)}) collective-permute-start(f32[2,128]{1,0:T(2,128)S(1)} %pad_maximum_fusion.refs_0_), channel_id=1, source_target_pairs={{0,64},{64,128},{128,192},{192,0},{32,224},{96,32},{160,96},{224,1... | collective-permute-start | bytes 3080 | tf_op jit(solution)/shard_map/ppermute | solution.py:60
  84.5 3.6 %collective-permute-start.22 = (f32[2,128]{1,0:T(2,128)S(1)}, f32[2,128]{1,0:T(2,128)S(1)}, u32[]{:S(2)}, u32[]{:S(2)}) collective-permute-start(f32[2,128]{1,0:T(2,128)S(1)} %pad_maximum_fusion.refs_0_), channel_id=1, source_target_pairs={{0,192},{64,0},{128,64},{192,128},{32,96},{96,160},{160,224},{224,... | collective-permute-start | bytes 3080 | tf_op jit(solution)/shard_map/ppermute | solution.py:60
  84.5 5.1 %collective-permute-start.23 = (f32[2,128]{1,0:T(2,128)S(1)}, f32[2,128]{1,0:T(2,128)S(1)}, u32[]{:S(2)}, u32[]{:S(2)}) collective-permute-start(f32[2,128]{1,0:T(2,128)S(1)} %pad_maximum_fusion.refs_0_), channel_id=1, source_target_pairs={{0,128},{64,192},{128,0},{192,64},{32,160},{96,224},{160,32},{224,... | collective-permute-start | bytes 3080 | tf_op jit(solution)/shard_map/ppermute | solution.py:60

commit v4 on v3

--- a/solution.py
+++ b/solution.py
@@ -16,6 +16,7 @@
 LEVELS = 65535
 FINE = 64
 BATCH = 4
+PIECES = 4
 MIB = 1024 * 1024
 VMEM = pl.BlockSpec(memory_space=pltpu.VMEM)
 SMEM = pl.BlockSpec(memory_space=pltpu.SMEM)
@@ -292,15 +293,37 @@
 
 
 def scale_kernel(n_total, keep_ref, recv_ref, *refs):
-    out_ref = refs[-1]
-    total = refs[0][...]
-    for ref in refs[1:-1]:
+    sums, (out_hbm, out_ref, sems) = refs[:-3], refs[-3:]
+    total = sums[0][...]
+    for ref in sums[1:]:
         total += ref[...]
     core = lax.axis_index("col")
-    own = jnp.float32(n_total) * keep_ref[...] / total[0:1, :]
-    other = jnp.float32(n_total) * recv_ref[...] / total[1:2, :]
-    out_ref[:, :TILE] = jnp.where(core == 0, own, other)
-    out_ref[:, TILE:] = jnp.where(core == 0, other, own)
+    rows = keep_ref.shape[0] // PIECES
+    copies = []
+    for i in range(PIECES):
+        part = slice(i * rows, (i + 1) * rows)
+        own = jnp.float32(n_total) * keep_ref[part, :] / total[0:1, :]
+        other = jnp.float32(n_total) * recv_ref[part, :] / total[1:2, :]
+        out_ref[part, :TILE] = jnp.where(core == 0, own, other)
+        out_ref[part, TILE:] = jnp.where(core == 0, other, own)
+        copies.append(
+            pltpu.make_async_copy(out_ref.at[part, :], out_hbm.at[part, :], sems.at[i])
+        )
+        copies[-1].start()
+    for copy in copies:
+        copy.wait()
+
+
+def scale(n_total, keep, recv, sums):
+    shape = (keep.shape[0], 2 * TILE)
+    return pl.pallas_call(
+        functools.partial(scale_kernel, n_total),
+        out_shape=struct(shape, jnp.float32),
+        in_specs=[VMEM] * (2 + len(sums)),
+        out_specs=pl.BlockSpec(memory_space=pl.ANY),
+        scratch_shapes=[pltpu.VMEM(shape, jnp.float32), pltpu.SemaphoreType.DMA((PIECES,))],
+        compiler_params=pltpu.CompilerParams(vmem_limit_bytes=8 * MIB),
+    )(keep, recv, *sums)
 
 
 def on_device(a_matrix, b_matrix, tile_map):
@@ -317,23 +340,23 @@
     )
     a1, b1 = hop(p, 1, 0), hop(p, -1, 0)
     blocks = call(block_kernel, [struct((512, TILE), b_matrix.dtype)] * 4, after(keep, p), recv)
-    blocks = [blocks[0]] + [hop(m, 0, d) for m, d in zip(blocks[1:], (1, -1, 2))]
+    far_y = hop(blocks[3], 0, 2)
+    blocks = [blocks[0], hop(blocks[1], 0, 1), hop(blocks[2], 0, -1), far_y]
     wide = call(widen_kernel, struct((512, 4 * TILE), b_matrix.dtype), *blocks)
 
     a1, b1 = after(a1, wide), after(b1, wide)
-    a2, b2, a4 = hop(a1, 1, 0), hop(b1, -1, 0), hop(a1, 3, 0)
+    a3, a2, b2 = hop(a1, 2, 0), hop(a1, 1, 0), hop(b1, -1, 0)
     back, ahead = hop_x(wide, 1), hop_x(wide, -1)
-    near = join([after(p, back, ahead, a4), a1, b1, a2, b2])
+    near = join([after(p, back, ahead), a1, b1, a2, b2, a3])
     near_other = swap(near)
-    a2, b2 = after(a2, back, ahead, a4), after(b2, back, ahead, a4)
-    a3, b3 = hop(a2, 1, 0), hop(b2, -1, 0)
+    a4, b3 = hop(after(a3, back, ahead), 1, 0), hop(after(b2, back, ahead), -1, 0)
     across = hop_x(back, 1)
 
     panels = stack([wide, ahead, back], (0, 1, 3))
-    near_steps, far_steps = (0, -1, 1, -2, 2), (-3, 3, -4)
+    near_steps, far_steps = (0, -1, 1, -2, 2, -3), (3, -4)
     held = (0, 1, 3)
     (total,) = product(panels, [near, near_other], [(0, held, near_steps), (1, held, near_steps)])
-    far = join([after(a3, across, total), b3, a4])
+    far = join([after(b3, across, total), a4])
     far_other = swap(far)
     panels = stack([across], (2,), panels)
     every = (0, 1, 2, 3)
@@ -365,15 +388,9 @@
         *sums,
     )
     column = jnp.concatenate([column, swap(column)])
-    recv = swap(send)
+    recv = swap(after(send, column))
     columns = [column] + [hop_x(column, d) for d in (1, -1, 2)]
-    return call(
-        functools.partial(scale_kernel, n_total),
-        struct((half, 2 * TILE), jnp.float32),
-        keep,
-        recv,
-        *columns,
-    )
+    return scale(n_total, keep, recv, columns)
 
 
 def solution(mesh):

time: 91.8 us -> 88.5 us (0.964)
  starting transfers between devices: 34.6 us -> 29.3 us
  waiting for transfers between devices: 38.1 us -> 40.8 us
    ppermute x6, waiting for transfers between devices: 2.35 us -> 9.65 us  [hop_x(): return lax.ppermute(x, ('row', 'col'), pairs)]
    ppermute x13, waiting for transfers between devices: 32.5 us -> 28.2 us  [hop(): return lax.ppermute(x, ('col', 'layer'), pairs)]
    ppermute x13, starting transfers between devices: 24.3 us -> 20.6 us  [hop(): return lax.ppermute(x, ('col', 'layer'), pairs)]
    pallas_call x15 -> x14, Pallas kernels: 15.1 us -> 13.8 us  [call(): pl.pallas_call(kernel, out_shape=out_shape, in_specs=[first] + [VMEM] * (...]
    ppermute x5, starting transfers between devices: 1.62 us -> 0.58 us  [swap(): return lax.ppermute(x, 'col', [(0, 1), (1, 0)])]
    pallas_call x0 -> x1, Pallas kernels: none -> 1.04 us  [scale(): pl.pallas_call(functools.partial(scale_kernel, n_total), out_shape=struct...]
  transfers between devices with their start and end apart: 24 -> 24, of which waited for: 12 -> 14; matrix products, arithmetic and copies ran while one was open for 0% -> 0% of each run, Pallas kernels for 11% -> 12%
where the time goes in v4:
time: 88.5 us; the launch traced here: 88.1 us
  waiting for transfers between devices  40.8 us (46%)
  starting transfers between devices  29.3 us (33%)
  Pallas kernels  14.9 us (17%)
  local copies, waits for them, and re-layouts  2.73 us (3%)
    ppermute x13, waiting for transfers between devices, hop(): return lax.ppermute(x, ('col', 'layer'), pairs)  28.2 us
    ppermute x13, starting transfers between devices, hop(): return lax.ppermute(x, ('col', 'layer'), pairs)  20.6 us
    pallas_call x14, Pallas kernels, call(): pl.pallas_call(kernel, out_shape=out_shape, in_specs=[first] + [VMEM] * (...  13.8 us
    ppermute x6, waiting for transfers between devices, hop_x(): return lax.ppermute(x, ('row', 'col'), pairs)  9.65 us
    ppermute x6, starting transfers between devices, hop_x(): return lax.ppermute(x, ('row', 'col'), pairs)  8.16 us
    ppermute x5, waiting for transfers between devices, swap(): return lax.ppermute(x, 'col', [(0, 1), (1, 0)])  2.98 us
    unnamed x6, local copies, waits for them, and re-layouts  2.73 us
  transfers between devices with their start and end apart: 24, of which 14 were waited for; matrix products, arithmetic and copies ran while one was open for 0% of the time, Pallas kernels for 12%

profile of v4, /device:TPU:2, one launch (start us, length us, event | category | flops | bytes accessed | tf_op | source)
XLA Modules:
  0.0 88.1 jit_solution(17432498656754557486)
XLA Ops:
  0.0 1.0 %copy-done = bf16[1024,256]{1,0:T(8,128)(2,1)S(1)} copy-done((bf16[1024,256]{1,0:T(8,128)(2,1)S(1)}, bf16[1024,256]{1,0:T(8,128)(2,1)}, u32[]{:S(2)}) %copy-start) | copy-done | bytes 524312
  1.3 1.0 %copy-done.1 = bf16[2048,128]{1,0:T(8,128)(2,1)S(1)} copy-done((bf16[2048,128]{1,0:T(8,128)(2,1)S(1)}, bf16[2048,128]{1,0:T(8,128)(2,1)}, u32[]{:S(2)}) %copy-start.1) | copy-done | bytes 524312
  3.0 0.8 shard_map.38.refs_0_
  3.8 1.7 %collective-permute-start.1 = (bf16[512,128]{1,0:T(8,128)(2,1)S(1)}, bf16[512,128]{1,0:T(8,128)(2,1)S(1)}, u32[]{:S(2)}, u32[]{:S(2)}) collective-permute-start(bf16[512,128]{1,0:T(8,128)(2,1)S(1)} %get-tuple-element.28), channel_id=1, source_target_pairs={{0,1},{1,2},{2,3},{3,0},{4,5},{5,6},{6,7},{7,4},{8,9},{9,10},{10,1... | collective-permute-start | bytes 393224 | tf_op jit(solution)/shard_map/ppermute | solution.py:53
  5.5 1.7 %collective-permute-start.2 = (bf16[512,128]{1,0:T(8,128)(2,1)S(1)}, bf16[512,128]{1,0:T(8,128)(2,1)S(1)}, u32[]{:S(2)}, u32[]{:S(2)}) collective-permute-start(bf16[512,128]{1,0:T(8,128)(2,1)S(1)} %get-tuple-element.29), channel_id=1, source_target_pairs={{0,3},{1,0},{2,1},{3,2},{4,7},{5,4},{6,5},{7,6},{8,11},{9,8},{10,9... | collective-permute-start | bytes 393224 | tf_op jit(solution)/shard_map/ppermute | solution.py:53
  7.1 2.0 %collective-permute-start.3 = (bf16[512,128]{1,0:T(8,128)(2,1)S(1)}, bf16[512,128]{1,0:T(8,128)(2,1)S(1)}, u32[]{:S(2)}, u32[]{:S(2)}) collective-permute-start(bf16[512,128]{1,0:T(8,128)(2,1)S(1)} %get-tuple-element.30), channel_id=1, source_target_pairs={{0,2},{1,3},{2,0},{3,1},{4,6},{5,7},{6,4},{7,5},{8,10},{9,11},{10,... | collective-permute-start | bytes 393224 | tf_op jit(solution)/shard_map/ppermute | solution.py:53
  9.1 1.9 %collective-permute-start.7 = (bf16[1040,128]{1,0:T(8,128)(2,1)S(1)}, bf16[1040,128]{1,0:T(8,128)(2,1)S(1)}, u32[]{:S(2)}, u32[]{:S(2)}) collective-permute-start(bf16[1040,128]{1,0:T(8,128)(2,1)S(1)} %shard_map.38.refs_0_), channel_id=1, source_target_pairs={{0,4},{1,5},{2,6},{3,7},{4,8},{5,9},{6,10},{7,11},{8,12},{9,13},{1... | collective-permute-start | bytes 798728 | tf_op jit(solution)/shard_map/ppermute | solution.py:53
  11.0 3.9 %collective-permute-start.8 = (bf16[1040,128]{1,0:T(8,128)(2,1)S(1)}, bf16[1040,128]{1,0:T(8,128)(2,1)S(1)}, u32[]{:S(2)}, u32[]{:S(2)}) collective-permute-start(bf16[1040,128]{1,0:T(8,128)(2,1)S(1)} %shard_map.38.refs_0_), channel_id=1, source_target_pairs={{0,28},{1,29},{2,30},{3,31},{4,0},{5,1},{6,2},{7,3},{8,4},{9,5},{1... | collective-permute-start | bytes 798728 | tf_op jit(solution)/shard_map/ppermute | solution.py:53
  15.6 1.6 %collective-permute-start.4 = (bf16[512,512]{1,0:T(8,128)(2,1)S(1)}, bf16[512,512]{1,0:T(8,128)(2,1)S(1)}, u32[]{:S(2)}, u32[]{:S(2)}) collective-permute-start(bf16[512,512]{1,0:T(8,128)(2,1)S(1)} %shard_map.40.refs_0_), channel_id=1, source_target_pairs={{0,64},{64,128},{128,192},{192,0},{32,224},{96,32},{160,96},{224,1... | collective-permute-start | bytes 1572872 | tf_op jit(solution)/shard_map/ppermute | solution.py:61
  17.7 2.8 %collective-permute-done.7.refs_1_ = bf16[1040,128]{1,0:T(8,128)(2,1)S(1)} collective-permute-done((bf16[1040,128]{1,0:T(8,128)(2,1)S(1)}, bf16[1040,128]{1,0:T(8,128)(2,1)S(1)}, u32[]{:S(2)}, u32[]{:S(2)}) %collective-permute-start.7) | collective-permute-done | bytes 266272 | tf_op jit(solution)/shard_map/ppermute | solution.py:53
  21.0 3.1 %collective-permute-start.10 = (bf16[1040,128]{1,0:T(8,128)(2,1)S(1)}, bf16[1040,128]{1,0:T(8,128)(2,1)S(1)}, u32[]{:S(2)}, u32[]{:S(2)}) collective-permute-start(bf16[1040,128]{1,0:T(8,128)(2,1)S(1)} %collective-permute-done.8.refs_2_), channel_id=1, source_target_pairs={{0,28},{1,29},{2,30},{3,31},{4,0},{5,1},{6,2},{7,3},{8,4},{9,5},{1... | collective-permute-start | bytes 798728 | tf_op jit(solution)/shard_map/ppermute | solution.py:53
  24.1 6.0 %collective-permute-done.4.refs_2_ = bf16[512,512]{1,0:T(8,128)(2,1)S(1)} collective-permute-done((bf16[512,512]{1,0:T(8,128)(2,1)S(1)}, bf16[512,512]{1,0:T(8,128)(2,1)S(1)}, u32[]{:S(2)}, u32[]{:S(2)}) %collective-permute-start.4) | collective-permute-done | bytes 524320 | tf_op jit(solution)/shard_map/ppermute | solution.py:61
  30.2 3.0 %collective-permute-done.11.refs_5_ = bf16[1040,128]{1,0:T(8,128)(2,1)S(1)} collective-permute-done((bf16[1040,128]{1,0:T(8,128)(2,1)S(1)}, bf16[1040,128]{1,0:T(8,128)(2,1)S(1)}, u32[]{:S(2)}, u32[]{:S(2)}) %collective-permute-start.11) | collective-permute-done | bytes 266272 | tf_op jit(solution)/shard_map/ppermute | solution.py:53
  33.6 3.0 %collective-permute-done.9.refs_3_ = bf16[1040,128]{1,0:T(8,128)(2,1)S(1)} collective-permute-done((bf16[1040,128]{1,0:T(8,128)(2,1)S(1)}, bf16[1040,128]{1,0:T(8,128)(2,1)S(1)}, u32[]{:S(2)}, u32[]{:S(2)}) %collective-permute-start.9) | collective-permute-done | bytes 266272 | tf_op jit(solution)/shard_map/ppermute | solution.py:53
  36.8 1.6 %collective-permute-start.5 = (bf16[512,512]{1,0:T(8,128)(2,1)S(1)}, bf16[512,512]{1,0:T(8,128)(2,1)S(1)}, u32[]{:S(2)}, u32[]{:S(2)}) collective-permute-start(bf16[512,512]{1,0:T(8,128)(2,1)S(1)} %collective-permute-done.4.refs_2_), channel_id=1, source_target_pairs={{0,64},{64,128},{128,192},{192,0},{32,224},{96,32},{160,96},{224,1... | collective-permute-start | bytes 1572872 | tf_op jit(solution)/shard_map/ppermute | solution.py:61
  38.4 1.9 %collective-permute-start.13 = (bf16[1040,128]{1,0:T(8,128)(2,1)S(1)}, bf16[1040,128]{1,0:T(8,128)(2,1)S(1)}, u32[]{:S(2)}, u32[]{:S(2)}) collective-permute-start(bf16[1040,128]{1,0:T(8,128)(2,1)S(1)} %collective-permute-done.10.refs_4_), channel_id=1, source_target_pairs={{0,28},{1,29},{2,30},{3,31},{4,0},{5,1},{6,2},{7,3},{8,4},{9,5},{1... | collective-permute-start | bytes 798728 | tf_op jit(solution)/shard_map/ppermute | solution.py:53
  40.5 3.7 %shard_map.44.refs_5_ = f32[2176,512]{1,0:T(8,128)S(1)} custom-call(bf16[4,512,512]{2,1,0:T(8,128)(2,1)S(1)} %shard_map.41.refs_1_.refs_0_, bf16[6,1040,128]{2,1,0:T(8,128)(2,1)S(1)} %shard_map.43.refs_1_, bf16[6,1040,128]{2,1,0:T(8,128)(2,1)S(1)} %collective-permute-done.12.refs_2_), custom_call_target="tpu_custom_call" | custom-call | flops 1635778560 | bytes 12779520 | tf_op jit(solution)/shard_map/pallas_call | solution.py:31
  44.3 2.7 %collective-permute-done.13.refs_0_ = bf16[1040,128]{1,0:T(8,128)(2,1)S(1)} collective-permute-done((bf16[1040,128]{1,0:T(8,128)(2,1)S(1)}, bf16[1040,128]{1,0:T(8,128)(2,1)S(1)}, u32[]{:S(2)}, u32[]{:S(2)}) %collective-permute-start.13) | collective-permute-done | bytes 266272 | tf_op jit(solution)/shard_map/ppermute | solution.py:53
  47.0 1.2 %collective-permute-done.14.refs_1_ = bf16[1040,128]{1,0:T(8,128)(2,1)S(1)} collective-permute-done((bf16[1040,128]{1,0:T(8,128)(2,1)S(1)}, bf16[1040,128]{1,0:T(8,128)(2,1)S(1)}, u32[]{:S(2)}, u32[]{:S(2)}) %collective-permute-start.14) | collective-permute-done | bytes 266272 | tf_op jit(solution)/shard_map/ppermute | solution.py:53
  48.4 1.9 %collective-permute-done.15.refs_4_ = bf16[2,1040,128]{2,1,0:T(8,128)(2,1)S(1)} collective-permute-done((bf16[2,1040,128]{2,1,0:T(8,128)(2,1)S(1)}, bf16[2,1040,128]{2,1,0:T(8,128)(2,1)S(1)}, u32[]{:S(2)}, u32[]{:S(2)}) %collective-permute-start.15) | collective-permute-done | bytes 532512 | tf_op jit(solution)/shard_map/ppermute | solution.py:65
  50.3 2.6 %shard_map.48 = s16[2064,128]{1,0:T(8,128)(2,1)S(1)} custom-call(bf16[4,512,512]{2,1,0:T(8,128)(2,1)S(1)} %shard_map.42.refs_0_, bf16[6,1040,128]{2,1,0:T(8,128)(2,1)S(1)} %shard_map.43.refs_1_, bf16[6,1040,128]{2,1,0:T(8,128)(2,1)S(1)} %collective-permute-done.12.refs_2_, bf16[2,1040,128]{2,1,0:T(8,128)(2,1)S(1)} %shard_map.45.refs_3_, ...), custom_call_target="tpu_custom_call" | custom-call | flops 545259520 | bytes 4259840 | tf_op jit(solution)/shard_map/pallas_call | solution.py:31
  53.3 2.8 %shard_map.47 = (s16[2064,128]{1,0:T(8,128)(2,1)S(1)}, f32[2176,128]{1,0:T(8,128)S(1)}) custom-call(bf16[4,512,512]{2,1,0:T(8,128)(2,1)S(1)} %shard_map.42.refs_0_, bf16[6,1040,128]{2,1,0:T(8,128)(2,1)S(1)} %shard_map.43.refs_1_, bf16[6,1040,128]{2,1,0:T(8,128)(2,1)S(1)} %collective-permute-done.12.refs_2_, bf16[2,1040,128]{2,1,0:T(8,128)(2,1)S(1)} %shard_map.45.refs_3_, ...), custom_call_target="tpu_custom_call" | custom-call | flops 1090519040 | bytes 8519680 | tf_op jit(solution)/shard_map/pallas_call | solution.py:31
  56.1 3.2 %collective-permute-start.16 = (s16[2064,128]{1,0:T(8,128)(2,1)S(1)}, s16[2064,128]{1,0:T(8,128)(2,1)S(1)}, u32[]{:S(2)}, u32[]{:S(2)}) collective-permute-start(s16[2064,128]{1,0:T(8,128)(2,1)S(1)} %get-tuple-element.37), channel_id=1, source_target_pairs={{0,3},{1,0},{2,1},{3,2},{4,7},{5,4},{6,5},{7,6},{8,11},{9,8},{10,9... | collective-permute-start | bytes 1585160 | tf_op jit(solution)/shard_map/ppermute | solution.py:53
  59.3 6.4 %collective-permute-done.17.recv_ref = s16[2064,128]{1,0:T(8,128)(2,1)S(1)} collective-permute-done((s16[2064,128]{1,0:T(8,128)(2,1)S(1)}, s16[2064,128]{1,0:T(8,128)(2,1)S(1)}, u32[]{:S(2)}, u32[]{:S(2)}) %collective-permute-start.17) | collective-permute-done | bytes 528416 | tf_op jit(solution)/shard_map/ppermute | solution.py:53
  66.4 2.3 %shard_map.46.total_ref = f32[2176,128]{1,0:T(8,128)S(1)} custom-call(bf16[4,512,512]{2,1,0:T(8,128)(2,1)S(1)} %shard_map.42.refs_0_, bf16[6,1040,128]{2,1,0:T(8,128)(2,1)S(1)} %shard_map.43.refs_1_, bf16[6,1040,128]{2,1,0:T(8,128)(2,1)S(1)} %collective-permute-done.12.refs_2_, bf16[2,1040,128]{2,1,0:T(8,128)(2,1)S(1)} %shard_map.45.refs_3_, ...), custom_call_target="tpu_custom_call" | custom-call | flops 545259520 | bytes 4259840 | tf_op jit(solution)/shard_map/pallas_call | solution.py:31
  68.7 8.1 %collective-permute-done.18.refs_1_ = s16[2064,128]{1,0:T(8,128)(2,1)S(1)} collective-permute-done((s16[2064,128]{1,0:T(8,128)(2,1)S(1)}, s16[2064,128]{1,0:T(8,128)(2,1)S(1)}, u32[]{:S(2)}, u32[]{:S(2)}) %collective-permute-start.18) | collective-permute-done | bytes 528416 | tf_op jit(solution)/shard_map/ppermute | solution.py:53
  77.5 1.1 %collective-permute-done.19 = f32[1,128]{1,0:T(1,128)S(1)} collective-permute-done((f32[1,128]{1,0:T(1,128)S(1)}, f32[1,128]{1,0:T(1,128)S(1)}, u32[]{:S(2)}, u32[]{:S(2)}) %collective-permute-start.19) | collective-permute-done | bytes 544 | tf_op jit(solution)/shard_map/ppermute | solution.py:65
  78.8 3.0 %collective-permute-start.21 = (f32[2,128]{1,0:T(2,128)S(1)}, f32[2,128]{1,0:T(2,128)S(1)}, u32[]{:S(2)}, u32[]{:S(2)}) collective-permute-start(f32[2,128]{1,0:T(2,128)S(1)} %pad_maximum_fusion.refs_0_), channel_id=1, source_target_pairs={{0,64},{64,128},{128,192},{192,0},{32,224},{96,32},{160,96},{224,1... | collective-permute-start | bytes 3080 | tf_op jit(solution)/shard_map/ppermute | solution.py:61
  81.8 1.5 %collective-permute-start.23 = (f32[2,128]{1,0:T(2,128)S(1)}, f32[2,128]{1,0:T(2,128)S(1)}, u32[]{:S(2)}, u32[]{:S(2)}) collective-permute-start(f32[2,128]{1,0:T(2,128)S(1)} %pad_maximum_fusion.refs_0_), channel_id=1, source_target_pairs={{0,128},{64,192},{128,0},{192,64},{32,160},{96,224},{160,32},{224,... | collective-permute-start | bytes 3080 | tf_op jit(solution)/shard_map/ppermute | solution.py:61
  83.3 2.1 %collective-permute-done.22.refs_2_ = f32[2,128]{1,0:T(2,128)S(1)} collective-permute-done((f32[2,128]{1,0:T(2,128)S(1)}, f32[2,128]{1,0:T(2,128)S(1)}, u32[]{:S(2)}, u32[]{:S(2)}) %collective-permute-start.22) | collective-permute-done | bytes 1056 | tf_op jit(solution)/shard_map/ppermute | solution.py:61
  85.4 1.5 %collective-permute-done.23.refs_3_ = f32[2,128]{1,0:T(2,128)S(1)} collective-permute-done((f32[2,128]{1,0:T(2,128)S(1)}, f32[2,128]{1,0:T(2,128)S(1)}, u32[]{:S(2)}, u32[]{:S(2)}) %collective-permute-start.23) | collective-permute-done | bytes 1056 | tf_op jit(solution)/shard_map/ppermute | solution.py:61
  86.9 1.0 %shard_map.51 = f32[1024,256]{1,0:T(8,128)} custom-call(f32[1024,128]{1,0:T(8,128)S(1)} %get-tuple-element.39.keep_ref, f32[1024,128]{1,0:T(8,128)S(1)} %collective-permute-done.20.recv_ref, f32[2,128]{1,0:T(2,128)S(1)} %pad_maximum_fusion.refs_0_, f32[2,128]{1,0:T(2,128)S(1)} %collective-permute-done.21.refs_1_, ...), custom_call_target="tpu_custom_call" | custom-call | tf_op jit(solution)/shard_map/pallas_call | solution.py:319
  (38 shorter events, 5.6 us)
Async XLA Ops:
  0.0 1.0 %copy-start = (bf16[1024,256]{1,0:T(8,128)(2,1)S(1)}, bf16[1024,256]{1,0:T(8,128)(2,1)}, u32[]{:S(2)}) copy-start(bf16[1024,256]{1,0:T(8,128)(2,1)} %b_ref.1) | copy-start | bytes 1572868
  1.2 2.6 %collective-permute-start = (bf16[1024,128]{1,0:T(8,128)(2,1)S(1)}, bf16[1024,128]{1,0:T(8,128)(2,1)S(1)}, u32[]{:S(2)}, u32[]{:S(2)}) collective-permute-start(bf16[1024,128]{1,0:T(8,128)(2,1)S(1)} %get-tuple-element.26), channel_id=1, source_target_pairs={{0,32},{32,0},{1,33},{33,1},{2,34},{34,2},{3,35},{35,3},{4,36},{36... | collective-permute-start | bytes 786440 | tf_op jit(solution)/shard_map/ppermute | solution.py:65
  1.3 1.0 %copy-start.1 = (bf16[2048,128]{1,0:T(8,128)(2,1)S(1)}, bf16[2048,128]{1,0:T(8,128)(2,1)}, u32[]{:S(2)}) copy-start(bf16[2048,128]{1,0:T(8,128)(2,1)} %a_ref.1) | copy-start | bytes 1572868
  2.3 0.7 copy-start.2
  3.8 11.2 %collective-permute-start.1 = (bf16[512,128]{1,0:T(8,128)(2,1)S(1)}, bf16[512,128]{1,0:T(8,128)(2,1)S(1)}, u32[]{:S(2)}, u32[]{:S(2)}) collective-permute-start(bf16[512,128]{1,0:T(8,128)(2,1)S(1)} %get-tuple-element.28), channel_id=1, source_target_pairs={{0,1},{1,2},{2,3},{3,0},{4,5},{5,6},{6,7},{7,4},{8,9},{9,10},{10,1... | collective-permute-start | bytes 393224 | tf_op jit(solution)/shard_map/ppermute | solution.py:53
  5.5 9.5 %collective-permute-start.2 = (bf16[512,128]{1,0:T(8,128)(2,1)S(1)}, bf16[512,128]{1,0:T(8,128)(2,1)S(1)}, u32[]{:S(2)}, u32[]{:S(2)}) collective-permute-start(bf16[512,128]{1,0:T(8,128)(2,1)S(1)} %get-tuple-element.29), channel_id=1, source_target_pairs={{0,3},{1,0},{2,1},{3,2},{4,7},{5,4},{6,5},{7,6},{8,11},{9,8},{10,9... | collective-permute-start | bytes 393224 | tf_op jit(solution)/shard_map/ppermute | solution.py:53
  7.1 8.4 %collective-permute-start.3 = (bf16[512,128]{1,0:T(8,128)(2,1)S(1)}, bf16[512,128]{1,0:T(8,128)(2,1)S(1)}, u32[]{:S(2)}, u32[]{:S(2)}) collective-permute-start(bf16[512,128]{1,0:T(8,128)(2,1)S(1)} %get-tuple-element.30), channel_id=1, source_target_pairs={{0,2},{1,3},{2,0},{3,1},{4,6},{5,7},{6,4},{7,5},{8,10},{9,11},{10,... | collective-permute-start | bytes 393224 | tf_op jit(solution)/shard_map/ppermute | solution.py:53
  9.1 11.4 %collective-permute-start.7 = (bf16[1040,128]{1,0:T(8,128)(2,1)S(1)}, bf16[1040,128]{1,0:T(8,128)(2,1)S(1)}, u32[]{:S(2)}, u32[]{:S(2)}) collective-permute-start(bf16[1040,128]{1,0:T(8,128)(2,1)S(1)} %shard_map.38.refs_0_), channel_id=1, source_target_pairs={{0,4},{1,5},{2,6},{3,7},{4,8},{5,9},{6,10},{7,11},{8,12},{9,13},{1... | collective-permute-start | bytes 798728 | tf_op jit(solution)/shard_map/ppermute | solution.py:53
  11.0 10.0 %collective-permute-start.8 = (bf16[1040,128]{1,0:T(8,128)(2,1)S(1)}, bf16[1040,128]{1,0:T(8,128)(2,1)S(1)}, u32[]{:S(2)}, u32[]{:S(2)}) collective-permute-start(bf16[1040,128]{1,0:T(8,128)(2,1)S(1)} %shard_map.38.refs_0_), channel_id=1, source_target_pairs={{0,28},{1,29},{2,30},{3,31},{4,0},{5,1},{6,2},{7,3},{8,4},{9,5},{1... | collective-permute-start | bytes 798728 | tf_op jit(solution)/shard_map/ppermute | solution.py:53
  15.6 14.6 %collective-permute-start.4 = (bf16[512,512]{1,0:T(8,128)(2,1)S(1)}, bf16[512,512]{1,0:T(8,128)(2,1)S(1)}, u32[]{:S(2)}, u32[]{:S(2)}) collective-permute-start(bf16[512,512]{1,0:T(8,128)(2,1)S(1)} %shard_map.40.refs_0_), channel_id=1, source_target_pairs={{0,64},{64,128},{128,192},{192,0},{32,224},{96,32},{160,96},{224,1... | collective-permute-start | bytes 1572872 | tf_op jit(solution)/shard_map/ppermute | solution.py:61
  17.2 13.0 %collective-permute-start.6 = (bf16[512,512]{1,0:T(8,128)(2,1)S(1)}, bf16[512,512]{1,0:T(8,128)(2,1)S(1)}, u32[]{:S(2)}, u32[]{:S(2)}) collective-permute-start(bf16[512,512]{1,0:T(8,128)(2,1)S(1)} %shard_map.40.refs_0_), channel_id=1, source_target_pairs={{0,192},{64,0},{128,64},{192,128},{32,96},{96,160},{160,224},{224,... | collective-permute-start | bytes 1572872 | tf_op jit(solution)/shard_map/ppermute | solution.py:61
  20.5 12.6 %collective-permute-start.11 = (bf16[1040,128]{1,0:T(8,128)(2,1)S(1)}, bf16[1040,128]{1,0:T(8,128)(2,1)S(1)}, u32[]{:S(2)}, u32[]{:S(2)}) collective-permute-start(bf16[1040,128]{1,0:T(8,128)(2,1)S(1)} %collective-permute-done.7.refs_1_), channel_id=1, source_target_pairs={{0,8},{1,9},{2,10},{3,11},{4,12},{5,13},{6,14},{7,15},{8,16},{9,17... | collective-permute-start | bytes 798728 | tf_op jit(solution)/shard_map/ppermute | solution.py:53
  21.0 12.6 %collective-permute-start.10 = (bf16[1040,128]{1,0:T(8,128)(2,1)S(1)}, bf16[1040,128]{1,0:T(8,128)(2,1)S(1)}, u32[]{:S(2)}, u32[]{:S(2)}) collective-permute-start(bf16[1040,128]{1,0:T(8,128)(2,1)S(1)} %collective-permute-done.8.refs_2_), channel_id=1, source_target_pairs={{0,28},{1,29},{2,30},{3,31},{4,0},{5,1},{6,2},{7,3},{8,4},{9,5},{1... | collective-permute-start | bytes 798728 | tf_op jit(solution)/shard_map/ppermute | solution.py:53
  24.1 12.5 %collective-permute-start.9 = (bf16[1040,128]{1,0:T(8,128)(2,1)S(1)}, bf16[1040,128]{1,0:T(8,128)(2,1)S(1)}, u32[]{:S(2)}, u32[]{:S(2)}) collective-permute-start(bf16[1040,128]{1,0:T(8,128)(2,1)S(1)} %collective-permute-done.7.refs_1_), channel_id=1, source_target_pairs={{0,4},{1,5},{2,6},{3,7},{4,8},{5,9},{6,10},{7,11},{8,12},{9,13},{1... | collective-permute-start | bytes 798728 | tf_op jit(solution)/shard_map/ppermute | solution.py:53
  36.7 3.8 %collective-permute-start.12 = (bf16[6,1040,128]{2,1,0:T(8,128)(2,1)S(1)}, bf16[6,1040,128]{2,1,0:T(8,128)(2,1)S(1)}, u32[]{:S(2)}, u32[]{:S(2)}) collective-permute-start(bf16[6,1040,128]{2,1,0:T(8,128)(2,1)S(1)} %shard_map.43.refs_1_), channel_id=1, source_target_pairs={{0,32},{32,0},{1,33},{33,1},{2,34},{34,2},{3,35},{35,3},{4,36},{36... | collective-permute-start | bytes 4792328 | tf_op jit(solution)/shard_map/ppermute | solution.py:65
  36.8 10.2 %collective-permute-start.5 = (bf16[512,512]{1,0:T(8,128)(2,1)S(1)}, bf16[512,512]{1,0:T(8,128)(2,1)S(1)}, u32[]{:S(2)}, u32[]{:S(2)}) collective-permute-start(bf16[512,512]{1,0:T(8,128)(2,1)S(1)} %collective-permute-done.4.refs_2_), channel_id=1, source_target_pairs={{0,64},{64,128},{128,192},{192,0},{32,224},{96,32},{160,96},{224,1... | collective-permute-start | bytes 1572872 | tf_op jit(solution)/shard_map/ppermute | solution.py:61
  38.4 8.6 %collective-permute-start.13 = (bf16[1040,128]{1,0:T(8,128)(2,1)S(1)}, bf16[1040,128]{1,0:T(8,128)(2,1)S(1)}, u32[]{:S(2)}, u32[]{:S(2)}) collective-permute-start(bf16[1040,128]{1,0:T(8,128)(2,1)S(1)} %collective-permute-done.10.refs_4_), channel_id=1, source_target_pairs={{0,28},{1,29},{2,30},{3,31},{4,0},{5,1},{6,2},{7,3},{8,4},{9,5},{1... | collective-permute-start | bytes 798728 | tf_op jit(solution)/shard_map/ppermute | solution.py:53
  40.3 7.9 %collective-permute-start.14 = (bf16[1040,128]{1,0:T(8,128)(2,1)S(1)}, bf16[1040,128]{1,0:T(8,128)(2,1)S(1)}, u32[]{:S(2)}, u32[]{:S(2)}) collective-permute-start(bf16[1040,128]{1,0:T(8,128)(2,1)S(1)} %collective-permute-done.11.refs_5_), channel_id=1, source_target_pairs={{0,4},{1,5},{2,6},{3,7},{4,8},{5,9},{6,10},{7,11},{8,12},{9,13},{1... | collective-permute-start | bytes 798728 | tf_op jit(solution)/shard_map/ppermute | solution.py:53
  48.2 2.0 %collective-permute-start.15 = (bf16[2,1040,128]{2,1,0:T(8,128)(2,1)S(1)}, bf16[2,1040,128]{2,1,0:T(8,128)(2,1)S(1)}, u32[]{:S(2)}, u32[]{:S(2)}) collective-permute-start(bf16[2,1040,128]{2,1,0:T(8,128)(2,1)S(1)} %shard_map.45.refs_3_), channel_id=1, source_target_pairs={{0,32},{32,0},{1,33},{33,1},{2,34},{34,2},{3,35},{35,3},{4,36},{36... | collective-permute-start | bytes 1597448 | tf_op jit(solution)/shard_map/ppermute | solution.py:65
  52.8 12.9 %collective-permute-start.17 = (s16[2064,128]{1,0:T(8,128)(2,1)S(1)}, s16[2064,128]{1,0:T(8,128)(2,1)S(1)}, u32[]{:S(2)}, u32[]{:S(2)}) collective-permute-start(s16[2064,128]{1,0:T(8,128)(2,1)S(1)} %shard_map.48), channel_id=1, source_target_pairs={{0,1},{1,2},{2,3},{3,0},{4,5},{5,6},{6,7},{7,4},{8,9},{9,10},{10,1... | collective-permute-start | bytes 1585160 | tf_op jit(solution)/shard_map/ppermute | solution.py:53
  56.1 12.6 %collective-permute-start.16 = (s16[2064,128]{1,0:T(8,128)(2,1)S(1)}, s16[2064,128]{1,0:T(8,128)(2,1)S(1)}, u32[]{:S(2)}, u32[]{:S(2)}) collective-permute-start(s16[2064,128]{1,0:T(8,128)(2,1)S(1)} %get-tuple-element.37), channel_id=1, source_target_pairs={{0,3},{1,0},{2,1},{3,2},{4,7},{5,4},{6,5},{7,6},{8,11},{9,8},{10,9... | collective-permute-start | bytes 1585160 | tf_op jit(solution)/shard_map/ppermute | solution.py:53
  66.3 10.5 %collective-permute-start.18 = (s16[2064,128]{1,0:T(8,128)(2,1)S(1)}, s16[2064,128]{1,0:T(8,128)(2,1)S(1)}, u32[]{:S(2)}, u32[]{:S(2)}) collective-permute-start(s16[2064,128]{1,0:T(8,128)(2,1)S(1)} %shard_map.49), channel_id=1, source_target_pairs={{0,1},{1,2},{2,3},{3,0},{4,5},{5,6},{6,7},{7,4},{8,9},{9,10},{10,1... | collective-permute-start | bytes 1585160 | tf_op jit(solution)/shard_map/ppermute | solution.py:53
  77.4 1.2 %collective-permute-start.19 = (f32[1,128]{1,0:T(1,128)S(1)}, f32[1,128]{1,0:T(1,128)S(1)}, u32[]{:S(2)}, u32[]{:S(2)}) collective-permute-start(f32[1,128]{1,0:T(1,128)S(1)} %get-tuple-element.41), channel_id=1, source_target_pairs={{0,32},{32,0},{1,33},{33,1},{2,34},{34,2},{3,35},{35,3},{4,36},{36... | collective-permute-start | bytes 1544 | tf_op jit(solution)/shard_map/ppermute | solution.py:65
  78.6 8.3 %collective-permute-start.20 = (f32[1024,128]{1,0:T(8,128)S(1)}, f32[1024,128]{1,0:T(8,128)S(1)}, u32[]{:S(2)}, u32[]{:S(2)}) collective-permute-start(f32[1024,128]{1,0:T(8,128)S(1)} %get-tuple-element.42), channel_id=1, source_target_pairs={{0,32},{32,0},{1,33},{33,1},{2,34},{34,2},{3,35},{35,3},{4,36},{36... | collective-permute-start | bytes 1572872 | tf_op jit(solution)/shard_map/ppermute | solution.py:65
  78.8 4.5 %collective-permute-start.21 = (f32[2,128]{1,0:T(2,128)S(1)}, f32[2,128]{1,0:T(2,128)S(1)}, u32[]{:S(2)}, u32[]{:S(2)}) collective-permute-start(f32[2,128]{1,0:T(2,128)S(1)} %pad_maximum_fusion.refs_0_), channel_id=1, source_target_pairs={{0,64},{64,128},{128,192},{192,0},{32,224},{96,32},{160,96},{224,1... | collective-permute-start | bytes 3080 | tf_op jit(solution)/shard_map/ppermute | solution.py:61
  81.8 3.6 %collective-permute-start.22 = (f32[2,128]{1,0:T(2,128)S(1)}, f32[2,128]{1,0:T(2,128)S(1)}, u32[]{:S(2)}, u32[]{:S(2)}) collective-permute-start(f32[2,128]{1,0:T(2,128)S(1)} %pad_maximum_fusion.refs_0_), channel_id=1, source_target_pairs={{0,192},{64,0},{128,64},{192,128},{32,96},{96,160},{160,224},{224,... | collective-permute-start | bytes 3080 | tf_op jit(solution)/shard_map/ppermute | solution.py:61
  81.8 5.1 %collective-permute-start.23 = (f32[2,128]{1,0:T(2,128)S(1)}, f32[2,128]{1,0:T(2,128)S(1)}, u32[]{:S(2)}, u32[]{:S(2)}) collective-permute-start(f32[2,128]{1,0:T(2,128)S(1)} %pad_maximum_fusion.refs_0_), channel_id=1, source_target_pairs={{0,128},{64,192},{128,0},{192,64},{32,160},{96,224},{160,32},{224,... | collective-permute-start | bytes 3080 | tf_op jit(solution)/shard_map/ppermute | solution.py:61

commit v5 on v4

--- a/solution.py
+++ b/solution.py
@@ -15,7 +15,7 @@
 ROWS = 2048
 LEVELS = 65535
 FINE = 64
-BATCH = 4
+BATCH = 8
 PIECES = 4
 MIB = 1024 * 1024
 VMEM = pl.BlockSpec(memory_space=pltpu.VMEM)
@@ -196,28 +196,27 @@
             return carry
 
         lax.fori_loop(0, (count + BATCH - 1) // BATCH, step, 0)
-    for i, (coded, out_ref) in enumerate(zip(outs, out_refs)):
-        part = slice(i * TILE, (i + 1) * TILE)
-        if coded:
-            encode(total_ref, part, out_ref)
-        elif len(outs) == 1:
+    for out, out_ref in zip(outs, out_refs):
+        if out is None:
             out_ref[...] = total_ref[...]
+        elif isinstance(out, int):
+            out_ref[...] = total_ref[:, out * TILE : (out + 1) * TILE]
         else:
-            out_ref[...] = total_ref[:, part]
-
-
-def product(b_panels, parts, plan, total=None, slots=(0, 1, 2, 3), outs=(False,)):
+            slot, start, _ = out
+            encode(total_ref, slice(slot * TILE, (slot + 1) * TILE), out_ref, start)
+
+
+def product(b_panels, parts, plan, total=None, slots=(0, 1, 2, 3), outs=(None,)):
     cols = len(slots) * TILE
     count = sum(len(steps) for _, _, steps in plan)
     flops = sum(p.size for p in parts) * cols * 2
-    width = cols // len(outs)
     return call(
         functools.partial(product_kernel, tuple(plan), slots, outs),
         [
-            struct((ROWS + HEAD, TILE), jnp.int16)
-            if coded
-            else struct((ROWS + TILE, width), jnp.float32)
-            for coded in outs
+            struct((out[2] + HEAD, TILE), jnp.int16)
+            if isinstance(out, tuple)
+            else struct((ROWS + TILE, cols if out is None else TILE), jnp.float32)
+            for out in outs
         ],
         b_panels,
         *parts,
@@ -234,61 +233,72 @@
     )
 
 
-def encode(total_ref, lanes, out_ref):
-    top = total_ref[:TILE, lanes]
-    for i in range(1, ROWS // TILE):
-        top = jnp.maximum(top, total_ref[i * TILE : (i + 1) * TILE, lanes])
+def encode(total_ref, lanes, out_ref, start):
+    rows = out_ref.shape[0] - HEAD
+    top = total_ref[start : start + TILE, lanes]
+    for i in range(TILE, rows, TILE):
+        top = jnp.maximum(top, total_ref[start + i : start + i + TILE, lanes])
     top = jnp.maximum(jnp.max(top, axis=0, keepdims=True), jnp.float32(2.0**-100))
     exponent = jnp.ceil(jnp.log2(top) * FINE)
     inverse = LEVELS * jnp.exp2(exponent * (-1.0 / FINE))
-    for i in range(ROWS // TILE):
-        part = slice(i * TILE, (i + 1) * TILE)
-        steps = jnp.minimum(total_ref[part, lanes] * inverse + 0.5, jnp.float32(LEVELS))
-        out_ref[part, :] = (steps.astype(jnp.int32) - 32768).astype(jnp.int16)
+    for i in range(0, rows, TILE):
+        sums = total_ref[start + i : start + i + TILE, lanes]
+        steps = jnp.minimum(sums * inverse + 0.5, jnp.float32(LEVELS))
+        out_ref[i : i + TILE, :] = (steps.astype(jnp.int32) - 32768).astype(jnp.int16)
     exponent = jnp.broadcast_to(exponent, (HEAD, TILE)).astype(jnp.int32)
-    out_ref[ROWS:, :] = exponent.astype(jnp.int16)
+    out_ref[rows:, :] = exponent.astype(jnp.int16)
 
 
 def scale_of(ref):
-    exponent = ref[ROWS:, :].astype(jnp.int32).astype(jnp.float32)[0:1, :]
+    exponent = ref[ref.shape[0] - HEAD :, :].astype(jnp.int32).astype(jnp.float32)[0:1, :]
     return jnp.exp2(exponent * (1.0 / FINE)) * jnp.float32(1.0 / LEVELS)
 
 
-def decode(ref, part, scale):
-    return (ref[part, :].astype(jnp.int32) + 32768).astype(jnp.float32) * scale
-
-
-def relay_kernel(total_ref, recv_ref, out_ref, sum_ref):
+def decode(ref, start, scale):
+    steps = ref[start : start + TILE, :].astype(jnp.int32) + 32768
+    return steps.astype(jnp.float32) * scale
+
+
+def relay_kernel(start, total_ref, recv_ref, out_ref, sum_ref):
     scale = scale_of(recv_ref)
-    for i in range(ROWS // TILE):
-        part = slice(i * TILE, (i + 1) * TILE)
-        sum_ref[part, :] = total_ref[part, :] + decode(recv_ref, part, scale)
-    encode(sum_ref, slice(0, TILE), out_ref)
-
-
-def square_kernel(weight, total_ref, *refs):
-    recv, (keep_ref, send_ref, sum_ref) = refs[:2], refs[2:]
+    for i in range(0, ROWS // 2, TILE):
+        sum_ref[i : i + TILE, :] = total_ref[start + i : start + i + TILE, :] + decode(
+            recv_ref, i, scale
+        )
+    encode(sum_ref, slice(0, TILE), out_ref, 0)
+
+
+def relay(side, passed, start):
+    return call(
+        functools.partial(relay_kernel, start),
+        struct(passed.shape, jnp.int16),
+        side,
+        passed,
+        scratch_shapes=[pltpu.VMEM((ROWS // 2, TILE), jnp.float32)],
+    )
+
+
+def square_kernel(weight, total_ref, whole_ref, low_ref, high_ref, keep_ref, send_ref, sum_ref):
     core = lax.axis_index("col")
     first_col = lax.axis_index("layer") * 2 * TILE + core * TILE
-    scales = [scale_of(ref) for ref in recv]
+    whole_scale, scales = scale_of(whole_ref), [scale_of(ref) for ref in (low_ref, high_ref)]
     row = lax.broadcasted_iota(jnp.int32, (TILE, TILE), 0)
     col = lax.broadcasted_iota(jnp.int32, (TILE, TILE), 1)
     column = jnp.zeros((TILE, TILE), jnp.float32)
     half = ROWS // 2
-    for i in range(half // TILE):
-        for own, out_ref in ((1, keep_ref), (0, send_ref)):
-            start = (core if own else 1 - core) * half + i * TILE
-            part = pl.ds(pl.multiple_of(start, TILE), TILE)
-            first_row = lax.axis_index("row") * ROWS + start
+    for i in range(0, half, TILE):
+        powers = []
+        for start, ref, scale in ((0, low_ref, scales[0]), (half, high_ref, scales[1])):
+            first_row = lax.axis_index("row") * ROWS + start + i
             diagonal = row + (first_row - first_col) == col
-            expanded = total_ref[part, :] + jnp.where(
+            expanded = total_ref[start + i : start + i + TILE, :] + jnp.where(
                 diagonal, jnp.float32(weight), jnp.float32(0)
             )
-            for ref, scale in zip(recv, scales):
-                expanded += decode(ref, part, scale)
-            power = expanded * expanded
-            out_ref[i * TILE : (i + 1) * TILE, :] = power
-            column += power
+            expanded += decode(whole_ref, start + i, whole_scale) + decode(ref, i, scale)
+            powers.append(expanded * expanded)
+            column += powers[-1]
+        keep_ref[i : i + TILE, :] = jnp.where(core == 0, powers[0], powers[1])
+        send_ref[i : i + TILE, :] = jnp.where(core == 0, powers[1], powers[0])
     sum_ref[...] = jnp.sum(column, axis=0, keepdims=True)
 
 
@@ -368,18 +378,12 @@
         total,
     )
 
-    (code,) = rest(slots=(3,), outs=(True,))
-    passed = hop(code, 0, 1)
-    code, side = rest(slots=(1, 2), outs=(True, False))
+    low, high = rest(slots=(3,), outs=((0, 0, half), (0, half, half)))
+    low, high = hop(low, 0, 1), hop(high, 0, 1)
+    code, side = rest(slots=(1, 2), outs=((0, 0, ROWS), 1))
     sums = [hop(code, 0, -1)]
-    code = call(
-        relay_kernel,
-        struct((ROWS + HEAD, TILE), jnp.int16),
-        side,
-        passed,
-        scratch_shapes=[pltpu.VMEM((ROWS, TILE), jnp.float32)],
-    )
-    sums.append(hop(code, 0, 1))
+    sums.append(hop(relay(side, low, 0), 0, 1))
+    sums.append(hop(relay(side, high, half), 0, 1))
     (own,) = rest(slots=(0,))
     keep, send, column = call(
         functools.partial(square_kernel, n_total / 32),

time: 88.5 us -> 86.1 us (0.973)
  waiting for transfers between devices: 40.8 us -> 37.9 us
  Pallas kernels: 14.9 us -> 16.3 us
  starting transfers between devices: 29.3 us -> 28.3 us
    ppermute x13 -> x15, waiting for transfers between devices: 28.2 us -> 25.3 us  [hop(): return lax.ppermute(x, ('col', 'layer'), pairs)]
    pallas_call x14 -> x15, Pallas kernels: 13.8 us -> 15.2 us  [call(): pl.pallas_call(kernel, out_shape=out_shape, in_specs=[first] + [VMEM] * (...]
    ppermute x6, starting transfers between devices: 8.16 us -> 7.18 us  [hop_x(): return lax.ppermute(x, ('row', 'col'), pairs)]
    ppermute x13 -> x15, starting transfers between devices: 20.6 us -> 20.5 us  [hop(): return lax.ppermute(x, ('col', 'layer'), pairs)]
  transfers between devices with their start and end apart: 24 -> 26, of which waited for: 14 -> 17; matrix products, arithmetic and copies ran while one was open for 0% -> 0% of each run, Pallas kernels for 12% -> 13%
where the time goes in v5:
time: 86.1 us; the launch traced here: 85.6 us
  waiting for transfers between devices  37.9 us (44%)
  starting transfers between devices  28.3 us (33%)
  Pallas kernels  16.3 us (19%)
  local copies, waits for them, and re-layouts  2.73 us (3%)
    ppermute x15, waiting for transfers between devices, hop(): return lax.ppermute(x, ('col', 'layer'), pairs)  25.3 us
    ppermute x15, starting transfers between devices, hop(): return lax.ppermute(x, ('col', 'layer'), pairs)  20.5 us
    pallas_call x15, Pallas kernels, call(): pl.pallas_call(kernel, out_shape=out_shape, in_specs=[first] + [VMEM] * (...  15.2 us
    ppermute x6, waiting for transfers between devices, hop_x(): return lax.ppermute(x, ('row', 'col'), pairs)  9.63 us
    ppermute x6, starting transfers between devices, hop_x(): return lax.ppermute(x, ('row', 'col'), pairs)  7.18 us
    ppermute x5, waiting for transfers between devices, swap(): return lax.ppermute(x, 'col', [(0, 1), (1, 0)])  2.98 us
    unnamed x6, local copies, waits for them, and re-layouts  2.73 us
  transfers between devices with their start and end apart: 26, of which 17 were waited for; matrix products, arithmetic and copies ran while one was open for 0% of the time, Pallas kernels for 13%

profile of v5, /device:TPU:2, one launch (start us, length us, event | category | flops | bytes accessed | tf_op | source)
XLA Modules:
  0.0 85.6 jit_solution(6764728410349924207)
XLA Ops:
  0.0 1.0 %copy-done = bf16[1024,256]{1,0:T(8,128)(2,1)S(1)} copy-done((bf16[1024,256]{1,0:T(8,128)(2,1)S(1)}, bf16[1024,256]{1,0:T(8,128)(2,1)}, u32[]{:S(2)}) %copy-start) | copy-done | bytes 524312
  1.3 1.0 %copy-done.1 = bf16[2048,128]{1,0:T(8,128)(2,1)S(1)} copy-done((bf16[2048,128]{1,0:T(8,128)(2,1)S(1)}, bf16[2048,128]{1,0:T(8,128)(2,1)}, u32[]{:S(2)}) %copy-start.1) | copy-done | bytes 524312
  3.8 1.7 %collective-permute-start.1 = (bf16[512,128]{1,0:T(8,128)(2,1)S(1)}, bf16[512,128]{1,0:T(8,128)(2,1)S(1)}, u32[]{:S(2)}, u32[]{:S(2)}) collective-permute-start(bf16[512,128]{1,0:T(8,128)(2,1)S(1)} %get-tuple-element.30), channel_id=1, source_target_pairs={{0,1},{1,2},{2,3},{3,0},{4,5},{5,6},{6,7},{7,4},{8,9},{9,10},{10,1... | collective-permute-start | bytes 393224 | tf_op jit(solution)/shard_map/ppermute | solution.py:53
  5.5 1.7 %collective-permute-start.2 = (bf16[512,128]{1,0:T(8,128)(2,1)S(1)}, bf16[512,128]{1,0:T(8,128)(2,1)S(1)}, u32[]{:S(2)}, u32[]{:S(2)}) collective-permute-start(bf16[512,128]{1,0:T(8,128)(2,1)S(1)} %get-tuple-element.31), channel_id=1, source_target_pairs={{0,3},{1,0},{2,1},{3,2},{4,7},{5,4},{6,5},{7,6},{8,11},{9,8},{10,9... | collective-permute-start | bytes 393224 | tf_op jit(solution)/shard_map/ppermute | solution.py:53
  7.1 2.0 %collective-permute-start.3 = (bf16[512,128]{1,0:T(8,128)(2,1)S(1)}, bf16[512,128]{1,0:T(8,128)(2,1)S(1)}, u32[]{:S(2)}, u32[]{:S(2)}) collective-permute-start(bf16[512,128]{1,0:T(8,128)(2,1)S(1)} %get-tuple-element.32), channel_id=1, source_target_pairs={{0,2},{1,3},{2,0},{3,1},{4,6},{5,7},{6,4},{7,5},{8,10},{9,11},{10,... | collective-permute-start | bytes 393224 | tf_op jit(solution)/shard_map/ppermute | solution.py:53
  9.1 1.9 %collective-permute-start.7 = (bf16[1040,128]{1,0:T(8,128)(2,1)S(1)}, bf16[1040,128]{1,0:T(8,128)(2,1)S(1)}, u32[]{:S(2)}, u32[]{:S(2)}) collective-permute-start(bf16[1040,128]{1,0:T(8,128)(2,1)S(1)} %shard_map.38.refs_0_), channel_id=1, source_target_pairs={{0,4},{1,5},{2,6},{3,7},{4,8},{5,9},{6,10},{7,11},{8,12},{9,13},{1... | collective-permute-start | bytes 798728 | tf_op jit(solution)/shard_map/ppermute | solution.py:53
  11.0 3.9 %collective-permute-start.8 = (bf16[1040,128]{1,0:T(8,128)(2,1)S(1)}, bf16[1040,128]{1,0:T(8,128)(2,1)S(1)}, u32[]{:S(2)}, u32[]{:S(2)}) collective-permute-start(bf16[1040,128]{1,0:T(8,128)(2,1)S(1)} %shard_map.38.refs_0_), channel_id=1, source_target_pairs={{0,28},{1,29},{2,30},{3,31},{4,0},{5,1},{6,2},{7,3},{8,4},{9,5},{1... | collective-permute-start | bytes 798728 | tf_op jit(solution)/shard_map/ppermute | solution.py:53
  15.6 1.6 %collective-permute-start.4 = (bf16[512,512]{1,0:T(8,128)(2,1)S(1)}, bf16[512,512]{1,0:T(8,128)(2,1)S(1)}, u32[]{:S(2)}, u32[]{:S(2)}) collective-permute-start(bf16[512,512]{1,0:T(8,128)(2,1)S(1)} %shard_map.40.refs_0_), channel_id=1, source_target_pairs={{0,64},{64,128},{128,192},{192,0},{32,224},{96,32},{160,96},{224,1... | collective-permute-start | bytes 1572872 | tf_op jit(solution)/shard_map/ppermute | solution.py:61
  17.7 2.8 %collective-permute-done.7.refs_1_ = bf16[1040,128]{1,0:T(8,128)(2,1)S(1)} collective-permute-done((bf16[1040,128]{1,0:T(8,128)(2,1)S(1)}, bf16[1040,128]{1,0:T(8,128)(2,1)S(1)}, u32[]{:S(2)}, u32[]{:S(2)}) %collective-permute-start.7) | collective-permute-done | bytes 266272 | tf_op jit(solution)/shard_map/ppermute | solution.py:53
  21.0 3.1 %collective-permute-start.10 = (bf16[1040,128]{1,0:T(8,128)(2,1)S(1)}, bf16[1040,128]{1,0:T(8,128)(2,1)S(1)}, u32[]{:S(2)}, u32[]{:S(2)}) collective-permute-start(bf16[1040,128]{1,0:T(8,128)(2,1)S(1)} %collective-permute-done.8.refs_2_), channel_id=1, source_target_pairs={{0,28},{1,29},{2,30},{3,31},{4,0},{5,1},{6,2},{7,3},{8,4},{9,5},{1... | collective-permute-start | bytes 798728 | tf_op jit(solution)/shard_map/ppermute | solution.py:53
  24.1 6.0 %collective-permute-done.4.refs_2_ = bf16[512,512]{1,0:T(8,128)(2,1)S(1)} collective-permute-done((bf16[512,512]{1,0:T(8,128)(2,1)S(1)}, bf16[512,512]{1,0:T(8,128)(2,1)S(1)}, u32[]{:S(2)}, u32[]{:S(2)}) %collective-permute-start.4) | collective-permute-done | bytes 524320 | tf_op jit(solution)/shard_map/ppermute | solution.py:61
  30.2 3.0 %collective-permute-done.11.refs_5_ = bf16[1040,128]{1,0:T(8,128)(2,1)S(1)} collective-permute-done((bf16[1040,128]{1,0:T(8,128)(2,1)S(1)}, bf16[1040,128]{1,0:T(8,128)(2,1)S(1)}, u32[]{:S(2)}, u32[]{:S(2)}) %collective-permute-start.11) | collective-permute-done | bytes 266272 | tf_op jit(solution)/shard_map/ppermute | solution.py:53
  33.6 3.0 %collective-permute-done.9.refs_3_ = bf16[1040,128]{1,0:T(8,128)(2,1)S(1)} collective-permute-done((bf16[1040,128]{1,0:T(8,128)(2,1)S(1)}, bf16[1040,128]{1,0:T(8,128)(2,1)S(1)}, u32[]{:S(2)}, u32[]{:S(2)}) %collective-permute-start.9) | collective-permute-done | bytes 266272 | tf_op jit(solution)/shard_map/ppermute | solution.py:53
  36.8 1.6 %collective-permute-start.5 = (bf16[512,512]{1,0:T(8,128)(2,1)S(1)}, bf16[512,512]{1,0:T(8,128)(2,1)S(1)}, u32[]{:S(2)}, u32[]{:S(2)}) collective-permute-start(bf16[512,512]{1,0:T(8,128)(2,1)S(1)} %collective-permute-done.4.refs_2_), channel_id=1, source_target_pairs={{0,64},{64,128},{128,192},{192,0},{32,224},{96,32},{160,96},{224,1... | collective-permute-start | bytes 1572872 | tf_op jit(solution)/shard_map/ppermute | solution.py:61
  38.4 1.9 %collective-permute-start.13 = (bf16[1040,128]{1,0:T(8,128)(2,1)S(1)}, bf16[1040,128]{1,0:T(8,128)(2,1)S(1)}, u32[]{:S(2)}, u32[]{:S(2)}) collective-permute-start(bf16[1040,128]{1,0:T(8,128)(2,1)S(1)} %collective-permute-done.10.refs_4_), channel_id=1, source_target_pairs={{0,28},{1,29},{2,30},{3,31},{4,0},{5,1},{6,2},{7,3},{8,4},{9,5},{1... | collective-permute-start | bytes 798728 | tf_op jit(solution)/shard_map/ppermute | solution.py:53
  40.5 3.3 %shard_map.44.refs_5_ = f32[2176,512]{1,0:T(8,128)S(1)} custom-call(bf16[4,512,512]{2,1,0:T(8,128)(2,1)S(1)} %shard_map.41.refs_1_.refs_0_, bf16[6,1040,128]{2,1,0:T(8,128)(2,1)S(1)} %shard_map.43.refs_1_, bf16[6,1040,128]{2,1,0:T(8,128)(2,1)S(1)} %collective-permute-done.12.refs_2_), custom_call_target="tpu_custom_call" | custom-call | flops 1635778560 | bytes 12779520 | tf_op jit(solution)/shard_map/pallas_call | solution.py:31
  43.8 3.2 %collective-permute-done.13.refs_0_ = bf16[1040,128]{1,0:T(8,128)(2,1)S(1)} collective-permute-done((bf16[1040,128]{1,0:T(8,128)(2,1)S(1)}, bf16[1040,128]{1,0:T(8,128)(2,1)S(1)}, u32[]{:S(2)}, u32[]{:S(2)}) %collective-permute-start.13) | collective-permute-done | bytes 266272 | tf_op jit(solution)/shard_map/ppermute | solution.py:53
  47.0 1.2 %collective-permute-done.14.refs_1_ = bf16[1040,128]{1,0:T(8,128)(2,1)S(1)} collective-permute-done((bf16[1040,128]{1,0:T(8,128)(2,1)S(1)}, bf16[1040,128]{1,0:T(8,128)(2,1)S(1)}, u32[]{:S(2)}, u32[]{:S(2)}) %collective-permute-start.14) | collective-permute-done | bytes 266272 | tf_op jit(solution)/shard_map/ppermute | solution.py:53
  48.4 1.9 %collective-permute-done.15.refs_4_ = bf16[2,1040,128]{2,1,0:T(8,128)(2,1)S(1)} collective-permute-done((bf16[2,1040,128]{2,1,0:T(8,128)(2,1)S(1)}, bf16[2,1040,128]{2,1,0:T(8,128)(2,1)S(1)}, u32[]{:S(2)}, u32[]{:S(2)}) %collective-permute-start.15) | collective-permute-done | bytes 532512 | tf_op jit(solution)/shard_map/ppermute | solution.py:65
  50.3 3.0 %shard_map.48 = (s16[1040,128]{1,0:T(8,128)(2,1)S(1)}, s16[1040,128]{1,0:T(8,128)(2,1)S(1)}) custom-call(bf16[4,512,512]{2,1,0:T(8,128)(2,1)S(1)} %shard_map.42.refs_0_, bf16[6,1040,128]{2,1,0:T(8,128)(2,1)S(1)} %shard_map.43.refs_1_, bf16[6,1040,128]{2,1,0:T(8,128)(2,1)S(1)} %collective-permute-done.12.refs_2_, ...), custom_call_target="tpu_custom_call" | custom-call | flops 545259520 | bytes 4259840 | tf_op jit(solution)/shard_map/pallas_call | solution.py:31
  54.1 3.4 %shard_map.47 = (s16[2064,128]{1,0:T(8,128)(2,1)S(1)}, f32[2176,128]{1,0:T(8,128)S(1)}) custom-call(bf16[4,512,512]{2,1,0:T(8,128)(2,1)S(1)} %shard_map.42.refs_0_, bf16[6,1040,128]{2,1,0:T(8,128)(2,1)S(1)} %shard_map.43.refs_1_, bf16[6,1040,128]{2,1,0:T(8,128)(2,1)S(1)} %collective-permute-done.12.refs_2_, bf16[2,1040,128]{2,1,0:T(8,128)(2,1)S(1)} %shard_map.45.refs_3_, ...), custom_call_target="tpu_custom_call" | custom-call | flops 1090519040 | bytes 8519680 | tf_op jit(solution)/shard_map/pallas_call | solution.py:31
  57.5 2.8 %collective-permute-start.16 = (s16[2064,128]{1,0:T(8,128)(2,1)S(1)}, s16[2064,128]{1,0:T(8,128)(2,1)S(1)}, u32[]{:S(2)}, u32[]{:S(2)}) collective-permute-start(s16[2064,128]{1,0:T(8,128)(2,1)S(1)} %get-tuple-element.39), channel_id=1, source_target_pairs={{0,3},{1,0},{2,1},{3,2},{4,7},{5,4},{6,5},{7,6},{8,11},{9,8},{10,9... | collective-permute-start | bytes 1585160 | tf_op jit(solution)/shard_map/ppermute | solution.py:53
  61.4 4.9 %collective-permute-done.17.recv_ref = s16[1040,128]{1,0:T(8,128)(2,1)S(1)} collective-permute-done((s16[1040,128]{1,0:T(8,128)(2,1)S(1)}, s16[1040,128]{1,0:T(8,128)(2,1)S(1)}, u32[]{:S(2)}, u32[]{:S(2)}) %collective-permute-start.17) | collective-permute-done | bytes 266272 | tf_op jit(solution)/shard_map/ppermute | solution.py:53
  66.6 3.0 %shard_map.46.total_ref = f32[2176,128]{1,0:T(8,128)S(1)} custom-call(bf16[4,512,512]{2,1,0:T(8,128)(2,1)S(1)} %shard_map.42.refs_0_, bf16[6,1040,128]{2,1,0:T(8,128)(2,1)S(1)} %shard_map.43.refs_1_, bf16[6,1040,128]{2,1,0:T(8,128)(2,1)S(1)} %collective-permute-done.12.refs_2_, bf16[2,1040,128]{2,1,0:T(8,128)(2,1)S(1)} %shard_map.45.refs_3_, ...), custom_call_target="tpu_custom_call" | custom-call | flops 545259520 | bytes 4259840 | tf_op jit(solution)/shard_map/pallas_call | solution.py:31
  69.6 3.0 %collective-permute-done.16.whole_ref = s16[2064,128]{1,0:T(8,128)(2,1)S(1)} collective-permute-done((s16[2064,128]{1,0:T(8,128)(2,1)S(1)}, s16[2064,128]{1,0:T(8,128)(2,1)S(1)}, u32[]{:S(2)}, u32[]{:S(2)}) %collective-permute-start.16) | collective-permute-done | bytes 528416 | tf_op jit(solution)/shard_map/ppermute | solution.py:53
  72.6 2.6 %collective-permute-done.18.low_ref = s16[1040,128]{1,0:T(8,128)(2,1)S(1)} collective-permute-done((s16[1040,128]{1,0:T(8,128)(2,1)S(1)}, s16[1040,128]{1,0:T(8,128)(2,1)S(1)}, u32[]{:S(2)}, u32[]{:S(2)}) %collective-permute-start.18) | collective-permute-done | bytes 266272 | tf_op jit(solution)/shard_map/ppermute | solution.py:53
  75.9 1.1 %collective-permute-done.21 = f32[1,128]{1,0:T(1,128)S(1)} collective-permute-done((f32[1,128]{1,0:T(1,128)S(1)}, f32[1,128]{1,0:T(1,128)S(1)}, u32[]{:S(2)}, u32[]{:S(2)}) %collective-permute-start.21) | collective-permute-done | bytes 544 | tf_op jit(solution)/shard_map/ppermute | solution.py:65
  77.2 1.8 %collective-permute-start.23 = (f32[2,128]{1,0:T(2,128)S(1)}, f32[2,128]{1,0:T(2,128)S(1)}, u32[]{:S(2)}, u32[]{:S(2)}) collective-permute-start(f32[2,128]{1,0:T(2,128)S(1)} %pad_maximum_fusion.refs_0_), channel_id=1, source_target_pairs={{0,64},{64,128},{128,192},{192,0},{32,224},{96,32},{160,96},{224,1... | collective-permute-start | bytes 3080 | tf_op jit(solution)/shard_map/ppermute | solution.py:61
  79.3 1.5 %collective-permute-start.25 = (f32[2,128]{1,0:T(2,128)S(1)}, f32[2,128]{1,0:T(2,128)S(1)}, u32[]{:S(2)}, u32[]{:S(2)}) collective-permute-start(f32[2,128]{1,0:T(2,128)S(1)} %pad_maximum_fusion.refs_0_), channel_id=1, source_target_pairs={{0,128},{64,192},{128,0},{192,64},{32,160},{96,224},{160,32},{224,... | collective-permute-start | bytes 3080 | tf_op jit(solution)/shard_map/ppermute | solution.py:61
  80.8 1.8 %collective-permute-done.24.refs_2_ = f32[2,128]{1,0:T(2,128)S(1)} collective-permute-done((f32[2,128]{1,0:T(2,128)S(1)}, f32[2,128]{1,0:T(2,128)S(1)}, u32[]{:S(2)}, u32[]{:S(2)}) %collective-permute-start.24) | collective-permute-done | bytes 1056 | tf_op jit(solution)/shard_map/ppermute | solution.py:61
  82.6 1.7 %collective-permute-done.25.refs_3_ = f32[2,128]{1,0:T(2,128)S(1)} collective-permute-done((f32[2,128]{1,0:T(2,128)S(1)}, f32[2,128]{1,0:T(2,128)S(1)}, u32[]{:S(2)}, u32[]{:S(2)}) %collective-permute-start.25) | collective-permute-done | bytes 1056 | tf_op jit(solution)/shard_map/ppermute | solution.py:61
  84.4 1.0 %shard_map.52 = f32[1024,256]{1,0:T(8,128)} custom-call(f32[1024,128]{1,0:T(8,128)S(1)} %get-tuple-element.43.keep_ref, f32[1024,128]{1,0:T(8,128)S(1)} %collective-permute-done.22.recv_ref, f32[2,128]{1,0:T(2,128)S(1)} %pad_maximum_fusion.refs_0_, f32[2,128]{1,0:T(2,128)S(1)} %collective-permute-done.23.refs_1_, ...), custom_call_target="tpu_custom_call" | custom-call | tf_op jit(solution)/shard_map/pallas_call | solution.py:329
  (43 shorter events, 7.9 us)
Async XLA Ops:
  0.0 1.0 %copy-start = (bf16[1024,256]{1,0:T(8,128)(2,1)S(1)}, bf16[1024,256]{1,0:T(8,128)(2,1)}, u32[]{:S(2)}) copy-start(bf16[1024,256]{1,0:T(8,128)(2,1)} %b_ref.1) | copy-start | bytes 1572868
  1.2 2.6 %collective-permute-start = (bf16[1024,128]{1,0:T(8,128)(2,1)S(1)}, bf16[1024,128]{1,0:T(8,128)(2,1)S(1)}, u32[]{:S(2)}, u32[]{:S(2)}) collective-permute-start(bf16[1024,128]{1,0:T(8,128)(2,1)S(1)} %get-tuple-element.28), channel_id=1, source_target_pairs={{0,32},{32,0},{1,33},{33,1},{2,34},{34,2},{3,35},{35,3},{4,36},{36... | collective-permute-start | bytes 786440 | tf_op jit(solution)/shard_map/ppermute | solution.py:65
  1.3 1.0 %copy-start.1 = (bf16[2048,128]{1,0:T(8,128)(2,1)S(1)}, bf16[2048,128]{1,0:T(8,128)(2,1)}, u32[]{:S(2)}) copy-start(bf16[2048,128]{1,0:T(8,128)(2,1)} %a_ref.1) | copy-start | bytes 1572868
  2.3 0.7 copy-start.2
  3.8 11.2 %collective-permute-start.1 = (bf16[512,128]{1,0:T(8,128)(2,1)S(1)}, bf16[512,128]{1,0:T(8,128)(2,1)S(1)}, u32[]{:S(2)}, u32[]{:S(2)}) collective-permute-start(bf16[512,128]{1,0:T(8,128)(2,1)S(1)} %get-tuple-element.30), channel_id=1, source_target_pairs={{0,1},{1,2},{2,3},{3,0},{4,5},{5,6},{6,7},{7,4},{8,9},{9,10},{10,1... | collective-permute-start | bytes 393224 | tf_op jit(solution)/shard_map/ppermute | solution.py:53
  5.5 9.5 %collective-permute-start.2 = (bf16[512,128]{1,0:T(8,128)(2,1)S(1)}, bf16[512,128]{1,0:T(8,128)(2,1)S(1)}, u32[]{:S(2)}, u32[]{:S(2)}) collective-permute-start(bf16[512,128]{1,0:T(8,128)(2,1)S(1)} %get-tuple-element.31), channel_id=1, source_target_pairs={{0,3},{1,0},{2,1},{3,2},{4,7},{5,4},{6,5},{7,6},{8,11},{9,8},{10,9... | collective-permute-start | bytes 393224 | tf_op jit(solution)/shard_map/ppermute | solution.py:53
  7.1 8.4 %collective-permute-start.3 = (bf16[512,128]{1,0:T(8,128)(2,1)S(1)}, bf16[512,128]{1,0:T(8,128)(2,1)S(1)}, u32[]{:S(2)}, u32[]{:S(2)}) collective-permute-start(bf16[512,128]{1,0:T(8,128)(2,1)S(1)} %get-tuple-element.32), channel_id=1, source_target_pairs={{0,2},{1,3},{2,0},{3,1},{4,6},{5,7},{6,4},{7,5},{8,10},{9,11},{10,... | collective-permute-start | bytes 393224 | tf_op jit(solution)/shard_map/ppermute | solution.py:53
  9.1 11.4 %collective-permute-start.7 = (bf16[1040,128]{1,0:T(8,128)(2,1)S(1)}, bf16[1040,128]{1,0:T(8,128)(2,1)S(1)}, u32[]{:S(2)}, u32[]{:S(2)}) collective-permute-start(bf16[1040,128]{1,0:T(8,128)(2,1)S(1)} %shard_map.38.refs_0_), channel_id=1, source_target_pairs={{0,4},{1,5},{2,6},{3,7},{4,8},{5,9},{6,10},{7,11},{8,12},{9,13},{1... | collective-permute-start | bytes 798728 | tf_op jit(solution)/shard_map/ppermute | solution.py:53
  11.0 10.0 %collective-permute-start.8 = (bf16[1040,128]{1,0:T(8,128)(2,1)S(1)}, bf16[1040,128]{1,0:T(8,128)(2,1)S(1)}, u32[]{:S(2)}, u32[]{:S(2)}) collective-permute-start(bf16[1040,128]{1,0:T(8,128)(2,1)S(1)} %shard_map.38.refs_0_), channel_id=1, source_target_pairs={{0,28},{1,29},{2,30},{3,31},{4,0},{5,1},{6,2},{7,3},{8,4},{9,5},{1... | collective-permute-start | bytes 798728 | tf_op jit(solution)/shard_map/ppermute | solution.py:53
  15.6 14.6 %collective-permute-start.4 = (bf16[512,512]{1,0:T(8,128)(2,1)S(1)}, bf16[512,512]{1,0:T(8,128)(2,1)S(1)}, u32[]{:S(2)}, u32[]{:S(2)}) collective-permute-start(bf16[512,512]{1,0:T(8,128)(2,1)S(1)} %shard_map.40.refs_0_), channel_id=1, source_target_pairs={{0,64},{64,128},{128,192},{192,0},{32,224},{96,32},{160,96},{224,1... | collective-permute-start | bytes 1572872 | tf_op jit(solution)/shard_map/ppermute | solution.py:61
  17.2 13.0 %collective-permute-start.6 = (bf16[512,512]{1,0:T(8,128)(2,1)S(1)}, bf16[512,512]{1,0:T(8,128)(2,1)S(1)}, u32[]{:S(2)}, u32[]{:S(2)}) collective-permute-start(bf16[512,512]{1,0:T(8,128)(2,1)S(1)} %shard_map.40.refs_0_), channel_id=1, source_target_pairs={{0,192},{64,0},{128,64},{192,128},{32,96},{96,160},{160,224},{224,... | collective-permute-start | bytes 1572872 | tf_op jit(solution)/shard_map/ppermute | solution.py:61
  20.5 12.6 %collective-permute-start.11 = (bf16[1040,128]{1,0:T(8,128)(2,1)S(1)}, bf16[1040,128]{1,0:T(8,128)(2,1)S(1)}, u32[]{:S(2)}, u32[]{:S(2)}) collective-permute-start(bf16[1040,128]{1,0:T(8,128)(2,1)S(1)} %collective-permute-done.7.refs_1_), channel_id=1, source_target_pairs={{0,8},{1,9},{2,10},{3,11},{4,12},{5,13},{6,14},{7,15},{8,16},{9,17... | collective-permute-start | bytes 798728 | tf_op jit(solution)/shard_map/ppermute | solution.py:53
  21.0 12.6 %collective-permute-start.10 = (bf16[1040,128]{1,0:T(8,128)(2,1)S(1)}, bf16[1040,128]{1,0:T(8,128)(2,1)S(1)}, u32[]{:S(2)}, u32[]{:S(2)}) collective-permute-start(bf16[1040,128]{1,0:T(8,128)(2,1)S(1)} %collective-permute-done.8.refs_2_), channel_id=1, source_target_pairs={{0,28},{1,29},{2,30},{3,31},{4,0},{5,1},{6,2},{7,3},{8,4},{9,5},{1... | collective-permute-start | bytes 798728 | tf_op jit(solution)/shard_map/ppermute | solution.py:53
  24.1 12.5 %collective-permute-start.9 = (bf16[1040,128]{1,0:T(8,128)(2,1)S(1)}, bf16[1040,128]{1,0:T(8,128)(2,1)S(1)}, u32[]{:S(2)}, u32[]{:S(2)}) collective-permute-start(bf16[1040,128]{1,0:T(8,128)(2,1)S(1)} %collective-permute-done.7.refs_1_), channel_id=1, source_target_pairs={{0,4},{1,5},{2,6},{3,7},{4,8},{5,9},{6,10},{7,11},{8,12},{9,13},{1... | collective-permute-start | bytes 798728 | tf_op jit(solution)/shard_map/ppermute | solution.py:53
  36.7 3.8 %collective-permute-start.12 = (bf16[6,1040,128]{2,1,0:T(8,128)(2,1)S(1)}, bf16[6,1040,128]{2,1,0:T(8,128)(2,1)S(1)}, u32[]{:S(2)}, u32[]{:S(2)}) collective-permute-start(bf16[6,1040,128]{2,1,0:T(8,128)(2,1)S(1)} %shard_map.43.refs_1_), channel_id=1, source_target_pairs={{0,32},{32,0},{1,33},{33,1},{2,34},{34,2},{3,35},{35,3},{4,36},{36... | collective-permute-start | bytes 4792328 | tf_op jit(solution)/shard_map/ppermute | solution.py:65
  36.8 10.2 %collective-permute-start.5 = (bf16[512,512]{1,0:T(8,128)(2,1)S(1)}, bf16[512,512]{1,0:T(8,128)(2,1)S(1)}, u32[]{:S(2)}, u32[]{:S(2)}) collective-permute-start(bf16[512,512]{1,0:T(8,128)(2,1)S(1)} %collective-permute-done.4.refs_2_), channel_id=1, source_target_pairs={{0,64},{64,128},{128,192},{192,0},{32,224},{96,32},{160,96},{224,1... | collective-permute-start | bytes 1572872 | tf_op jit(solution)/shard_map/ppermute | solution.py:61
  38.4 8.6 %collective-permute-start.13 = (bf16[1040,128]{1,0:T(8,128)(2,1)S(1)}, bf16[1040,128]{1,0:T(8,128)(2,1)S(1)}, u32[]{:S(2)}, u32[]{:S(2)}) collective-permute-start(bf16[1040,128]{1,0:T(8,128)(2,1)S(1)} %collective-permute-done.10.refs_4_), channel_id=1, source_target_pairs={{0,28},{1,29},{2,30},{3,31},{4,0},{5,1},{6,2},{7,3},{8,4},{9,5},{1... | collective-permute-start | bytes 798728 | tf_op jit(solution)/shard_map/ppermute | solution.py:53
  40.3 7.9 %collective-permute-start.14 = (bf16[1040,128]{1,0:T(8,128)(2,1)S(1)}, bf16[1040,128]{1,0:T(8,128)(2,1)S(1)}, u32[]{:S(2)}, u32[]{:S(2)}) collective-permute-start(bf16[1040,128]{1,0:T(8,128)(2,1)S(1)} %collective-permute-done.11.refs_5_), channel_id=1, source_target_pairs={{0,4},{1,5},{2,6},{3,7},{4,8},{5,9},{6,10},{7,11},{8,12},{9,13},{1... | collective-permute-start | bytes 798728 | tf_op jit(solution)/shard_map/ppermute | solution.py:53
  48.2 2.0 %collective-permute-start.15 = (bf16[2,1040,128]{2,1,0:T(8,128)(2,1)S(1)}, bf16[2,1040,128]{2,1,0:T(8,128)(2,1)S(1)}, u32[]{:S(2)}, u32[]{:S(2)}) collective-permute-start(bf16[2,1040,128]{2,1,0:T(8,128)(2,1)S(1)} %shard_map.45.refs_3_), channel_id=1, source_target_pairs={{0,32},{32,0},{1,33},{33,1},{2,34},{34,2},{3,35},{35,3},{4,36},{36... | collective-permute-start | bytes 1597448 | tf_op jit(solution)/shard_map/ppermute | solution.py:65
  53.3 7.7 %collective-permute-start.19 = (s16[1040,128]{1,0:T(8,128)(2,1)S(1)}, s16[1040,128]{1,0:T(8,128)(2,1)S(1)}, u32[]{:S(2)}, u32[]{:S(2)}) collective-permute-start(s16[1040,128]{1,0:T(8,128)(2,1)S(1)} %get-tuple-element.42), channel_id=1, source_target_pairs={{0,1},{1,2},{2,3},{3,0},{4,5},{5,6},{6,7},{7,4},{8,9},{9,10},{10,1... | collective-permute-start | bytes 798728 | tf_op jit(solution)/shard_map/ppermute | solution.py:53
  54.0 12.2 %collective-permute-start.17 = (s16[1040,128]{1,0:T(8,128)(2,1)S(1)}, s16[1040,128]{1,0:T(8,128)(2,1)S(1)}, u32[]{:S(2)}, u32[]{:S(2)}) collective-permute-start(s16[1040,128]{1,0:T(8,128)(2,1)S(1)} %get-tuple-element.41), channel_id=1, source_target_pairs={{0,1},{1,2},{2,3},{3,0},{4,5},{5,6},{6,7},{7,4},{8,9},{9,10},{10,1... | collective-permute-start | bytes 798728 | tf_op jit(solution)/shard_map/ppermute | solution.py:53
  57.5 15.1 %collective-permute-start.16 = (s16[2064,128]{1,0:T(8,128)(2,1)S(1)}, s16[2064,128]{1,0:T(8,128)(2,1)S(1)}, u32[]{:S(2)}, u32[]{:S(2)}) collective-permute-start(s16[2064,128]{1,0:T(8,128)(2,1)S(1)} %get-tuple-element.39), channel_id=1, source_target_pairs={{0,3},{1,0},{2,1},{3,2},{4,7},{5,4},{6,5},{7,6},{8,11},{9,8},{10,9... | collective-permute-start | bytes 1585160 | tf_op jit(solution)/shard_map/ppermute | solution.py:53
  61.3 11.3 %collective-permute-start.20 = (s16[1040,128]{1,0:T(8,128)(2,1)S(1)}, s16[1040,128]{1,0:T(8,128)(2,1)S(1)}, u32[]{:S(2)}, u32[]{:S(2)}) collective-permute-start(s16[1040,128]{1,0:T(8,128)(2,1)S(1)} %shard_map.50), channel_id=1, source_target_pairs={{0,1},{1,2},{2,3},{3,0},{4,5},{5,6},{6,7},{7,4},{8,9},{9,10},{10,1... | collective-permute-start | bytes 798728 | tf_op jit(solution)/shard_map/ppermute | solution.py:53
  66.5 8.7 %collective-permute-start.18 = (s16[1040,128]{1,0:T(8,128)(2,1)S(1)}, s16[1040,128]{1,0:T(8,128)(2,1)S(1)}, u32[]{:S(2)}, u32[]{:S(2)}) collective-permute-start(s16[1040,128]{1,0:T(8,128)(2,1)S(1)} %shard_map.49), channel_id=1, source_target_pairs={{0,1},{1,2},{2,3},{3,0},{4,5},{5,6},{6,7},{7,4},{8,9},{9,10},{10,1... | collective-permute-start | bytes 798728 | tf_op jit(solution)/shard_map/ppermute | solution.py:53
  75.8 1.2 %collective-permute-start.21 = (f32[1,128]{1,0:T(1,128)S(1)}, f32[1,128]{1,0:T(1,128)S(1)}, u32[]{:S(2)}, u32[]{:S(2)}) collective-permute-start(f32[1,128]{1,0:T(1,128)S(1)} %get-tuple-element.45), channel_id=1, source_target_pairs={{0,32},{32,0},{1,33},{33,1},{2,34},{34,2},{3,35},{35,3},{4,36},{36... | collective-permute-start | bytes 1544 | tf_op jit(solution)/shard_map/ppermute | solution.py:65
  77.0 7.3 %collective-permute-start.22 = (f32[1024,128]{1,0:T(8,128)S(1)}, f32[1024,128]{1,0:T(8,128)S(1)}, u32[]{:S(2)}, u32[]{:S(2)}) collective-permute-start(f32[1024,128]{1,0:T(8,128)S(1)} %get-tuple-element.46), channel_id=1, source_target_pairs={{0,32},{32,0},{1,33},{33,1},{2,34},{34,2},{3,35},{35,3},{4,36},{36... | collective-permute-start | bytes 1572872 | tf_op jit(solution)/shard_map/ppermute | solution.py:65
  77.2 3.6 %collective-permute-start.23 = (f32[2,128]{1,0:T(2,128)S(1)}, f32[2,128]{1,0:T(2,128)S(1)}, u32[]{:S(2)}, u32[]{:S(2)}) collective-permute-start(f32[2,128]{1,0:T(2,128)S(1)} %pad_maximum_fusion.refs_0_), channel_id=1, source_target_pairs={{0,64},{64,128},{128,192},{192,0},{32,224},{96,32},{160,96},{224,1... | collective-permute-start | bytes 3080 | tf_op jit(solution)/shard_map/ppermute | solution.py:61
  79.1 3.6 %collective-permute-start.24 = (f32[2,128]{1,0:T(2,128)S(1)}, f32[2,128]{1,0:T(2,128)S(1)}, u32[]{:S(2)}, u32[]{:S(2)}) collective-permute-start(f32[2,128]{1,0:T(2,128)S(1)} %pad_maximum_fusion.refs_0_), channel_id=1, source_target_pairs={{0,192},{64,0},{128,64},{192,128},{32,96},{96,160},{160,224},{224,... | collective-permute-start | bytes 3080 | tf_op jit(solution)/shard_map/ppermute | solution.py:61
  79.3 5.1 %collective-permute-start.25 = (f32[2,128]{1,0:T(2,128)S(1)}, f32[2,128]{1,0:T(2,128)S(1)}, u32[]{:S(2)}, u32[]{:S(2)}) collective-permute-start(f32[2,128]{1,0:T(2,128)S(1)} %pad_maximum_fusion.refs_0_), channel_id=1, source_target_pairs={{0,128},{64,192},{128,0},{192,64},{32,160},{96,224},{160,32},{224,... | collective-permute-start | bytes 3080 | tf_op jit(solution)/shard_map/ppermute | solution.py:61

commit v6 on v5

--- a/solution.py
+++ b/solution.py
@@ -142,6 +142,8 @@
     b_ref, parts, given = refs[0], refs[1 : n + 1], refs[n + 1 : -5 - len(outs)]
     out_refs = refs[-5 - len(outs) : -5]
     total_ref, heads_ref, table_ref, work_ref, sem = refs[-5:]
+    if outs == (None,):
+        total_ref = out_refs[0]
     at = 0
     for part, (_, _, steps) in zip(parts, plan):
         for j in range(len(steps)):
@@ -198,8 +200,8 @@
         lax.fori_loop(0, (count + BATCH - 1) // BATCH, step, 0)
     for out, out_ref in zip(outs, out_refs):
         if out is None:
-            out_ref[...] = total_ref[...]
-        elif isinstance(out, int):
+            continue
+        if isinstance(out, int):
             out_ref[...] = total_ref[:, out * TILE : (out + 1) * TILE]
         else:
             slot, start, _ = out
@@ -223,7 +225,7 @@
         *([] if total is None else [total]),
         mib=24,
         scratch_shapes=[
-            pltpu.VMEM((ROWS + TILE, cols), jnp.float32),
+            pltpu.VMEM((8 if outs == (None,) else ROWS + TILE, cols), jnp.float32),
             pltpu.VMEM((count, TILE), jnp.int32),
             pltpu.SMEM((count, TILE), jnp.int32),
             pltpu.SMEM((8, TILE), jnp.int32),

time: 86.1 us -> 86.3 us (level)
  transfers between devices with their start and end apart: 26 -> 26, of which waited for: 17 -> 16; matrix products, arithmetic and copies ran while one was open for 0% -> 0% of each run, Pallas kernels for 13% -> 13%
where the time goes in v6:
time: 86.3 us; the launch traced here: 85.7 us
  waiting for transfers between devices  38.1 us (44%)
  starting transfers between devices  28.6 us (33%)
  Pallas kernels  15.9 us (18%)
  local copies, waits for them, and re-layouts  2.73 us (3%)
    ppermute x15, waiting for transfers between devices, hop(): return lax.ppermute(x, ('col', 'layer'), pairs)  25.5 us
    ppermute x15, starting transfers between devices, hop(): return lax.ppermute(x, ('col', 'layer'), pairs)  20.6 us
    pallas_call x15, Pallas kernels, call(): pl.pallas_call(kernel, out_shape=out_shape, in_specs=[first] + [VMEM] * (...  14.9 us
    ppermute x6, waiting for transfers between devices, hop_x(): return lax.ppermute(x, ('row', 'col'), pairs)  9.6 us
    ppermute x6, starting transfers between devices, hop_x(): return lax.ppermute(x, ('row', 'col'), pairs)  7.2 us
    ppermute x5, waiting for transfers between devices, swap(): return lax.ppermute(x, 'col', [(0, 1), (1, 0)])  2.98 us
    unnamed x6, local copies, waits for them, and re-layouts  2.73 us
  transfers between devices with their start and end apart: 26, of which 16 were waited for; matrix products, arithmetic and copies ran while one was open for 0% of the time, Pallas kernels for 13%

profile of v6, /device:TPU:2, one launch (start us, length us, event | category | flops | bytes accessed | tf_op | source)
XLA Modules:
  0.0 85.7 jit_solution(1293448348499772761)
XLA Ops:
  0.0 1.0 %copy-done = bf16[1024,256]{1,0:T(8,128)(2,1)S(1)} copy-done((bf16[1024,256]{1,0:T(8,128)(2,1)S(1)}, bf16[1024,256]{1,0:T(8,128)(2,1)}, u32[]{:S(2)}) %copy-start) | copy-done | bytes 524312
  1.3 1.0 %copy-done.1 = bf16[2048,128]{1,0:T(8,128)(2,1)S(1)} copy-done((bf16[2048,128]{1,0:T(8,128)(2,1)S(1)}, bf16[2048,128]{1,0:T(8,128)(2,1)}, u32[]{:S(2)}) %copy-start.1) | copy-done | bytes 524312
  3.8 1.7 %collective-permute-start.1 = (bf16[512,128]{1,0:T(8,128)(2,1)S(1)}, bf16[512,128]{1,0:T(8,128)(2,1)S(1)}, u32[]{:S(2)}, u32[]{:S(2)}) collective-permute-start(bf16[512,128]{1,0:T(8,128)(2,1)S(1)} %get-tuple-element.30), channel_id=1, source_target_pairs={{0,1},{1,2},{2,3},{3,0},{4,5},{5,6},{6,7},{7,4},{8,9},{9,10},{10,1... | collective-permute-start | bytes 393224 | tf_op jit(solution)/shard_map/ppermute | solution.py:53
  5.5 1.7 %collective-permute-start.2 = (bf16[512,128]{1,0:T(8,128)(2,1)S(1)}, bf16[512,128]{1,0:T(8,128)(2,1)S(1)}, u32[]{:S(2)}, u32[]{:S(2)}) collective-permute-start(bf16[512,128]{1,0:T(8,128)(2,1)S(1)} %get-tuple-element.31), channel_id=1, source_target_pairs={{0,3},{1,0},{2,1},{3,2},{4,7},{5,4},{6,5},{7,6},{8,11},{9,8},{10,9... | collective-permute-start | bytes 393224 | tf_op jit(solution)/shard_map/ppermute | solution.py:53
  7.1 2.0 %collective-permute-start.3 = (bf16[512,128]{1,0:T(8,128)(2,1)S(1)}, bf16[512,128]{1,0:T(8,128)(2,1)S(1)}, u32[]{:S(2)}, u32[]{:S(2)}) collective-permute-start(bf16[512,128]{1,0:T(8,128)(2,1)S(1)} %get-tuple-element.32), channel_id=1, source_target_pairs={{0,2},{1,3},{2,0},{3,1},{4,6},{5,7},{6,4},{7,5},{8,10},{9,11},{10,... | collective-permute-start | bytes 393224 | tf_op jit(solution)/shard_map/ppermute | solution.py:53
  9.1 1.9 %collective-permute-start.7 = (bf16[1040,128]{1,0:T(8,128)(2,1)S(1)}, bf16[1040,128]{1,0:T(8,128)(2,1)S(1)}, u32[]{:S(2)}, u32[]{:S(2)}) collective-permute-start(bf16[1040,128]{1,0:T(8,128)(2,1)S(1)} %shard_map.38.refs_0_), channel_id=1, source_target_pairs={{0,4},{1,5},{2,6},{3,7},{4,8},{5,9},{6,10},{7,11},{8,12},{9,13},{1... | collective-permute-start | bytes 798728 | tf_op jit(solution)/shard_map/ppermute | solution.py:53
  11.0 3.9 %collective-permute-start.8 = (bf16[1040,128]{1,0:T(8,128)(2,1)S(1)}, bf16[1040,128]{1,0:T(8,128)(2,1)S(1)}, u32[]{:S(2)}, u32[]{:S(2)}) collective-permute-start(bf16[1040,128]{1,0:T(8,128)(2,1)S(1)} %shard_map.38.refs_0_), channel_id=1, source_target_pairs={{0,28},{1,29},{2,30},{3,31},{4,0},{5,1},{6,2},{7,3},{8,4},{9,5},{1... | collective-permute-start | bytes 798728 | tf_op jit(solution)/shard_map/ppermute | solution.py:53
  15.6 1.6 %collective-permute-start.4 = (bf16[512,512]{1,0:T(8,128)(2,1)S(1)}, bf16[512,512]{1,0:T(8,128)(2,1)S(1)}, u32[]{:S(2)}, u32[]{:S(2)}) collective-permute-start(bf16[512,512]{1,0:T(8,128)(2,1)S(1)} %shard_map.40.refs_0_), channel_id=1, source_target_pairs={{0,64},{64,128},{128,192},{192,0},{32,224},{96,32},{160,96},{224,1... | collective-permute-start | bytes 1572872 | tf_op jit(solution)/shard_map/ppermute | solution.py:61
  17.7 2.8 %collective-permute-done.7.refs_1_ = bf16[1040,128]{1,0:T(8,128)(2,1)S(1)} collective-permute-done((bf16[1040,128]{1,0:T(8,128)(2,1)S(1)}, bf16[1040,128]{1,0:T(8,128)(2,1)S(1)}, u32[]{:S(2)}, u32[]{:S(2)}) %collective-permute-start.7) | collective-permute-done | bytes 266272 | tf_op jit(solution)/shard_map/ppermute | solution.py:53
  21.0 3.1 %collective-permute-start.10 = (bf16[1040,128]{1,0:T(8,128)(2,1)S(1)}, bf16[1040,128]{1,0:T(8,128)(2,1)S(1)}, u32[]{:S(2)}, u32[]{:S(2)}) collective-permute-start(bf16[1040,128]{1,0:T(8,128)(2,1)S(1)} %collective-permute-done.8.refs_2_), channel_id=1, source_target_pairs={{0,28},{1,29},{2,30},{3,31},{4,0},{5,1},{6,2},{7,3},{8,4},{9,5},{1... | collective-permute-start | bytes 798728 | tf_op jit(solution)/shard_map/ppermute | solution.py:53
  24.1 6.0 %collective-permute-done.4.refs_2_ = bf16[512,512]{1,0:T(8,128)(2,1)S(1)} collective-permute-done((bf16[512,512]{1,0:T(8,128)(2,1)S(1)}, bf16[512,512]{1,0:T(8,128)(2,1)S(1)}, u32[]{:S(2)}, u32[]{:S(2)}) %collective-permute-start.4) | collective-permute-done | bytes 524320 | tf_op jit(solution)/shard_map/ppermute | solution.py:61
  30.2 3.0 %collective-permute-done.11.refs_5_ = bf16[1040,128]{1,0:T(8,128)(2,1)S(1)} collective-permute-done((bf16[1040,128]{1,0:T(8,128)(2,1)S(1)}, bf16[1040,128]{1,0:T(8,128)(2,1)S(1)}, u32[]{:S(2)}, u32[]{:S(2)}) %collective-permute-start.11) | collective-permute-done | bytes 266272 | tf_op jit(solution)/shard_map/ppermute | solution.py:53
  33.6 3.0 %collective-permute-done.9.refs_3_ = bf16[1040,128]{1,0:T(8,128)(2,1)S(1)} collective-permute-done((bf16[1040,128]{1,0:T(8,128)(2,1)S(1)}, bf16[1040,128]{1,0:T(8,128)(2,1)S(1)}, u32[]{:S(2)}, u32[]{:S(2)}) %collective-permute-start.9) | collective-permute-done | bytes 266272 | tf_op jit(solution)/shard_map/ppermute | solution.py:53
  36.8 1.6 %collective-permute-start.5 = (bf16[512,512]{1,0:T(8,128)(2,1)S(1)}, bf16[512,512]{1,0:T(8,128)(2,1)S(1)}, u32[]{:S(2)}, u32[]{:S(2)}) collective-permute-start(bf16[512,512]{1,0:T(8,128)(2,1)S(1)} %collective-permute-done.4.refs_2_), channel_id=1, source_target_pairs={{0,64},{64,128},{128,192},{192,0},{32,224},{96,32},{160,96},{224,1... | collective-permute-start | bytes 1572872 | tf_op jit(solution)/shard_map/ppermute | solution.py:61
  38.4 1.9 %collective-permute-start.13 = (bf16[1040,128]{1,0:T(8,128)(2,1)S(1)}, bf16[1040,128]{1,0:T(8,128)(2,1)S(1)}, u32[]{:S(2)}, u32[]{:S(2)}) collective-permute-start(bf16[1040,128]{1,0:T(8,128)(2,1)S(1)} %collective-permute-done.10.refs_4_), channel_id=1, source_target_pairs={{0,28},{1,29},{2,30},{3,31},{4,0},{5,1},{6,2},{7,3},{8,4},{9,5},{1... | collective-permute-start | bytes 798728 | tf_op jit(solution)/shard_map/ppermute | solution.py:53
  40.5 3.4 %shard_map.44.refs_5_ = f32[2176,512]{1,0:T(8,128)S(1)} custom-call(bf16[4,512,512]{2,1,0:T(8,128)(2,1)S(1)} %shard_map.41.refs_1_.refs_0_, bf16[6,1040,128]{2,1,0:T(8,128)(2,1)S(1)} %shard_map.43.refs_1_, bf16[6,1040,128]{2,1,0:T(8,128)(2,1)S(1)} %collective-permute-done.12.refs_2_), custom_call_target="tpu_custom_call" | custom-call | flops 1635778560 | bytes 12779520 | tf_op jit(solution)/shard_map/pallas_call | solution.py:31
  43.9 3.0 %collective-permute-done.13.refs_0_ = bf16[1040,128]{1,0:T(8,128)(2,1)S(1)} collective-permute-done((bf16[1040,128]{1,0:T(8,128)(2,1)S(1)}, bf16[1040,128]{1,0:T(8,128)(2,1)S(1)}, u32[]{:S(2)}, u32[]{:S(2)}) %collective-permute-start.13) | collective-permute-done | bytes 266272 | tf_op jit(solution)/shard_map/ppermute | solution.py:53
  47.0 1.2 %collective-permute-done.14.refs_1_ = bf16[1040,128]{1,0:T(8,128)(2,1)S(1)} collective-permute-done((bf16[1040,128]{1,0:T(8,128)(2,1)S(1)}, bf16[1040,128]{1,0:T(8,128)(2,1)S(1)}, u32[]{:S(2)}, u32[]{:S(2)}) %collective-permute-start.14) | collective-permute-done | bytes 266272 | tf_op jit(solution)/shard_map/ppermute | solution.py:53
  48.4 1.9 %collective-permute-done.15.refs_4_ = bf16[2,1040,128]{2,1,0:T(8,128)(2,1)S(1)} collective-permute-done((bf16[2,1040,128]{2,1,0:T(8,128)(2,1)S(1)}, bf16[2,1040,128]{2,1,0:T(8,128)(2,1)S(1)}, u32[]{:S(2)}, u32[]{:S(2)}) %collective-permute-start.15) | collective-permute-done | bytes 532512 | tf_op jit(solution)/shard_map/ppermute | solution.py:65
  50.3 3.0 %shard_map.48 = (s16[1040,128]{1,0:T(8,128)(2,1)S(1)}, s16[1040,128]{1,0:T(8,128)(2,1)S(1)}) custom-call(bf16[4,512,512]{2,1,0:T(8,128)(2,1)S(1)} %shard_map.42.refs_0_, bf16[6,1040,128]{2,1,0:T(8,128)(2,1)S(1)} %shard_map.43.refs_1_, bf16[6,1040,128]{2,1,0:T(8,128)(2,1)S(1)} %collective-permute-done.12.refs_2_, ...), custom_call_target="tpu_custom_call" | custom-call | flops 545259520 | bytes 4259840 | tf_op jit(solution)/shard_map/pallas_call | solution.py:31
  54.0 3.4 %shard_map.47 = (s16[2064,128]{1,0:T(8,128)(2,1)S(1)}, f32[2176,128]{1,0:T(8,128)S(1)}) custom-call(bf16[4,512,512]{2,1,0:T(8,128)(2,1)S(1)} %shard_map.42.refs_0_, bf16[6,1040,128]{2,1,0:T(8,128)(2,1)S(1)} %shard_map.43.refs_1_, bf16[6,1040,128]{2,1,0:T(8,128)(2,1)S(1)} %collective-permute-done.12.refs_2_, bf16[2,1040,128]{2,1,0:T(8,128)(2,1)S(1)} %shard_map.45.refs_3_, ...), custom_call_target="tpu_custom_call" | custom-call | flops 1090519040 | bytes 8519680 | tf_op jit(solution)/shard_map/pallas_call | solution.py:31
  57.4 2.8 %collective-permute-start.16 = (s16[2064,128]{1,0:T(8,128)(2,1)S(1)}, s16[2064,128]{1,0:T(8,128)(2,1)S(1)}, u32[]{:S(2)}, u32[]{:S(2)}) collective-permute-start(s16[2064,128]{1,0:T(8,128)(2,1)S(1)} %get-tuple-element.39), channel_id=1, source_target_pairs={{0,3},{1,0},{2,1},{3,2},{4,7},{5,4},{6,5},{7,6},{8,11},{9,8},{10,9... | collective-permute-start | bytes 1585160 | tf_op jit(solution)/shard_map/ppermute | solution.py:53
  61.3 4.8 %collective-permute-done.17.recv_ref = s16[1040,128]{1,0:T(8,128)(2,1)S(1)} collective-permute-done((s16[1040,128]{1,0:T(8,128)(2,1)S(1)}, s16[1040,128]{1,0:T(8,128)(2,1)S(1)}, u32[]{:S(2)}, u32[]{:S(2)}) %collective-permute-start.17) | collective-permute-done | bytes 266272 | tf_op jit(solution)/shard_map/ppermute | solution.py:53
  66.6 2.6 %shard_map.46.total_ref = f32[2176,128]{1,0:T(8,128)S(1)} custom-call(bf16[4,512,512]{2,1,0:T(8,128)(2,1)S(1)} %shard_map.42.refs_0_, bf16[6,1040,128]{2,1,0:T(8,128)(2,1)S(1)} %shard_map.43.refs_1_, bf16[6,1040,128]{2,1,0:T(8,128)(2,1)S(1)} %collective-permute-done.12.refs_2_, bf16[2,1040,128]{2,1,0:T(8,128)(2,1)S(1)} %shard_map.45.refs_3_, ...), custom_call_target="tpu_custom_call" | custom-call | flops 545259520 | bytes 4259840 | tf_op jit(solution)/shard_map/pallas_call | solution.py:31
  69.2 3.4 %collective-permute-done.16.whole_ref = s16[2064,128]{1,0:T(8,128)(2,1)S(1)} collective-permute-done((s16[2064,128]{1,0:T(8,128)(2,1)S(1)}, s16[2064,128]{1,0:T(8,128)(2,1)S(1)}, u32[]{:S(2)}, u32[]{:S(2)}) %collective-permute-start.16) | collective-permute-done | bytes 528416 | tf_op jit(solution)/shard_map/ppermute | solution.py:53
  72.6 2.5 %collective-permute-done.18.low_ref = s16[1040,128]{1,0:T(8,128)(2,1)S(1)} collective-permute-done((s16[1040,128]{1,0:T(8,128)(2,1)S(1)}, s16[1040,128]{1,0:T(8,128)(2,1)S(1)}, u32[]{:S(2)}, u32[]{:S(2)}) %collective-permute-start.18) | collective-permute-done | bytes 266272 | tf_op jit(solution)/shard_map/ppermute | solution.py:53
  76.1 1.1 %collective-permute-done.21 = f32[1,128]{1,0:T(1,128)S(1)} collective-permute-done((f32[1,128]{1,0:T(1,128)S(1)}, f32[1,128]{1,0:T(1,128)S(1)}, u32[]{:S(2)}, u32[]{:S(2)}) %collective-permute-start.21) | collective-permute-done | bytes 544 | tf_op jit(solution)/shard_map/ppermute | solution.py:65
  77.4 1.8 %collective-permute-start.23 = (f32[2,128]{1,0:T(2,128)S(1)}, f32[2,128]{1,0:T(2,128)S(1)}, u32[]{:S(2)}, u32[]{:S(2)}) collective-permute-start(f32[2,128]{1,0:T(2,128)S(1)} %pad_maximum_fusion.refs_0_), channel_id=1, source_target_pairs={{0,64},{64,128},{128,192},{192,0},{32,224},{96,32},{160,96},{224,1... | collective-permute-start | bytes 3080 | tf_op jit(solution)/shard_map/ppermute | solution.py:61
  79.5 1.5 %collective-permute-start.25 = (f32[2,128]{1,0:T(2,128)S(1)}, f32[2,128]{1,0:T(2,128)S(1)}, u32[]{:S(2)}, u32[]{:S(2)}) collective-permute-start(f32[2,128]{1,0:T(2,128)S(1)} %pad_maximum_fusion.refs_0_), channel_id=1, source_target_pairs={{0,128},{64,192},{128,0},{192,64},{32,160},{96,224},{160,32},{224,... | collective-permute-start | bytes 3080 | tf_op jit(solution)/shard_map/ppermute | solution.py:61
  81.0 1.8 %collective-permute-done.24.refs_2_ = f32[2,128]{1,0:T(2,128)S(1)} collective-permute-done((f32[2,128]{1,0:T(2,128)S(1)}, f32[2,128]{1,0:T(2,128)S(1)}, u32[]{:S(2)}, u32[]{:S(2)}) %collective-permute-start.24) | collective-permute-done | bytes 1056 | tf_op jit(solution)/shard_map/ppermute | solution.py:61
  82.8 1.7 %collective-permute-done.25.refs_3_ = f32[2,128]{1,0:T(2,128)S(1)} collective-permute-done((f32[2,128]{1,0:T(2,128)S(1)}, f32[2,128]{1,0:T(2,128)S(1)}, u32[]{:S(2)}, u32[]{:S(2)}) %collective-permute-start.25) | collective-permute-done | bytes 1056 | tf_op jit(solution)/shard_map/ppermute | solution.py:61
  84.5 1.0 %shard_map.52 = f32[1024,256]{1,0:T(8,128)} custom-call(f32[1024,128]{1,0:T(8,128)S(1)} %get-tuple-element.43.keep_ref, f32[1024,128]{1,0:T(8,128)S(1)} %collective-permute-done.22.recv_ref, f32[2,128]{1,0:T(2,128)S(1)} %pad_maximum_fusion.refs_0_, f32[2,128]{1,0:T(2,128)S(1)} %collective-permute-done.23.refs_1_, ...), custom_call_target="tpu_custom_call" | custom-call | tf_op jit(solution)/shard_map/pallas_call | solution.py:331
  (43 shorter events, 8.1 us)
Async XLA Ops:
  0.0 1.0 %copy-start = (bf16[1024,256]{1,0:T(8,128)(2,1)S(1)}, bf16[1024,256]{1,0:T(8,128)(2,1)}, u32[]{:S(2)}) copy-start(bf16[1024,256]{1,0:T(8,128)(2,1)} %b_ref.1) | copy-start | bytes 1572868
  1.2 2.6 %collective-permute-start = (bf16[1024,128]{1,0:T(8,128)(2,1)S(1)}, bf16[1024,128]{1,0:T(8,128)(2,1)S(1)}, u32[]{:S(2)}, u32[]{:S(2)}) collective-permute-start(bf16[1024,128]{1,0:T(8,128)(2,1)S(1)} %get-tuple-element.28), channel_id=1, source_target_pairs={{0,32},{32,0},{1,33},{33,1},{2,34},{34,2},{3,35},{35,3},{4,36},{36... | collective-permute-start | bytes 786440 | tf_op jit(solution)/shard_map/ppermute | solution.py:65
  1.3 1.0 %copy-start.1 = (bf16[2048,128]{1,0:T(8,128)(2,1)S(1)}, bf16[2048,128]{1,0:T(8,128)(2,1)}, u32[]{:S(2)}) copy-start(bf16[2048,128]{1,0:T(8,128)(2,1)} %a_ref.1) | copy-start | bytes 1572868
  2.3 0.7 copy-start.2
  3.8 11.2 %collective-permute-start.1 = (bf16[512,128]{1,0:T(8,128)(2,1)S(1)}, bf16[512,128]{1,0:T(8,128)(2,1)S(1)}, u32[]{:S(2)}, u32[]{:S(2)}) collective-permute-start(bf16[512,128]{1,0:T(8,128)(2,1)S(1)} %get-tuple-element.30), channel_id=1, source_target_pairs={{0,1},{1,2},{2,3},{3,0},{4,5},{5,6},{6,7},{7,4},{8,9},{9,10},{10,1... | collective-permute-start | bytes 393224 | tf_op jit(solution)/shard_map/ppermute | solution.py:53
  5.5 9.5 %collective-permute-start.2 = (bf16[512,128]{1,0:T(8,128)(2,1)S(1)}, bf16[512,128]{1,0:T(8,128)(2,1)S(1)}, u32[]{:S(2)}, u32[]{:S(2)}) collective-permute-start(bf16[512,128]{1,0:T(8,128)(2,1)S(1)} %get-tuple-element.31), channel_id=1, source_target_pairs={{0,3},{1,0},{2,1},{3,2},{4,7},{5,4},{6,5},{7,6},{8,11},{9,8},{10,9... | collective-permute-start | bytes 393224 | tf_op jit(solution)/shard_map/ppermute | solution.py:53
  7.1 8.4 %collective-permute-start.3 = (bf16[512,128]{1,0:T(8,128)(2,1)S(1)}, bf16[512,128]{1,0:T(8,128)(2,1)S(1)}, u32[]{:S(2)}, u32[]{:S(2)}) collective-permute-start(bf16[512,128]{1,0:T(8,128)(2,1)S(1)} %get-tuple-element.32), channel_id=1, source_target_pairs={{0,2},{1,3},{2,0},{3,1},{4,6},{5,7},{6,4},{7,5},{8,10},{9,11},{10,... | collective-permute-start | bytes 393224 | tf_op jit(solution)/shard_map/ppermute | solution.py:53
  9.1 11.4 %collective-permute-start.7 = (bf16[1040,128]{1,0:T(8,128)(2,1)S(1)}, bf16[1040,128]{1,0:T(8,128)(2,1)S(1)}, u32[]{:S(2)}, u32[]{:S(2)}) collective-permute-start(bf16[1040,128]{1,0:T(8,128)(2,1)S(1)} %shard_map.38.refs_0_), channel_id=1, source_target_pairs={{0,4},{1,5},{2,6},{3,7},{4,8},{5,9},{6,10},{7,11},{8,12},{9,13},{1... | collective-permute-start | bytes 798728 | tf_op jit(solution)/shard_map/ppermute | solution.py:53
  11.0 10.0 %collective-permute-start.8 = (bf16[1040,128]{1,0:T(8,128)(2,1)S(1)}, bf16[1040,128]{1,0:T(8,128)(2,1)S(1)}, u32[]{:S(2)}, u32[]{:S(2)}) collective-permute-start(bf16[1040,128]{1,0:T(8,128)(2,1)S(1)} %shard_map.38.refs_0_), channel_id=1, source_target_pairs={{0,28},{1,29},{2,30},{3,31},{4,0},{5,1},{6,2},{7,3},{8,4},{9,5},{1... | collective-permute-start | bytes 798728 | tf_op jit(solution)/shard_map/ppermute | solution.py:53
  15.6 14.6 %collective-permute-start.4 = (bf16[512,512]{1,0:T(8,128)(2,1)S(1)}, bf16[512,512]{1,0:T(8,128)(2,1)S(1)}, u32[]{:S(2)}, u32[]{:S(2)}) collective-permute-start(bf16[512,512]{1,0:T(8,128)(2,1)S(1)} %shard_map.40.refs_0_), channel_id=1, source_target_pairs={{0,64},{64,128},{128,192},{192,0},{32,224},{96,32},{160,96},{224,1... | collective-permute-start | bytes 1572872 | tf_op jit(solution)/shard_map/ppermute | solution.py:61
  17.2 13.0 %collective-permute-start.6 = (bf16[512,512]{1,0:T(8,128)(2,1)S(1)}, bf16[512,512]{1,0:T(8,128)(2,1)S(1)}, u32[]{:S(2)}, u32[]{:S(2)}) collective-permute-start(bf16[512,512]{1,0:T(8,128)(2,1)S(1)} %shard_map.40.refs_0_), channel_id=1, source_target_pairs={{0,192},{64,0},{128,64},{192,128},{32,96},{96,160},{160,224},{224,... | collective-permute-start | bytes 1572872 | tf_op jit(solution)/shard_map/ppermute | solution.py:61
  20.5 12.6 %collective-permute-start.11 = (bf16[1040,128]{1,0:T(8,128)(2,1)S(1)}, bf16[1040,128]{1,0:T(8,128)(2,1)S(1)}, u32[]{:S(2)}, u32[]{:S(2)}) collective-permute-start(bf16[1040,128]{1,0:T(8,128)(2,1)S(1)} %collective-permute-done.7.refs_1_), channel_id=1, source_target_pairs={{0,8},{1,9},{2,10},{3,11},{4,12},{5,13},{6,14},{7,15},{8,16},{9,17... | collective-permute-start | bytes 798728 | tf_op jit(solution)/shard_map/ppermute | solution.py:53
  21.0 12.6 %collective-permute-start.10 = (bf16[1040,128]{1,0:T(8,128)(2,1)S(1)}, bf16[1040,128]{1,0:T(8,128)(2,1)S(1)}, u32[]{:S(2)}, u32[]{:S(2)}) collective-permute-start(bf16[1040,128]{1,0:T(8,128)(2,1)S(1)} %collective-permute-done.8.refs_2_), channel_id=1, source_target_pairs={{0,28},{1,29},{2,30},{3,31},{4,0},{5,1},{6,2},{7,3},{8,4},{9,5},{1... | collective-permute-start | bytes 798728 | tf_op jit(solution)/shard_map/ppermute | solution.py:53
  24.1 12.5 %collective-permute-start.9 = (bf16[1040,128]{1,0:T(8,128)(2,1)S(1)}, bf16[1040,128]{1,0:T(8,128)(2,1)S(1)}, u32[]{:S(2)}, u32[]{:S(2)}) collective-permute-start(bf16[1040,128]{1,0:T(8,128)(2,1)S(1)} %collective-permute-done.7.refs_1_), channel_id=1, source_target_pairs={{0,4},{1,5},{2,6},{3,7},{4,8},{5,9},{6,10},{7,11},{8,12},{9,13},{1... | collective-permute-start | bytes 798728 | tf_op jit(solution)/shard_map/ppermute | solution.py:53
  36.7 3.8 %collective-permute-start.12 = (bf16[6,1040,128]{2,1,0:T(8,128)(2,1)S(1)}, bf16[6,1040,128]{2,1,0:T(8,128)(2,1)S(1)}, u32[]{:S(2)}, u32[]{:S(2)}) collective-permute-start(bf16[6,1040,128]{2,1,0:T(8,128)(2,1)S(1)} %shard_map.43.refs_1_), channel_id=1, source_target_pairs={{0,32},{32,0},{1,33},{33,1},{2,34},{34,2},{3,35},{35,3},{4,36},{36... | collective-permute-start | bytes 4792328 | tf_op jit(solution)/shard_map/ppermute | solution.py:65
  36.8 10.2 %collective-permute-start.5 = (bf16[512,512]{1,0:T(8,128)(2,1)S(1)}, bf16[512,512]{1,0:T(8,128)(2,1)S(1)}, u32[]{:S(2)}, u32[]{:S(2)}) collective-permute-start(bf16[512,512]{1,0:T(8,128)(2,1)S(1)} %collective-permute-done.4.refs_2_), channel_id=1, source_target_pairs={{0,64},{64,128},{128,192},{192,0},{32,224},{96,32},{160,96},{224,1... | collective-permute-start | bytes 1572872 | tf_op jit(solution)/shard_map/ppermute | solution.py:61
  38.4 8.6 %collective-permute-start.13 = (bf16[1040,128]{1,0:T(8,128)(2,1)S(1)}, bf16[1040,128]{1,0:T(8,128)(2,1)S(1)}, u32[]{:S(2)}, u32[]{:S(2)}) collective-permute-start(bf16[1040,128]{1,0:T(8,128)(2,1)S(1)} %collective-permute-done.10.refs_4_), channel_id=1, source_target_pairs={{0,28},{1,29},{2,30},{3,31},{4,0},{5,1},{6,2},{7,3},{8,4},{9,5},{1... | collective-permute-start | bytes 798728 | tf_op jit(solution)/shard_map/ppermute | solution.py:53
  40.3 7.9 %collective-permute-start.14 = (bf16[1040,128]{1,0:T(8,128)(2,1)S(1)}, bf16[1040,128]{1,0:T(8,128)(2,1)S(1)}, u32[]{:S(2)}, u32[]{:S(2)}) collective-permute-start(bf16[1040,128]{1,0:T(8,128)(2,1)S(1)} %collective-permute-done.11.refs_5_), channel_id=1, source_target_pairs={{0,4},{1,5},{2,6},{3,7},{4,8},{5,9},{6,10},{7,11},{8,12},{9,13},{1... | collective-permute-start | bytes 798728 | tf_op jit(solution)/shard_map/ppermute | solution.py:53
  48.2 2.0 %collective-permute-start.15 = (bf16[2,1040,128]{2,1,0:T(8,128)(2,1)S(1)}, bf16[2,1040,128]{2,1,0:T(8,128)(2,1)S(1)}, u32[]{:S(2)}, u32[]{:S(2)}) collective-permute-start(bf16[2,1040,128]{2,1,0:T(8,128)(2,1)S(1)} %shard_map.45.refs_3_), channel_id=1, source_target_pairs={{0,32},{32,0},{1,33},{33,1},{2,34},{34,2},{3,35},{35,3},{4,36},{36... | collective-permute-start | bytes 1597448 | tf_op jit(solution)/shard_map/ppermute | solution.py:65
  53.2 7.7 %collective-permute-start.19 = (s16[1040,128]{1,0:T(8,128)(2,1)S(1)}, s16[1040,128]{1,0:T(8,128)(2,1)S(1)}, u32[]{:S(2)}, u32[]{:S(2)}) collective-permute-start(s16[1040,128]{1,0:T(8,128)(2,1)S(1)} %get-tuple-element.42), channel_id=1, source_target_pairs={{0,1},{1,2},{2,3},{3,0},{4,5},{5,6},{6,7},{7,4},{8,9},{9,10},{10,1... | collective-permute-start | bytes 798728 | tf_op jit(solution)/shard_map/ppermute | solution.py:53
  54.0 12.2 %collective-permute-start.17 = (s16[1040,128]{1,0:T(8,128)(2,1)S(1)}, s16[1040,128]{1,0:T(8,128)(2,1)S(1)}, u32[]{:S(2)}, u32[]{:S(2)}) collective-permute-start(s16[1040,128]{1,0:T(8,128)(2,1)S(1)} %get-tuple-element.41), channel_id=1, source_target_pairs={{0,1},{1,2},{2,3},{3,0},{4,5},{5,6},{6,7},{7,4},{8,9},{9,10},{10,1... | collective-permute-start | bytes 798728 | tf_op jit(solution)/shard_map/ppermute | solution.py:53
  57.4 15.2 %collective-permute-start.16 = (s16[2064,128]{1,0:T(8,128)(2,1)S(1)}, s16[2064,128]{1,0:T(8,128)(2,1)S(1)}, u32[]{:S(2)}, u32[]{:S(2)}) collective-permute-start(s16[2064,128]{1,0:T(8,128)(2,1)S(1)} %get-tuple-element.39), channel_id=1, source_target_pairs={{0,3},{1,0},{2,1},{3,2},{4,7},{5,4},{6,5},{7,6},{8,11},{9,8},{10,9... | collective-permute-start | bytes 1585160 | tf_op jit(solution)/shard_map/ppermute | solution.py:53
  61.2 11.4 %collective-permute-start.20 = (s16[1040,128]{1,0:T(8,128)(2,1)S(1)}, s16[1040,128]{1,0:T(8,128)(2,1)S(1)}, u32[]{:S(2)}, u32[]{:S(2)}) collective-permute-start(s16[1040,128]{1,0:T(8,128)(2,1)S(1)} %shard_map.50), channel_id=1, source_target_pairs={{0,1},{1,2},{2,3},{3,0},{4,5},{5,6},{6,7},{7,4},{8,9},{9,10},{10,1... | collective-permute-start | bytes 798728 | tf_op jit(solution)/shard_map/ppermute | solution.py:53
  66.5 8.7 %collective-permute-start.18 = (s16[1040,128]{1,0:T(8,128)(2,1)S(1)}, s16[1040,128]{1,0:T(8,128)(2,1)S(1)}, u32[]{:S(2)}, u32[]{:S(2)}) collective-permute-start(s16[1040,128]{1,0:T(8,128)(2,1)S(1)} %shard_map.49), channel_id=1, source_target_pairs={{0,1},{1,2},{2,3},{3,0},{4,5},{5,6},{6,7},{7,4},{8,9},{9,10},{10,1... | collective-permute-start | bytes 798728 | tf_op jit(solution)/shard_map/ppermute | solution.py:53
  75.8 1.4 %collective-permute-start.21 = (f32[1,128]{1,0:T(1,128)S(1)}, f32[1,128]{1,0:T(1,128)S(1)}, u32[]{:S(2)}, u32[]{:S(2)}) collective-permute-start(f32[1,128]{1,0:T(1,128)S(1)} %get-tuple-element.45), channel_id=1, source_target_pairs={{0,32},{32,0},{1,33},{33,1},{2,34},{34,2},{3,35},{35,3},{4,36},{36... | collective-permute-start | bytes 1544 | tf_op jit(solution)/shard_map/ppermute | solution.py:65
  77.2 7.3 %collective-permute-start.22 = (f32[1024,128]{1,0:T(8,128)S(1)}, f32[1024,128]{1,0:T(8,128)S(1)}, u32[]{:S(2)}, u32[]{:S(2)}) collective-permute-start(f32[1024,128]{1,0:T(8,128)S(1)} %get-tuple-element.46), channel_id=1, source_target_pairs={{0,32},{32,0},{1,33},{33,1},{2,34},{34,2},{3,35},{35,3},{4,36},{36... | collective-permute-start | bytes 1572872 | tf_op jit(solution)/shard_map/ppermute | solution.py:65
  77.4 3.6 %collective-permute-start.23 = (f32[2,128]{1,0:T(2,128)S(1)}, f32[2,128]{1,0:T(2,128)S(1)}, u32[]{:S(2)}, u32[]{:S(2)}) collective-permute-start(f32[2,128]{1,0:T(2,128)S(1)} %pad_maximum_fusion.refs_0_), channel_id=1, source_target_pairs={{0,64},{64,128},{128,192},{192,0},{32,224},{96,32},{160,96},{224,1... | collective-permute-start | bytes 3080 | tf_op jit(solution)/shard_map/ppermute | solution.py:61
  79.2 3.6 %collective-permute-start.24 = (f32[2,128]{1,0:T(2,128)S(1)}, f32[2,128]{1,0:T(2,128)S(1)}, u32[]{:S(2)}, u32[]{:S(2)}) collective-permute-start(f32[2,128]{1,0:T(2,128)S(1)} %pad_maximum_fusion.refs_0_), channel_id=1, source_target_pairs={{0,192},{64,0},{128,64},{192,128},{32,96},{96,160},{160,224},{224,... | collective-permute-start | bytes 3080 | tf_op jit(solution)/shard_map/ppermute | solution.py:61
  79.5 5.1 %collective-permute-start.25 = (f32[2,128]{1,0:T(2,128)S(1)}, f32[2,128]{1,0:T(2,128)S(1)}, u32[]{:S(2)}, u32[]{:S(2)}) collective-permute-start(f32[2,128]{1,0:T(2,128)S(1)} %pad_maximum_fusion.refs_0_), channel_id=1, source_target_pairs={{0,128},{64,192},{128,0},{192,64},{32,160},{96,224},{160,32},{224,... | collective-permute-start | bytes 3080 | tf_op jit(solution)/shard_map/ppermute | solution.py:61
